TPU v7x, 256 devices: a whole 4x4x8 slice. The times are simulated.
256 devices in a mesh: member: 16 (over x, y), tile: 16 (over z, core).
Axes of the slice: x: 4, y: 4, z: 8, core: 2. Of those that a mesh axis runs over, the one named last changes fastest.
Arguments:
- prior_members: bfloat16 [48, 16, 128, 2048], P('member', None, 'tile'), may hold values from -6 to 6
- measured_reading: float32 [16, 16, 256], P('tile', 'member'), may hold values from -6 to 6
- measure_error_spread: float32 [16, 16, 256], P('tile', 'member'), may hold values from 0.01 to 0.1
- measured_cell_index: int32 [16, 16, 256], P('tile', 'member'), may hold values from 0 to 1023
- active_measure_tally: int32 [16, 16], P('tile', 'member'), may hold values from 32 to 256, as said below
Outputs:
- analysis: bfloat16 [48, 16, 128, 2048], P('member', None, 'tile')
Inputs may be any that keep to these rules, and one draw needn't show every extreme that they name: `active_measure_tally`: slots from a domain's count on hold values that take no part; in every draw some domain has all 256 slots live.
All inputs are finite; a program needn't handle non-finite values.
Results may differ from a plain program's by a relative error of at most 0.001.
Values may be sent and summed in bfloat16 or wider, within the bound.
No kernel may reach another device: no remote copies, remote signals or barrier semaphores. Data moves between devices by JAX's collectives and lax.ppermute only.
A program may use at most 128 MiB of HBM per device.

v0:
```python
import math

import jax
import jax.numpy as jnp
from jax import lax
from jax.sharding import PartitionSpec as P

REVISED_LEVELS = 8
OBS_LAYERS = 2
TILE_SPAN_SECOND = 128
BLOCK = 4
SLOTS = 256
RADIUS = 8


precise = lax.Precision.HIGHEST


def with_halo(cells, sides, width):
    for axis, dim in sides:
        count = lax.axis_size(axis)
        ends = count - 1
        head = lax.slice_in_dim(cells, 0, width, axis=dim)
        tail = lax.slice_in_dim(cells, cells.shape[dim] - width, cells.shape[dim], axis=dim)
        cells = jnp.concatenate(
            [
                lax.ppermute(tail, axis, [(i, (i + 1) % count) for i in range(ends)]),
                cells,
                lax.ppermute(head, axis, [((i + 1) % count, i) for i in range(ends)]),
            ],
            axis=dim,
        )
    return cells


def observe(model_levels_stack, cell_ids, values, variances, live_count):
    members = model_levels_stack.shape[0]
    surface = jnp.mean(model_levels_stack[:, :OBS_LAYERS].astype(jnp.float32), axis=1).reshape(
        members, -1
    )
    sampled = jnp.take(surface, cell_ids, axis=1)
    obs_mean = jnp.mean(sampled, axis=0)
    usable = (jnp.arange(SLOTS, dtype=jnp.int32) < live_count).astype(jnp.float32)
    pos_x = (cell_ids // TILE_SPAN_SECOND).astype(jnp.float32)
    pos_y = (cell_ids % TILE_SPAN_SECOND).astype(jnp.float32)
    return jnp.concatenate(
        [
            sampled - obs_mean[None],
            (values - obs_mean)[None],
            (usable / variances)[None],
            pos_x[None],
            pos_y[None],
        ],
        axis=0,
    )


def analyse(neighbours, model_levels_stack):
    members = model_levels_stack.shape[0]
    rows_x = model_levels_stack.shape[2]
    rows_y = model_levels_stack.shape[3]
    count_x = rows_x // BLOCK
    count_y = rows_y // BLOCK
    radius_sq = float(RADIUS * RADIUS)
    centre_x = jnp.arange(count_x, dtype=jnp.float32) * BLOCK + (BLOCK - 1) / 2.0
    centre_y = jnp.arange(count_y, dtype=jnp.float32) * BLOCK + (BLOCK - 1) / 2.0
    gram_sum = jnp.zeros((count_x * count_y, members * members), jnp.float32)
    drive_sum = jnp.zeros((count_x * count_y, members), jnp.float32)
    for step_x in range(3):
        for step_y in range(3):
            parcel = neighbours[step_x, step_y]
            ens_rows = parcel[:members]
            innovation = parcel[members]
            weight = parcel[members + 1]
            pos_x = parcel[members + 2] + (step_x - 1) * rows_x
            pos_y = parcel[members + 3] + (step_y - 1) * rows_y
            gap_x = pos_x[None, None, :] - centre_x[:, None, None]
            gap_y = pos_y[None, None, :] - centre_y[None, :, None]
            distance = gap_x * gap_x + gap_y * gap_y
            ratio = 1.0 - distance / radius_sq
            tapered = jnp.where(distance < radius_sq, ratio * ratio, 0.0)
            scaled = (tapered * weight[None, None, :]).reshape(count_x * count_y, -1)
            outers = (ens_rows[:, None, :] * ens_rows[None, :, :]).reshape(members * members, -1)
            gram_sum = gram_sum + lax.dot_general(
                scaled, outers, (((1,), (1,)), ((), ())), precision=precise
            )
            drive_sum = drive_sum + lax.dot_general(
                scaled * innovation[None, :], ens_rows, (((1,), (1,)), ((), ())), precision=precise
            )
    identity = jnp.eye(members, dtype=jnp.float32)
    system = gram_sum.reshape(-1, members, members) + (members - 1.0) * identity[None]
    factor = jnp.linalg.cholesky(system)
    forward = jax.scipy.linalg.solve_triangular(factor, drive_sum[:, :, None], lower=True)
    mean_weight = jax.scipy.linalg.solve_triangular(factor, forward, lower=True, trans=1)[:, :, 0]
    square_root = jax.scipy.linalg.solve_triangular(
        factor, jnp.broadcast_to(identity, factor.shape), lower=True, trans=1
    )
    weights = square_root * math.sqrt(members - 1.0) + mean_weight[:, :, None]
    weights = weights.reshape(count_x, count_y, members, members)
    values = model_levels_stack.astype(jnp.float32)
    centre = jnp.mean(values, axis=0)
    spread = values - centre[None]
    blocks = spread.reshape(members, model_levels_stack.shape[1], count_x, BLOCK, count_y, BLOCK)
    shifted = jnp.einsum("iuapbq,abij->juapbq", blocks, weights, precision=precise)
    return (centre[None] + shifted.reshape(model_levels_stack.shape)).astype(jnp.bfloat16)


def body(
    prior_members, measured_reading, measure_error_spread, measured_cell_index, active_measure_tally
):
    received_border = lax.all_to_all(
        prior_members, "member", split_axis=3, concat_axis=0, tiled=True
    )
    model_levels_stack = received_border[:, :REVISED_LEVELS]
    payload = observe(
        model_levels_stack,
        measured_cell_index[0, 0],
        measured_reading[0, 0],
        measure_error_spread[0, 0],
        active_measure_tally[0, 0],
    )
    neighbours = with_halo(payload[None, None], (("member", 1), ("tile", 0)), 1)
    posterior_members = analyse(neighbours, model_levels_stack)
    combined = jnp.concatenate([posterior_members, received_border[:, REVISED_LEVELS:]], axis=1)
    return lax.all_to_all(combined, "member", split_axis=0, concat_axis=3, tiled=True)


def solution(mesh):
    return jax.shard_map(
        body,
        mesh=mesh,
        in_specs=(
            P("member", None, "tile", None),
            P("tile", "member", None),
            P("tile", "member", None),
            P("tile", "member", None),
            P("tile", "member"),
        ),
        out_specs=P("member", None, "tile", None),
        check_vma=False,
    )
```

profile of v0, /device:TPU:97, one launch (start us, length us, event | category | flops | bytes accessed | tf_op | source)
XLA Modules:
  0.0 514.5 jit_solution(4272738480475895058)
XLA Ops:
  0.0 13.3 %copy.165 = bf16[3,16,8,2048]{1,2,0,3:T(8,128)(2,1)} copy(bf16[3,16,8,2048]{3,2,1,0:T(8,128)(2,1)} %param.5) | data formatting | bytes 3145728 | tf_op args[0]
  13.3 17.7 %reshape.1926 = bf16[16,2,24576]{2,1,0:T(2,128)(2,1)} reshape(bf16[2048,3,8,16]{3,2,1,0:T(8,128)(2,1)} %bitcast.191) | data formatting | bytes 3145728
  30.9 6.9 %all-to-all-start = ((bf16[16,2,24576]{2,1,0:T(2,128)(2,1)}), bf16[16,2,24576]{2,1,0:T(2,128)(2,1)S(1)}, u32[]{:S(2)}, u32[]{:S(2)}) async-start(bf16[16,2,24576]{2,1,0:T(2,128)(2,1)} %reshape.1926), calls=%async_computation | async-start | bytes 3145728 | tf_op jit(solution)/shard_map/all_to_all | solution.py:111
  42.7 15.7 %all-to-all-done = bf16[16,2,24576]{2,1,0:T(2,128)(2,1)S(1)} async-done(((bf16[16,2,24576]{2,1,0:T(2,128)(2,1)}), bf16[16,2,24576]{2,1,0:T(2,128)(2,1)S(1)}, u32[]{:S(2)}, u32[]{:S(2)}) %all-to-all-start) | async-done | bytes 1572896 | tf_op jit(solution)/shard_map/all_to_all | solution.py:111
  58.5 12.0 %reshape.1927 = bf16[2048,3,8,16]{3,2,1,0:T(8,128)(2,1)} reshape(bf16[16,2,24576]{2,1,0:T(2,128)(2,1)S(1)} %all-to-all-done) | data formatting | bytes 3145728
  70.5 12.1 %copy.167 = bf16[16,3,16,8,128]{4,3,2,1,0:T(8,128)(2,1)S(1)} copy(bf16[16,3,16,8,128]{2,3,1,4,0:T(8,128)(2,1)} %bitcast.190) | data formatting | bytes 3145728 | tf_op jit(solution)/shard_map/all_to_all | solution.py:111
  91.6 3.5 copy.178
  95.7 9.0 %collective-permute-start.2 = (f32[1,3,52,256]{3,2,1,0:T(8,128)S(1)}, f32[1,3,52,256]{3,2,1,0:T(8,128)S(1)}, u32[]{:S(2)}, u32[]{:S(2)}) collective-permute-start(f32[1,3,52,256]{3,2,1,0:T(8,128)S(1)} %pad_maximum_fusion.1), channel_id=1, source_target_pairs={{0,1},{1,2},{2,3},{3,4},{4,5},{5,6},{6,7},{7,8},{8,9},{9,10},{10,1... | collective-permute-start | bytes 479240 | tf_op jit(solution)/shard_map/ppermute | solution.py:27
  108.5 4.3 collective-permute-done.3
  114.6 2.4 fusion.76
  117.7 2.4 convolution_add_fusion.7
  120.7 2.4 convolution_add_fusion.6
  126.1 2.4 convolution_add_fusion.4
  129.1 2.6 convolution_add_fusion.3
  132.3 2.4 convolution_add_fusion.2
  135.3 2.4 convolution_add_fusion.1
  138.3 2.4 convolution_add_fusion
  146.9 282.4 %custom-call.14 = f32[64,48,48]{2,1,0:T(8,128)} custom-call(f32[64,48,48]{2,1,0:T(8,128)S(1)} %fusion.5), custom_call_target="Cholesky" | custom-call | tf_op jit(solution)/shard_map/jit(cholesky)/cholesky | solution.py:92
  433.1 33.8 %custom-call.15 = f32[64,1,48,48]{0,2,3,1:T(8,128)S(1)} custom-call(f32[64,1,48,48]{0,3,2,1:T(8,128)} %select_bitcast_fusion), custom_call_target="InvertDiagBlocksLowerTriangular" | custom-call | tf_op jit(solution)/shard_map/jit(_solve_triangular)/vmap()/triangular_solve | solution.py:95
  469.7 2.5 fusion.77
  473.9 4.4 fusion.2
  478.3 2.4 copy.180
  480.8 4.0 copy.181
  486.1 26.3 %all_to_all.36 = bf16[48,16,8,128]{3,2,1,0:T(8,128)(2,1)S(1)} all-to-all(bf16[48,16,8,128]{3,2,1,0:T(8,128)(2,1)S(1)} %pad_maximum_fusion), channel_id=1, replica_groups=mesh['member'=16,'tile'=16] {'member'}, dimensions={0} | all-to-all | bytes 3145728 | tf_op jit(solution)/shard_map/all_to_all | solution.py:125
  (154 shorter events, 42.9 us)
Async XLA Ops:
  30.9 8.1 %copy-start.21 = (s32[1,1,256]{2,1,0:T(1,128)S(1)}, s32[1,1,256]{2,1,0:T(1,128)}, u32[]{:S(2)}) copy-start(s32[1,1,256]{2,1,0:T(1,128)} %param.8) | copy-start | bytes 3076
  30.9 11.2 %copy-start.28 = (f32[1,1,256]{2,1,0:T(1,128)S(1)}, f32[1,1,256]{2,1,0:T(1,128)}, u32[]{:S(2)}) copy-start(f32[1,1,256]{2,1,0:T(1,128)} %param.7) | copy-start | bytes 3076
  30.9 27.5 %all-to-all-start = ((bf16[16,2,24576]{2,1,0:T(2,128)(2,1)}), bf16[16,2,24576]{2,1,0:T(2,128)(2,1)S(1)}, u32[]{:S(2)}, u32[]{:S(2)}) async-start(bf16[16,2,24576]{2,1,0:T(2,128)(2,1)} %reshape.1926), calls=%async_computation | async-start | bytes 3145728 | tf_op jit(solution)/shard_map/all_to_all | solution.py:111
  40.9 43.5 %copy-start.23 = (pred[256]{0:T(512)(128)(4,1)}, pred[256]{0:T(512)(128)(4,1)S(1)}, u32[]{:S(2)}) copy-start(pred[256]{0:T(512)(128)(4,1)S(1)} %compare_and_fusion) | copy-start | bytes 772
  70.5 13.3 %copy-start.29 = (f32[1,1,256]{2,1,0:T(1,128)S(1)}, f32[1,1,256]{2,1,0:T(1,128)}, u32[]{:S(2)}) copy-start(f32[1,1,256]{2,1,0:T(1,128)} %param.6) | copy-start | bytes 3076
  85.0 10.1 %collective-permute-start = (f32[1,1,52,256]{3,2,1,0:T(8,128)S(1)}, f32[1,1,52,256]{3,2,1,0:T(8,128)S(1)}, u32[]{:S(2)}, u32[]{:S(2)}) collective-permute-start(f32[1,1,52,256]{3,2,1,0:T(8,128)S(1)} %bitcast.229), channel_id=1, source_target_pairs={{0,16},{16,32},{32,48},{48,64},{64,80},{80,96},{96,112},{112,128},... | collective-permute-start | bytes 159752 | tf_op jit(solution)/shard_map/ppermute | solution.py:27
  87.2 7.8 %collective-permute-start.1 = (f32[1,1,52,256]{3,2,1,0:T(8,128)S(1)}, f32[1,1,52,256]{3,2,1,0:T(8,128)S(1)}, u32[]{:S(2)}, u32[]{:S(2)}) collective-permute-start(f32[1,1,52,256]{3,2,1,0:T(8,128)S(1)} %bitcast.230), channel_id=1, source_target_pairs={{16,0},{32,16},{48,32},{64,48},{80,64},{96,80},{112,96},{128,112},... | collective-permute-start | bytes 159752 | tf_op jit(solution)/shard_map/ppermute | solution.py:29
  95.7 11.9 %collective-permute-start.2 = (f32[1,3,52,256]{3,2,1,0:T(8,128)S(1)}, f32[1,3,52,256]{3,2,1,0:T(8,128)S(1)}, u32[]{:S(2)}, u32[]{:S(2)}) collective-permute-start(f32[1,3,52,256]{3,2,1,0:T(8,128)S(1)} %pad_maximum_fusion.1), channel_id=1, source_target_pairs={{0,1},{1,2},{2,3},{3,4},{4,5},{5,6},{6,7},{7,8},{8,9},{9,10},{10,1... | collective-permute-start | bytes 479240 | tf_op jit(solution)/shard_map/ppermute | solution.py:27
  104.7 8.1 %collective-permute-start.3 = (f32[1,3,52,256]{3,2,1,0:T(8,128)S(1)}, f32[1,3,52,256]{3,2,1,0:T(8,128)S(1)}, u32[]{:S(2)}, u32[]{:S(2)}) collective-permute-start(f32[1,3,52,256]{3,2,1,0:T(8,128)S(1)} %pad_maximum_fusion.1), channel_id=1, source_target_pairs={{1,0},{2,1},{3,2},{4,3},{5,4},{6,5},{7,6},{8,7},{9,8},{10,9},{11,1... | collective-permute-start | bytes 479240 | tf_op jit(solution)/shard_map/ppermute | solution.py:29
  107.6 6.1 %copy-start.3 = (f32[1,3,52,256]{3,2,1,0:T(8,128)}, f32[1,3,52,256]{3,2,1,0:T(8,128)S(1)}, u32[]{:S(2)}) copy-start(f32[1,3,52,256]{3,2,1,0:T(8,128)S(1)} %collective-permute-done.2) | copy-start | bytes 479236
  113.7 3.3 copy-start.22
  431.2 35.7 %copy-start.10 = (f32[2,32,256]{2,1,0:T(8,128)S(1)}, f32[2,32,256]{2,1,0:T(8,128)}, u32[]{:S(2)}) copy-start(f32[2,32,256]{2,1,0:T(8,128)} %get-tuple-element.55) | copy-start | bytes 196612
  431.2 35.9 %copy-start.4 = (f32[1,3,52,256]{3,2,1,0:T(8,128)S(1)}, f32[1,3,52,256]{3,2,1,0:T(8,128)}, u32[]{:S(2)}) copy-start(f32[1,3,52,256]{3,2,1,0:T(8,128)} %copy-done.3) | copy-start | bytes 479236
  431.3 35.9 %copy-start.9 = (f32[2,32,256]{2,1,0:T(8,128)S(1)}, f32[2,32,256]{2,1,0:T(8,128)}, u32[]{:S(2)}) copy-start(f32[2,32,256]{2,1,0:T(8,128)} %get-tuple-element.53) | copy-start | bytes 196612
  431.3 36.1 %copy-start.8 = (f32[2,32,256]{2,1,0:T(8,128)S(1)}, f32[2,32,256]{2,1,0:T(8,128)}, u32[]{:S(2)}) copy-start(f32[2,32,256]{2,1,0:T(8,128)} %get-tuple-element.51) | copy-start | bytes 196612
  431.3 36.3 %copy-start.11 = (f32[2,32,256]{2,1,0:T(8,128)S(1)}, f32[2,32,256]{2,1,0:T(8,128)}, u32[]{:S(2)}) copy-start(f32[2,32,256]{2,1,0:T(8,128)} %get-tuple-element.57) | copy-start | bytes 196612
  431.3 36.5 %copy-start.12 = (f32[2,32,256]{2,1,0:T(8,128)S(1)}, f32[2,32,256]{2,1,0:T(8,128)}, u32[]{:S(2)}) copy-start(f32[2,32,256]{2,1,0:T(8,128)} %get-tuple-element.59) | copy-start | bytes 196612
  431.3 36.7 %copy-start.13 = (f32[2,32,256]{2,1,0:T(8,128)S(1)}, f32[2,32,256]{2,1,0:T(8,128)}, u32[]{:S(2)}) copy-start(f32[2,32,256]{2,1,0:T(8,128)} %get-tuple-element.61) | copy-start | bytes 196612
  431.3 36.9 %copy-start.14 = (f32[2,32,256]{2,1,0:T(8,128)S(1)}, f32[2,32,256]{2,1,0:T(8,128)}, u32[]{:S(2)}) copy-start(f32[2,32,256]{2,1,0:T(8,128)} %get-tuple-element.49) | copy-start | bytes 196612
  431.3 36.9 %copy-start.18 = (f32[64,48]{0,1:T(8,128)S(1)}, f32[64,48]{0,1:T(8,128)}, u32[]{:S(2)}) copy-start(f32[64,48]{0,1:T(8,128)} %fusion.14) | copy-start | bytes 36868
  431.3 37.1 %copy-start.7 = (f32[1,1,52,256]{3,2,1,0:T(8,128)S(1)}, f32[1,1,52,256]{3,2,1,0:T(8,128)}, u32[]{:S(2)}) copy-start(f32[1,1,52,256]{3,2,1,0:T(8,128)} %copy-done.5) | copy-start | bytes 159748
  431.3 37.1 %copy-start.15 = (f32[2,32,256]{2,1,0:T(8,128)S(1)}, f32[2,32,256]{2,1,0:T(8,128)}, u32[]{:S(2)}) copy-start(f32[2,32,256]{2,1,0:T(8,128)} %get-tuple-element.47) | copy-start | bytes 196612
  468.9 3.4 copy-start.16
  469.7 4.2 copy-start
  (13 other events, 21.7 us)
where the time goes:
time: 521 us; the launch traced here: 514 us
  other arithmetic  335 us (64%)
  local copies, waits for them, and re-layouts  76.6 us (15%)
  matrix products  32.7 us (6%)
  blocking collectives  26.3 us (5%)
  starting transfers between devices  21.6 us (4%)
  waiting for transfers between devices  20.1 us (4%)
    another operation x4, other arithmetic, analyse(): factor = jnp.linalg.cholesky(system)  283 us
    unnamed x67, local copies, waits for them, and re-layouts  45 us
    another operation x3, other arithmetic, analyse(): jax.scipy.linalg.solve_triangular(factor, jnp.broadcast_to(identity, fact...  35.1 us
    all_to_all x1, blocking collectives, body(): lax.all_to_all(combined, 'member', split_axis=0, concat_axis=3, tiled=True)  26.3 us
    dot_general x9, matrix products, analyse(): lax.dot_general(scaled, outers, (((1,), (1,)), ((), ())), precision=precise)  21.4 us
    all_to_all x1, waiting for transfers between devices, body(): lax.all_to_all(prior_members, 'member', split_axis=3, concat_axis=0, tile...  15.7 us
    all_to_all x1, local copies, waits for them, and re-layouts, body(): lax.all_to_all(prior_members, 'member', split_axis=3, concat_axis=0, tile...  12.1 us
    ppermute x2, starting transfers between devices, with_halo(): lax.ppermute(tail, axis, [(i, (i + 1) % count) for i in range(ends)])  11.2 us
  transfers between devices with their start and end apart: 5, of which 2 were waited for; matrix products, arithmetic and copies ran while one was open for 2% of the time, Pallas kernels for 0%

commit v1 on v0

v1 whole, which is shorter than its diff:
```python
import functools
import math

import jax
import jax.numpy as jnp
import numpy as np
from jax import lax
from jax.experimental import pallas as pl
from jax.experimental.pallas import tpu as pltpu
from jax.sharding import PartitionSpec as P

MEMBERS = 48
UPPER = 8
LANES = 128
SLOTS = 256
RADIUS = 8
BLOCK = 4
CHUNK = 16
GROUPS = LANES // CHUNK
BLOCKS_Y = LANES // BLOCK
ROWS = 64
PACK = 56
DOMS = 16
F32 = jnp.float32
BF16 = jnp.bfloat16


def split3(x):
    hi = x.astype(BF16)
    rest = x - hi.astype(F32)
    mid = rest.astype(BF16)
    low = (rest - mid.astype(F32)).astype(BF16)
    return hi, mid, low


def split2(x):
    hi = x.astype(BF16)
    return hi, (x - hi.astype(F32)).astype(BF16)


def nt(a, b):
    return lax.dot_general(a, b, (((1,), (1,)), ((), ())), preferred_element_type=F32)


def nn(a, b):
    return lax.dot_general(a, b, (((1,), (0,)), ((), ())), preferred_element_type=F32)


def row_spread():
    m = np.zeros((64, 48), np.float32)
    for x in range(8):
        for r in range(6):
            m[x * 8 + r, r * 8 + x] = 1.0
    return m


def row_compact():
    m = np.zeros((ROWS, 80), np.float32)
    for v in range(9):
        for r in range(6):
            m[v * 6 + r, v * 8 + r] = 1.0
    for r in range(6):
        m[54 + r, 72 + r] = 1.0
    return m


def row_sample():
    m = np.zeros((9 * PACK, DOMS * ROWS), np.float32)
    for v in range(9):
        for i in range(MEMBERS):
            for layer in range(2):
                m[v * PACK + i, (i // 3) * ROWS + v * 6 + (i % 3) * 2 + layer] = 0.5
    for s in range(DOMS):
        for r in range(3):
            m[8 * PACK + 48, s * ROWS + 54 + r] = 1.0
            m[8 * PACK + 49, s * ROWS + 57 + r] = 1.0
    return m


OFFSETS = (10, 14, 2, 6)


def taper_rows():
    lane = np.arange(LANES)
    x, y = lane // CHUNK, lane % CHUNK
    t = np.zeros((24, LANES), np.float32)
    for k, o in enumerate(OFFSETS):
        gap_y = np.where(y >= o, y - o, y - o + CHUNK) - 6 - 1.5
        for seg in range(3):
            for p in range(2):
                gap_x = (seg - 1) * 8 + x - (4 * p + 1.5)
                s = gap_x * gap_x + gap_y * gap_y
                t[(k * 3 + seg) * 2 + p] = np.where(s < RADIUS * RADIUS, (1 - s / 64.0) ** 2, 0.0)
    return t


def expand_rows():
    m = np.zeros((128, 512), np.float32)
    for h in range(2):
        for p in range(2):
            for y in range(128):
                m[h * 64 + p * 32 + y // 4, h * 256 + p * 128 + y] = 1.0
    return np.concatenate([m, m], 0)


def pack_kernel(where, tally, x_ref, reading, error, cell, spread, compact, out, own, work):
    me = where[0]
    live = lax.broadcasted_iota(jnp.int32, (1, SLOTS), 1) < tally[0]
    prec = jnp.where(live, 1.0 / error[...], 0.0)
    vals = jnp.where(live, prec * reading[...], 0.0)
    c = cell[...]
    x, y = c // LANES, c % LANES
    group = y // CHUNK
    lane = x * CHUNK + y % CHUNK
    hit = lax.broadcasted_iota(jnp.int32, (8, SLOTS), 0) == group
    spot = (lax.broadcasted_iota(jnp.int32, (LANES, SLOTS), 0) == lane).astype(F32).astype(BF16)
    pv = jnp.concatenate([jnp.where(hit, prec, 0.0), jnp.where(hit, vals, 0.0)], 0)
    a, b, d = split3(pv)
    pv = nt(a, spot) + nt(b, spot) + nt(d, spot)
    own[...] = pv
    sub = lax.broadcasted_iota(jnp.int32, (8, LANES), 0)
    col = lax.broadcasted_iota(jnp.int32, (8, LANES), 1)
    high = (col % CHUNK) >= 8

    def edge(g):
        res = jnp.zeros((8, LANES), F32)
        for n in range(2):
            parts = split3(jnp.broadcast_to(pv[n * 8 + g : n * 8 + g + 1, :], (8, LANES)))
            for k in range(3):
                res = jnp.where(sub == n * 3 + k, parts[k].astype(F32), res)
        return res

    last = jnp.where(high, edge(7), 0.0)
    first = jnp.where(high, 0.0, edge(0))

    flat = x_ref[...].reshape(48, 16 * LANES)
    rows = nn(spread[...], flat)
    for d in range(DOMS):
        v = [rows[8 * k : 8 * k + 8, d * LANES : (d + 1) * LANES] for k in range(8)]
        for step in (4, 2, 1):
            width = step * CHUNK
            low = ((col // width) % 2) == 0
            new = list(v)
            for k in range(8):
                if not k & step:
                    a, b = v[k], v[k + step]
                    new[k] = jnp.where(low, a, pltpu.roll(b, width, 1))
                    new[k + step] = jnp.where(low, pltpu.roll(a, LANES - width, 1), b)
            v = new
        for k in range(8):
            work[d, 8 * k : 8 * k + 8, :] = v[k]
    for d in range(DOMS):
        left = work[(d - 1) % DOMS, 56:64, :]
        right = work[(d + 1) % DOMS, 0:8, :]
        work[d, 64:72, :] = jnp.where(high, left, right)
        work[d, 72:80, :] = jnp.where(
            me == d - 1, last, jnp.where(me == d + 1, first, jnp.zeros_like(first))
        )
    for d in range(DOMS):
        out[d] = nn(compact[...], work[d].astype(BF16)).astype(BF16)


def sample_kernel(r_ref, own, choose, out):
    pv = own[...]
    res = nn(choose[...], r_ref[...].reshape(DOMS * ROWS, LANES))
    for v in range(9):
        s = res[v * PACK : v * PACK + MEMBERS]
        mean = jnp.sum(s, axis=0, keepdims=True) * (1.0 / MEMBERS)
        if v < 8:
            prec, vals = pv[v : v + 1], pv[8 + v : 9 + v]
        else:
            prec, vals = res[v * PACK + 48 : v * PACK + 49], res[v * PACK + 49 : v * PACK + 50]
        out[v, 0:48, :] = s - mean
        sub = lax.broadcasted_iota(jnp.int32, (8, LANES), 0)
        out[v, 48:56, :] = jnp.where(
            sub == 0, prec, jnp.where(sub == 1, vals - prec * mean, 0.0)
        )


def solve_kernel(up, own, down, taper, out, grams, mat, piv, fac):
    segs = (up, own, down)
    lane = lax.broadcasted_iota(jnp.int32, (1, LANES), 1) % CHUNK

    def group(g, carry):
        before = jnp.where(g == 0, 8, g - 1)
        after = jnp.where(g == 7, 8, g + 1)
        for k, o in enumerate(OFFSETS):
            v0, v1 = (before, g) if k < 2 else (g, after)
            mask = lane >= o
            ahi, alo = [], []
            lhi, llo = [], []
            for s in range(3):
                w = jnp.where(mask, segs[s][v0], segs[s][v1])
                a = w[0:48]
                prec, drv = w[48:49], w[49:50]
                h, l = split2(a)
                ahi.append(h)
                alo.append(l)
                t0 = taper[(k * 3 + s) * 2 : (k * 3 + s) * 2 + 1, :]
                t1 = taper[(k * 3 + s) * 2 + 1 : (k * 3 + s) * 2 + 2, :]
                sub = lax.broadcasted_iota(jnp.int32, (16, LANES), 0)
                lhs = jnp.concatenate(
                    [
                        a * (prec * t0),
                        a * (prec * t1),
                        jnp.where(sub == 0, drv * t0, jnp.where(sub == 1, drv * t1, 0.0)),
                    ],
                    0,
                )
                h, l = split2(lhs)
                lhi.append(h)
                llo.append(l)
            left = jnp.concatenate(lhi + lhi + llo, 1)
            right = jnp.concatenate(ahi + alo + ahi, 1)
            res = nt(left, right)
            q = g * 4 + k
            res = jnp.concatenate([res, jnp.zeros((112, LANES - MEMBERS), F32)], 1)
            row0 = pl.multiple_of(q * PACK, 8)
            row1 = pl.multiple_of((q + BLOCKS_Y) * PACK, 8)
            grams[pl.ds(row0, 48), :] = res[0:48]
            grams[pl.ds(row0 + 48, 8), :] = res[96:104]
            grams[pl.ds(row1, 48), :] = res[48:96]
            grams[pl.ds(row1 + 48, 8), :] = pltpu.roll(res[96:104], 7, 0)
        return carry

    lax.fori_loop(0, 8, group, 0)

    for t in range(25):
        a = grams[pl.ds(2 * t, 64, stride=PACK), :]
        b = grams[pl.ds(2 * t + 1, 64, stride=PACK), :] if t < 24 else a
        mat[t] = jnp.concatenate([a, b], 0).T[0:48, :]

    sub = lax.broadcasted_iota(jnp.int32, (8, LANES), 0)
    half = lax.broadcasted_iota(jnp.int32, (8, LANES), 1) // 64
    half0 = half == 0

    def tiles(t):
        return [mat[t, 8 * j : 8 * j + 8, :] for j in range(6)]

    drive = tiles(24)
    scale = []
    for panel in range(6):
        rows = [tiles(4 * panel + n) for n in range(4)]
        for n in range(4):
            diag = jnp.where(sub == 2 * n + half, MEMBERS - 1.0, 0.0)
            rows[n][panel] = rows[n][panel] + diag
        for k in range(8):
            n, h = k // 2, k % 2
            mine = half == h
            row = [jnp.where(mine, x, pltpu.roll(x, 64, 1)) for x in rows[n]]
            inv = 1.0 / jnp.broadcast_to(row[panel][k : k + 1, :], (8, LANES))
            scale.append(jnp.sqrt((MEMBERS - 1.0) * inv[0:1, :]))
            here = sub == k
            f = row[panel] * inv
            for j in range(panel + 1, 6):
                fac[k, 8 * j : 8 * j + 8, :] = row[j] * inv
            row[panel] = jnp.where(here, 1.0, row[panel])
            for j in range(6):
                if j != panel:
                    piv[k, 8 * j : 8 * j + 8, :] = row[j]
            piv[k, 8 * panel : 8 * panel + 8, :] = jnp.where(sub <= k, row[panel], 0.0)
            fd = jnp.broadcast_to(drive[panel][k : k + 1, :], (8, LANES)) * inv
            drive[panel] = jnp.where(here, 0.0, drive[panel])
            drive = [drive[j] - fd * row[j] for j in range(6)]
            for n2 in range(n, 4):
                if n2 == n and h == 1:
                    rows[n][panel] = jnp.where(
                        jnp.logical_and(here, mine), 1.0, rows[n][panel]
                    )
                    continue
                fb = jnp.broadcast_to(f[2 * n2 + 1 : 2 * n2 + 2, :], (8, LANES))
                if n2 == n:
                    fp = jnp.where(half0, 0.0, fb)
                    rows[n][panel] = jnp.where(
                        here, jnp.where(half0, 1.0, 0.0), rows[n][panel]
                    )
                else:
                    fa = jnp.broadcast_to(f[2 * n2 : 2 * n2 + 1, :], (8, LANES))
                    fp = jnp.where(half0, fa, fb)
                    rows[n2][panel] = jnp.where(here, 0.0, rows[n2][panel])
                rows[n2] = [rows[n2][j] - fp * row[j] for j in range(6)]
        for n in range(4):
            for j in range(panel + 1):
                mat[4 * panel + n, 8 * j : 8 * j + 8, :] = rows[n][j]
        for block in range(panel + 1, 6):
            js = list(range(panel + 1)) + list(range(block, 6))
            acc = [
                {
                    j: jnp.zeros((8, LANES), F32)
                    if j == panel
                    else mat[4 * block + n, 8 * j : 8 * j + 8, :]
                    for j in js
                }
                for n in range(4)
            ]
            for k in range(8):
                pr = {j: piv[k, 8 * j : 8 * j + 8, :] for j in js}
                for n in range(4):
                    i = 8 * block + 2 * n
                    fa = jnp.broadcast_to(fac[k, i : i + 1, :], (8, LANES))
                    fb = jnp.broadcast_to(fac[k, i + 1 : i + 2, :], (8, LANES))
                    fp = jnp.where(half0, fa, fb)
                    for j in js:
                        acc[n][j] = acc[n][j] - fp * pr[j]
            for n in range(4):
                for j in js:
                    mat[4 * block + n, 8 * j : 8 * j + 8, :] = acc[n][j]

    for t in range(24):
        panel, n = t // 4, t % 4
        sc = jnp.where(half0, scale[2 * t], scale[2 * t + 1])
        w = []
        for j in range(6):
            x = -drive[j]
            if j <= panel:
                e = mat[t, 8 * j : 8 * j + 8, :]
                if j == panel:
                    e = jnp.where(sub <= 2 * n + half, e, 0.0)
                x = x + sc * e
            w.append(x)
        total = jnp.sum(w[0] + w[1] + w[2] + w[3] + w[4] + w[5], axis=0, keepdims=True)
        fix = (1.0 - total) * (1.0 / MEMBERS)
        for j in range(6):
            out[t, 8 * j : 8 * j + 8, :] = w[j] + fix


def transform_kernel(w_ref, x_ref, expand, out, wide, xs):
    w = w_ref[...].reshape(24 * 48, LANES)
    hi, low = split2(w)
    wide[...] = nn(jnp.concatenate([hi, low], 1), expand[...])

    def widen(i, c):
        for l in range(8):
            xs[i, l] = x_ref[i, l].astype(F32)
        return c

    lax.fori_loop(0, MEMBERS, widen, 0)
    top = lax.broadcasted_iota(jnp.int32, (8, LANES), 0) < 4

    def pair(t, c):
        def step(i, acc):
            acc = list(acc)
            for u in range(4):
                r = t * 48 + i * 4 + u
                line = wide[pl.ds(r, 1), :]
                ws = []
                for h in range(2):
                    a = jnp.broadcast_to(line[:, h * 256 : h * 256 + 128], (8, LANES))
                    b = jnp.broadcast_to(line[:, h * 256 + 128 : h * 256 + 256], (8, LANES))
                    ws.append(jnp.where(top, a, b))
                for l in range(8):
                    x = xs[i * 4 + u, l]
                    acc[l] = acc[l] + x * ws[0]
                    acc[8 + l] = acc[8 + l] + x * ws[1]
            return tuple(acc)

        acc = lax.fori_loop(0, 12, step, tuple(jnp.zeros((8, LANES), F32) for _ in range(16)))
        for h in range(2):
            for l in range(8):
                out[2 * t + h, l] = acc[8 * h + l].astype(BF16)
        return c

    lax.fori_loop(0, 24, pair, 0)


def send_kernel(x_ref, out, sems):
    copies = []
    for d in range(DOMS):
        copies.append(
            pltpu.make_async_copy(
                x_ref.at[:, 0:UPPER, :, pl.ds(d * LANES, LANES)], out.at[d], sems.at[d]
            )
        )
    for c in copies:
        c.start()
    for c in copies:
        c.wait()


def finish_kernel(b_ref, x_ref, out, sems):
    copies = [
        pltpu.make_async_copy(
            x_ref.at[:, UPPER : 2 * UPPER], out.at[:, UPPER : 2 * UPPER], sems.at[DOMS]
        )
    ]
    for d in range(DOMS):
        copies.append(
            pltpu.make_async_copy(
                b_ref.at[d], out.at[:, 0:UPPER, :, pl.ds(d * LANES, LANES)], sems.at[d]
            )
        )
    for c in copies:
        c.start()
    for c in copies:
        c.wait()


VM = pl.BlockSpec(memory_space=pltpu.VMEM)
SM = pl.BlockSpec(memory_space=pltpu.SMEM)
ANY = pl.BlockSpec(memory_space=pl.ANY)
LIMIT = pltpu.CompilerParams(vmem_limit_bytes=48 * 2**20)


def body(prior, reading, error, cell, tally):
    me = lax.axis_index("member").astype(jnp.int32).reshape(1)
    const = lambda a, t: jnp.asarray(a, t)
    packed, own = pl.pallas_call(
        pack_kernel,
        grid=(1,),
        in_specs=[
            SM,
            SM,
            pl.BlockSpec((3, 2, 8, 2048), lambda g: (0, 0, 0, 0)),
            VM,
            VM,
            VM,
            VM,
            VM,
        ],
        out_specs=[VM, VM],
        out_shape=[
            jax.ShapeDtypeStruct((DOMS, ROWS, LANES), BF16),
            jax.ShapeDtypeStruct((16, LANES), F32),
        ],
        scratch_shapes=[pltpu.VMEM((DOMS, 80, LANES), F32)],
        compiler_params=LIMIT,
        name="pack",
    )(
        me,
        tally.reshape(1),
        prior,
        reading.reshape(1, SLOTS),
        error.reshape(1, SLOTS),
        cell.reshape(1, SLOTS),
        const(row_spread(), BF16),
        const(row_compact(), BF16),
    )
    fields = pl.pallas_call(
        send_kernel,
        in_specs=[ANY],
        out_specs=ANY,
        out_shape=jax.ShapeDtypeStruct((DOMS, 3, UPPER, 8, LANES), BF16),
        scratch_shapes=[pltpu.SemaphoreType.DMA((DOMS,))],
        name="send",
    )(prior)
    packed = lax.all_to_all(packed, "member", 0, 0, tiled=True)
    fields = lax.all_to_all(
        fields.reshape(MEMBERS, UPPER, 8, LANES), "member", 0, 0, tiled=True
    )
    sampled = pl.pallas_call(
        sample_kernel,
        in_specs=[VM, VM, VM],
        out_specs=VM,
        out_shape=jax.ShapeDtypeStruct((9, PACK, LANES), F32),
        compiler_params=LIMIT,
        name="sample",
    )(packed, own, const(row_sample(), BF16))
    ends = lax.axis_size("tile") - 1
    up = lax.ppermute(sampled, "tile", [(i, i + 1) for i in range(ends)])
    down = lax.ppermute(sampled, "tile", [(i + 1, i) for i in range(ends)])
    weights = pl.pallas_call(
        solve_kernel,
        in_specs=[VM, VM, VM, VM],
        out_specs=VM,
        out_shape=jax.ShapeDtypeStruct((24, 48, LANES), F32),
        scratch_shapes=[
            pltpu.VMEM((64 * PACK, LANES), F32),
            pltpu.VMEM((25, 48, LANES), F32),
            pltpu.VMEM((8, 48, LANES), F32),
            pltpu.VMEM((8, 48, LANES), F32),
        ],
        compiler_params=LIMIT,
        name="solve",
    )(up, sampled, down, const(taper_rows(), F32))
    result = pl.pallas_call(
        transform_kernel,
        in_specs=[VM, VM, VM],
        out_specs=VM,
        out_shape=jax.ShapeDtypeStruct((MEMBERS, UPPER, 8, LANES), BF16),
        scratch_shapes=[
            pltpu.VMEM((24 * 48, 512), F32),
            pltpu.VMEM((MEMBERS, UPPER, 8, LANES), F32),
        ],
        compiler_params=LIMIT,
        name="transform",
    )(weights, fields, const(expand_rows(), BF16))
    result = lax.all_to_all(result, "member", 0, 0, tiled=True)
    return pl.pallas_call(
        finish_kernel,
        in_specs=[ANY, ANY],
        out_specs=ANY,
        out_shape=jax.ShapeDtypeStruct(prior.shape, BF16),
        scratch_shapes=[pltpu.SemaphoreType.DMA((DOMS + 1,))],
        name="finish",
    )(result.reshape(DOMS, 3, UPPER, 8, LANES), prior)


def solution(mesh):
    return jax.shard_map(
        body,
        mesh=mesh,
        in_specs=(
            P("member", None, "tile", None),
            P("tile", "member", None),
            P("tile", "member", None),
            P("tile", "member", None),
            P("tile", "member"),
        ),
        out_specs=P("member", None, "tile", None),
        check_vma=False,
    )
```

time: 521 us -> 145 us (0.28); the launches traced: 514 us -> 144 us
  other arithmetic: 335 us -> 0 us
  Pallas kernels: 0 us -> 92.8 us
  local copies, waits for them, and re-layouts: 76.6 us -> 4.89 us
  matrix products: 32.7 us -> 0 us
  waiting for transfers between devices: 20.1 us -> 3.26 us
  blocking collectives: 26.3 us -> 20.4 us
    another operation x7 -> x0, other arithmetic: 318 us -> none  [the longest x4 283 us: analyse(): factor = jnp.linalg.cholesky(system)]
    pallas_call x0 -> x6, Pallas kernels: none -> 92.8 us  [the longest x1 48.9 us: body(): pl.pallas_call(finish_kernel, in_specs=[ANY, ANY], out_specs=ANY, out_sha...]
    unnamed x67 -> x18, local copies, waits for them, and re-layouts: 45 us -> 4.89 us
    dot_general x19 -> x0, matrix products: 28.5 us -> none  [the longest x9 21.4 us: analyse(): lax.dot_general(scaled, outers, (((1,), (1,)), ((), ())), precision=precise)]
    all_to_all x1 -> x2, waiting for transfers between devices: 15.7 us -> 0.01 us  [the longest x1 0.01 us: body(): packed = lax.all_to_all(packed, 'member', 0, 0, tiled=True)]
    all_to_all x2 -> x0, local copies, waits for them, and re-layouts: 13.7 us -> none  [the longest x1 12.1 us: body(): lax.all_to_all(prior_members, 'member', split_axis=3, concat_axis=0, tile...]
    mul x21 -> x0, other arithmetic: 9.91 us -> none  [the longest x9 5.22 us: analyse(): scaled * innovation[None, :]]
    ppermute x4 -> x2, starting transfers between devices: 14.7 us -> 8.08 us  [the longest x1 4.65 us: body(): up = lax.ppermute(sampled, 'tile', [(i, i + 1) for i in range(ends)])]
  transfers between devices with their start and end apart: 5 -> 4, of which waited for: 2 -> 2; matrix products, arithmetic and copies ran while one was open for 2% -> 0% of each run, Pallas kernels for 0% -> 6%
where the time goes in v1:
time: 145 us; the launch traced here: 144 us
  Pallas kernels  92.8 us (64%)
  starting transfers between devices  21.5 us (15%)
  blocking collectives  20.4 us (14%)
  local copies, waits for them, and re-layouts  4.89 us (3%)
  waiting for transfers between devices  3.26 us (2%)
    pallas_call x1, Pallas kernels, body(): pl.pallas_call(finish_kernel, in_specs=[ANY, ANY], out_specs=ANY, out_sha...  48.9 us
    pallas_call x1, Pallas kernels, body(): pl.pallas_call(send_kernel, in_specs=[ANY], out_specs=ANY, out_shape=jax....  25.1 us
    all_to_all x1, blocking collectives, body(): result = lax.all_to_all(result, 'member', 0, 0, tiled=True)  20.4 us
    pallas_call x1, Pallas kernels, body(): pl.pallas_call(solve_kernel, in_specs=[VM, VM, VM, VM], out_specs=VM, out...  8.57 us
    pallas_call x1, Pallas kernels, body(): pl.pallas_call(transform_kernel, in_specs=[VM, VM, VM], out_specs=VM, out...  8.4 us
    all_to_all x1, starting transfers between devices, body(): packed = lax.all_to_all(packed, 'member', 0, 0, tiled=True)  6.75 us
    all_to_all x1, starting transfers between devices, body(): lax.all_to_all(fields.reshape(MEMBERS, UPPER, 8, LANES), 'member', 0, 0,...  6.67 us
    unnamed x18, local copies, waits for them, and re-layouts  4.89 us
  transfers between devices with their start and end apart: 4, of which 2 were waited for; matrix products, arithmetic and copies ran while one was open for 0% of the time, Pallas kernels for 6%

profile of v1, /device:TPU:97, one launch (start us, length us, event | category | flops | bytes accessed | tf_op | source)
XLA Modules:
  0.0 143.7 jit_solution(9251596920073316787)
XLA Ops:
  0.7 0.0 copy-start
  0.7 1.4 copy-done
  2.1 0.7 copy-done.3
  2.8 0.7 copy-done.4
  3.5 0.7 copy-done.6
  4.2 0.7 copy-done.7
  4.9 0.7 copy-done.8
  5.5 1.4 pack.1
  7.0 6.8 %all-to-all-start = ((bf16[16,64,128]{2,1,0:T(8,128)(2,1)}), bf16[16,64,128]{2,1,0:T(8,128)(2,1)S(1)}, u32[]{:S(2)}, u32[]{:S(2)}) async-start(bf16[16,64,128]{2,1,0:T(8,128)(2,1)} %get-tuple-element.7), calls=%async_computation | async-start | bytes 524288 | tf_op jit(solution)/shard_map/all_to_all | solution.py:446
  13.7 0.0 copy-start.1
  13.7 25.1 %send.1 = bf16[16,3,8,8,128]{4,3,2,1,0:T(8,128)(2,1)} custom-call(bf16[3,16,8,2048]{3,2,1,0:T(8,128)(2,1)} %x_ref.5), custom_call_target="tpu_custom_call" | custom-call | tf_op jit(solution)/shard_map/send/pallas_call | solution.py:438
  38.8 0.0 copy-start.5
  38.8 0.0 all-to-all-done.r_ref
  38.8 6.7 %all-to-all-start.1 = ((bf16[48,8,8,128]{3,2,1,0:T(8,128)(2,1)}), bf16[48,8,8,128]{3,2,1,0:T(8,128)(2,1)S(1)}, u32[]{:S(2)}, u32[]{:S(2)}) async-start(bf16[48,8,8,128]{3,2,1,0:T(8,128)(2,1)} %bitcast.11), calls=%async_computation.1 | async-start | bytes 1572864 | tf_op jit(solution)/shard_map/all_to_all | solution.py:447
  45.5 0.0 copy-start.2
  45.5 0.4 sample.1.own
  46.0 3.4 %collective-permute-start.1 = (f32[9,56,128]{2,1,0:T(8,128)S(1)}, f32[9,56,128]{2,1,0:T(8,128)S(1)}, u32[]{:S(2)}, u32[]{:S(2)}) collective-permute-start(f32[9,56,128]{2,1,0:T(8,128)S(1)} %sample.1.own), channel_id=1, source_target_pairs={{1,0},{2,1},{3,2},{4,3},{5,4},{6,5},{7,6},{8,7},{9,8},{10,9},{11,1... | collective-permute-start | bytes 774152 | tf_op jit(solution)/shard_map/ppermute | solution.py:460
  49.4 4.7 %collective-permute-start = (f32[9,56,128]{2,1,0:T(8,128)S(1)}, f32[9,56,128]{2,1,0:T(8,128)S(1)}, u32[]{:S(2)}, u32[]{:S(2)}) collective-permute-start(f32[9,56,128]{2,1,0:T(8,128)S(1)} %sample.1.own), channel_id=1, source_target_pairs={{0,1},{1,2},{2,3},{3,4},{4,5},{5,6},{6,7},{7,8},{8,9},{9,10},{10,1... | collective-permute-start | bytes 774152 | tf_op jit(solution)/shard_map/ppermute | solution.py:459
  54.1 2.4 %collective-permute-done.1.down = f32[9,56,128]{2,1,0:T(8,128)S(1)} collective-permute-done((f32[9,56,128]{2,1,0:T(8,128)S(1)}, f32[9,56,128]{2,1,0:T(8,128)S(1)}, u32[]{:S(2)}, u32[]{:S(2)}) %collective-permute-start.1) | collective-permute-done | bytes 258080 | tf_op jit(solution)/shard_map/ppermute | solution.py:460
  56.5 0.9 collective-permute-done.up
  57.3 8.6 %solve.1.w_ref = f32[24,48,128]{2,1,0:T(8,128)S(1)} custom-call(f32[9,56,128]{2,1,0:T(8,128)S(1)} %collective-permute-done.up, f32[9,56,128]{2,1,0:T(8,128)S(1)} %sample.1.own, f32[9,56,128]{2,1,0:T(8,128)S(1)} %collective-permute-done.1.down, f32[24,128]{1,0:T(8,128)S(1)} %copy-done.5), custom_call_target="tpu_custom_call" | custom-call | tf_op jit(solution)/shard_map/solve/pallas_call | solution.py:461
  65.9 8.4 %transform.1 = bf16[48,8,8,128]{3,2,1,0:T(8,128)(2,1)S(1)} custom-call(f32[24,48,128]{2,1,0:T(8,128)S(1)} %solve.1.w_ref, bf16[48,8,8,128]{3,2,1,0:T(8,128)(2,1)S(1)} %all-to-all-done.1.x_ref, bf16[256,512]{1,0:T(8,128)(2,1)S(1)} %copy-done.2), custom_call_target="tpu_custom_call" | custom-call | tf_op jit(solution)/shard_map/transform/pallas_call | solution.py:475
  74.4 20.4 %all_to_all.15 = bf16[48,8,8,128]{3,2,1,0:T(8,128)(2,1)} all-to-all(bf16[48,8,8,128]{3,2,1,0:T(8,128)(2,1)S(1)} %transform.1), channel_id=1, replica_groups=mesh['member'=16,'tile'=16] {'member'}, dimensions={0} | all-to-all | bytes 1572864 | tf_op jit(solution)/shard_map/all_to_all | solution.py:487
  94.8 48.9 %finish.1 = bf16[3,16,8,2048]{3,2,1,0:T(8,128)(2,1)} custom-call(bf16[16,3,8,8,128]{4,3,2,1,0:T(8,128)(2,1)} %bitcast.12, bf16[3,16,8,2048]{3,2,1,0:T(8,128)(2,1)} %x_ref.5), custom_call_target="tpu_custom_call" | custom-call | tf_op jit(solution)/shard_map/finish/pallas_call | solution.py:488
  (9 shorter events, 0.0 us)
Async XLA Ops:
  0.7 1.4 copy-start
  2.1 0.7 copy-start.3
  2.8 0.7 copy-start.4
  3.5 0.7 copy-start.6
  4.2 0.7 copy-start.7
  4.9 0.7 copy-start.8
  7.0 31.9 %all-to-all-start = ((bf16[16,64,128]{2,1,0:T(8,128)(2,1)}), bf16[16,64,128]{2,1,0:T(8,128)(2,1)S(1)}, u32[]{:S(2)}, u32[]{:S(2)}) async-start(bf16[16,64,128]{2,1,0:T(8,128)(2,1)} %get-tuple-element.7), calls=%async_computation | async-start | bytes 524288 | tf_op jit(solution)/shard_map/all_to_all | solution.py:446
  13.7 31.8 %copy-start.1 = (bf16[504,1024]{1,0:T(8,128)(2,1)S(1)}, bf16[504,1024]{1,0:T(8,128)(2,1)}, u32[]{:S(2)}) copy-start(bf16[504,1024]{1,0:T(8,128)(2,1)} %constant.17.clone.choose) | copy-start | bytes 3096580
  38.8 18.5 %copy-start.5 = (f32[24,128]{1,0:T(8,128)S(1)}, f32[24,128]{1,0:T(8,128)}, u32[]{:S(2)}) copy-start(f32[24,128]{1,0:T(8,128)} %constant.18.clone.taper) | copy-start | bytes 36868
  38.8 27.1 %all-to-all-start.1 = ((bf16[48,8,8,128]{3,2,1,0:T(8,128)(2,1)}), bf16[48,8,8,128]{3,2,1,0:T(8,128)(2,1)S(1)}, u32[]{:S(2)}, u32[]{:S(2)}) async-start(bf16[48,8,8,128]{3,2,1,0:T(8,128)(2,1)} %bitcast.11), calls=%async_computation.1 | async-start | bytes 1572864 | tf_op jit(solution)/shard_map/all_to_all | solution.py:447
  45.5 20.4 %copy-start.2 = (bf16[256,512]{1,0:T(8,128)(2,1)S(1)}, bf16[256,512]{1,0:T(8,128)(2,1)}, u32[]{:S(2)}) copy-start(bf16[256,512]{1,0:T(8,128)(2,1)} %constant.19.clone.expand) | copy-start | bytes 786436
  46.0 10.5 %collective-permute-start.1 = (f32[9,56,128]{2,1,0:T(8,128)S(1)}, f32[9,56,128]{2,1,0:T(8,128)S(1)}, u32[]{:S(2)}, u32[]{:S(2)}) collective-permute-start(f32[9,56,128]{2,1,0:T(8,128)S(1)} %sample.1.own), channel_id=1, source_target_pairs={{1,0},{2,1},{3,2},{4,3},{5,4},{6,5},{7,6},{8,7},{9,8},{10,9},{11,1... | collective-permute-start | bytes 774152 | tf_op jit(solution)/shard_map/ppermute | solution.py:460
  49.4 7.9 %collective-permute-start = (f32[9,56,128]{2,1,0:T(8,128)S(1)}, f32[9,56,128]{2,1,0:T(8,128)S(1)}, u32[]{:S(2)}, u32[]{:S(2)}) collective-permute-start(f32[9,56,128]{2,1,0:T(8,128)S(1)} %sample.1.own), channel_id=1, source_target_pairs={{0,1},{1,2},{2,3},{3,4},{4,5},{5,6},{6,7},{7,8},{8,9},{9,10},{10,1... | collective-permute-start | bytes 774152 | tf_op jit(solution)/shard_map/ppermute | solution.py:459

commit v2 on v1

--- a/solution.py
+++ b/solution.py
@@ -363,59 +363,52 @@
     lax.fori_loop(0, 24, pair, 0)
 
 
-def send_kernel(x_ref, out, sems):
+def send_kernel(x_ref, out):
+    for d in range(DOMS):
+        for m in range(3):
+            out[d, m] = x_ref[m, :, :, d * LANES : (d + 1) * LANES]
+
+
+def lower_kernel(x_ref, out):
+    out[...] = x_ref[...]
+
+
+def finish_kernel(b_ref, partial, out, work, sems):
+    del partial
     copies = []
-    for d in range(DOMS):
-        copies.append(
-            pltpu.make_async_copy(
-                x_ref.at[:, 0:UPPER, :, pl.ds(d * LANES, LANES)], out.at[d], sems.at[d]
-            )
-        )
-    for c in copies:
-        c.start()
-    for c in copies:
-        c.wait()
-
-
-def finish_kernel(b_ref, x_ref, out, sems):
-    copies = [
-        pltpu.make_async_copy(
-            x_ref.at[:, UPPER : 2 * UPPER], out.at[:, UPPER : 2 * UPPER], sems.at[DOMS]
-        )
-    ]
-    for d in range(DOMS):
-        copies.append(
-            pltpu.make_async_copy(
-                b_ref.at[d], out.at[:, 0:UPPER, :, pl.ds(d * LANES, LANES)], sems.at[d]
-            )
-        )
-    for c in copies:
-        c.start()
-    for c in copies:
-        c.wait()
+    for m in range(3):
+        for d in range(DOMS):
+            work[m, :, :, d * LANES : (d + 1) * LANES] = b_ref[d, m]
+        copy = pltpu.make_async_copy(work.at[m], out.at[m, 0:UPPER], sems.at[m])
+        copy.start()
+        copies.append(copy)
+    for copy in copies:
+        copy.wait()
 
 
 VM = pl.BlockSpec(memory_space=pltpu.VMEM)
 SM = pl.BlockSpec(memory_space=pltpu.SMEM)
 ANY = pl.BlockSpec(memory_space=pl.ANY)
+FULL = pltpu.CompilerParams(vmem_limit_bytes=62000000)
 LIMIT = pltpu.CompilerParams(vmem_limit_bytes=48 * 2**20)
 
 
 def body(prior, reading, error, cell, tally):
     me = lax.axis_index("member").astype(jnp.int32).reshape(1)
     const = lambda a, t: jnp.asarray(a, t)
+    whole = lambda *shape: pl.BlockSpec(shape, lambda g: (0,) * len(shape))
     packed, own = pl.pallas_call(
         pack_kernel,
         grid=(1,),
         in_specs=[
             SM,
             SM,
-            pl.BlockSpec((3, 2, 8, 2048), lambda g: (0, 0, 0, 0)),
-            VM,
-            VM,
-            VM,
-            VM,
-            VM,
+            whole(3, 2, 8, 2048),
+            whole(1, SLOTS),
+            whole(1, SLOTS),
+            whole(1, SLOTS),
+            whole(64, 48),
+            whole(ROWS, 80),
         ],
         out_specs=[VM, VM],
         out_shape=[
@@ -423,7 +416,7 @@
             jax.ShapeDtypeStruct((16, LANES), F32),
         ],
         scratch_shapes=[pltpu.VMEM((DOMS, 80, LANES), F32)],
-        compiler_params=LIMIT,
+        compiler_params=FULL,
         name="pack",
     )(
         me,
@@ -437,11 +430,22 @@
     )
     fields = pl.pallas_call(
         send_kernel,
-        in_specs=[ANY],
-        out_specs=ANY,
+        grid=(1,),
+        in_specs=[whole(3, UPPER, 8, 2048)],
+        out_specs=VM,
         out_shape=jax.ShapeDtypeStruct((DOMS, 3, UPPER, 8, LANES), BF16),
-        scratch_shapes=[pltpu.SemaphoreType.DMA((DOMS,))],
+        compiler_params=FULL,
         name="send",
+    )(prior)
+    lower = pl.BlockSpec((1, UPPER, 8, 2048), lambda g: (g, 1, 0, 0))
+    partial = pl.pallas_call(
+        lower_kernel,
+        grid=(3,),
+        in_specs=[lower],
+        out_specs=lower,
+        out_shape=jax.ShapeDtypeStruct(prior.shape, BF16),
+        compiler_params=FULL,
+        name="lower",
     )(prior)
     packed = lax.all_to_all(packed, "member", 0, 0, tiled=True)
     fields = lax.all_to_all(
@@ -487,12 +491,17 @@
     result = lax.all_to_all(result, "member", 0, 0, tiled=True)
     return pl.pallas_call(
         finish_kernel,
-        in_specs=[ANY, ANY],
+        in_specs=[VM, ANY],
         out_specs=ANY,
         out_shape=jax.ShapeDtypeStruct(prior.shape, BF16),
-        scratch_shapes=[pltpu.SemaphoreType.DMA((DOMS + 1,))],
+        scratch_shapes=[
+            pltpu.VMEM((3, UPPER, 8, 2048), BF16),
+            pltpu.SemaphoreType.DMA((3,)),
+        ],
+        input_output_aliases={1: 0},
+        compiler_params=LIMIT,
         name="finish",
-    )(result.reshape(DOMS, 3, UPPER, 8, LANES), prior)
+    )(result.reshape(DOMS, 3, UPPER, 8, LANES), partial)
 
 
 def solution(mesh):

time: 145 us -> 74.5 us (0.51)
  Pallas kernels: 92.8 us -> 26.7 us
  blocking collectives: 20.4 us -> 0 us
  waiting for transfers between devices: 3.26 us -> 20 us
  local copies, waits for them, and re-layouts: 4.89 us -> 0.02 us
  starting transfers between devices: 21.5 us -> 25.9 us
    pallas_call x3 -> x4, Pallas kernels: 75.4 us -> 8.43 us  [the longest x1 2.86 us: body(): pl.pallas_call(lower_kernel, grid=(3,), in_specs=[lower], out_specs=lower...]
    all_to_all x1 -> x0, blocking collectives: 20.4 us -> none  [body(): result = lax.all_to_all(result, 'member', 0, 0, tiled=True)]
    all_to_all x0 -> x1, waiting for transfers between devices: none -> 11.5 us  [body(): result = lax.all_to_all(result, 'member', 0, 0, tiled=True)]
    all_to_all x0 -> x1, starting transfers between devices: none -> 6.93 us  [body(): result = lax.all_to_all(result, 'member', 0, 0, tiled=True)]
    all_to_all x1, waiting for transfers between devices: 0.01 us -> 5.19 us  [body(): packed = lax.all_to_all(packed, 'member', 0, 0, tiled=True)]
    unnamed x18 -> x8, local copies, waits for them, and re-layouts: 4.89 us -> 0.02 us
    all_to_all x1, starting transfers between devices: 6.67 us -> 3.61 us  [body(): lax.all_to_all(fields.reshape(MEMBERS, UPPER, 8, LANES), 'member', 0, 0,...]
  transfers between devices with their start and end apart: 4 -> 5, of which waited for: 2 -> 4; matrix products, arithmetic and copies ran while one was open for 0% -> 0% of each run, Pallas kernels for 6% -> 16%
where the time goes in v2:
time: 74.5 us; the launch traced here: 73.4 us
  Pallas kernels  26.7 us (36%)
  starting transfers between devices  25.9 us (35%)
  waiting for transfers between devices  20 us (27%)
  between operations  0.76 us (1%)
    all_to_all x1, waiting for transfers between devices, body(): result = lax.all_to_all(result, 'member', 0, 0, tiled=True)  11.5 us
    pallas_call x1, Pallas kernels, body(): pl.pallas_call(transform_kernel, in_specs=[VM, VM, VM], out_specs=VM, out...  9.28 us
    pallas_call x1, Pallas kernels, body(): pl.pallas_call(solve_kernel, in_specs=[VM, VM, VM, VM], out_specs=VM, out...  8.58 us
    all_to_all x1, starting transfers between devices, body(): result = lax.all_to_all(result, 'member', 0, 0, tiled=True)  6.93 us
    all_to_all x1, starting transfers between devices, body(): packed = lax.all_to_all(packed, 'member', 0, 0, tiled=True)  6.75 us
    all_to_all x1, waiting for transfers between devices, body(): packed = lax.all_to_all(packed, 'member', 0, 0, tiled=True)  5.19 us
    ppermute x1, starting transfers between devices, body(): up = lax.ppermute(sampled, 'tile', [(i, i + 1) for i in range(ends)])  4.66 us
    ppermute x1, starting transfers between devices, body(): down = lax.ppermute(sampled, 'tile', [(i + 1, i) for i in range(ends)])  3.94 us
  transfers between devices with their start and end apart: 5, of which 4 were waited for; matrix products, arithmetic and copies ran while one was open for 0% of the time, Pallas kernels for 16%

profile of v2, /device:TPU:97, one launch (start us, length us, event | category | flops | bytes accessed | tf_op | source)
XLA Modules:
  0.0 73.4 jit_solution(9126363005513334234)
XLA Ops:
  0.7 2.4 %pack.1 = (bf16[16,64,128]{2,1,0:T(8,128)(2,1)}, f32[16,128]{1,0:T(8,128)}) custom-call(s32[1]{0:T(128)} %bitcast.where, s32[1]{0:T(128)} %bitcast.7.tally, bf16[3,16,8,2048]{3,2,1,0:T(8,128)(2,1)} %x_ref.5, f32[1,256]{1,0:T(1,128)} %bitcast.10, f32[1,256]{1,0:T(1,128)} %bitcast.11, s32[1,256]{1,0:T(1,128)} %bitcast.12, ...), custom_call_target="tpu_custom_call" | custom-call | tf_op jit(solution)/shard_map/pack/pallas_call | solution.py:400
  3.0 6.8 %all-to-all-start = ((bf16[16,64,128]{2,1,0:T(8,128)(2,1)}), bf16[16,64,128]{2,1,0:T(8,128)(2,1)S(1)}, u32[]{:S(2)}, u32[]{:S(2)}) async-start(bf16[16,64,128]{2,1,0:T(8,128)(2,1)} %get-tuple-element.7), calls=%async_computation | async-start | bytes 524288 | tf_op jit(solution)/shard_map/all_to_all | solution.py:450
  9.8 0.0 copy-start
  9.8 0.0 copy-start.3
  9.8 2.2 %send.1 = bf16[16,3,8,8,128]{4,3,2,1,0:T(8,128)(2,1)} custom-call(bf16[3,16,8,2048]{3,2,1,0:T(8,128)(2,1)} %x_ref.5), custom_call_target="tpu_custom_call" | custom-call | tf_op jit(solution)/shard_map/send/pallas_call | solution.py:431
  12.1 5.2 %all-to-all-done.r_ref = bf16[16,64,128]{2,1,0:T(8,128)(2,1)S(1)} async-done(((bf16[16,64,128]{2,1,0:T(8,128)(2,1)}), bf16[16,64,128]{2,1,0:T(8,128)(2,1)S(1)}, u32[]{:S(2)}, u32[]{:S(2)}) %all-to-all-start) | async-done | bytes 262176 | tf_op jit(solution)/shard_map/all_to_all | solution.py:450
  17.3 3.6 %all-to-all-start.1 = ((bf16[48,8,8,128]{3,2,1,0:T(8,128)(2,1)}), bf16[48,8,8,128]{3,2,1,0:T(8,128)(2,1)S(1)}, u32[]{:S(2)}, u32[]{:S(2)}) async-start(bf16[48,8,8,128]{3,2,1,0:T(8,128)(2,1)} %bitcast.9), calls=%async_computation.1 | async-start | bytes 1572864 | tf_op jit(solution)/shard_map/all_to_all | solution.py:451
  20.9 0.0 copy-start.1
  20.9 0.0 copy-done
  20.9 0.0 copy-done.3
  20.9 0.4 sample.1.own
  21.4 3.9 %collective-permute-start.1 = (f32[9,56,128]{2,1,0:T(8,128)S(1)}, f32[9,56,128]{2,1,0:T(8,128)S(1)}, u32[]{:S(2)}, u32[]{:S(2)}) collective-permute-start(f32[9,56,128]{2,1,0:T(8,128)S(1)} %sample.1.own), channel_id=1, source_target_pairs={{1,0},{2,1},{3,2},{4,3},{5,4},{6,5},{7,6},{8,7},{9,8},{10,9},{11,1... | collective-permute-start | bytes 774152 | tf_op jit(solution)/shard_map/ppermute | solution.py:464
  25.3 4.7 %collective-permute-start = (f32[9,56,128]{2,1,0:T(8,128)S(1)}, f32[9,56,128]{2,1,0:T(8,128)S(1)}, u32[]{:S(2)}, u32[]{:S(2)}) collective-permute-start(f32[9,56,128]{2,1,0:T(8,128)S(1)} %sample.1.own), channel_id=1, source_target_pairs={{0,1},{1,2},{2,3},{3,4},{4,5},{5,6},{6,7},{7,8},{8,9},{9,10},{10,1... | collective-permute-start | bytes 774152 | tf_op jit(solution)/shard_map/ppermute | solution.py:463
  30.0 2.4 %collective-permute-done.1.down = f32[9,56,128]{2,1,0:T(8,128)S(1)} collective-permute-done((f32[9,56,128]{2,1,0:T(8,128)S(1)}, f32[9,56,128]{2,1,0:T(8,128)S(1)}, u32[]{:S(2)}, u32[]{:S(2)}) %collective-permute-start.1) | collective-permute-done | bytes 258080 | tf_op jit(solution)/shard_map/ppermute | solution.py:464
  32.3 0.9 %collective-permute-done.up = f32[9,56,128]{2,1,0:T(8,128)S(1)} collective-permute-done((f32[9,56,128]{2,1,0:T(8,128)S(1)}, f32[9,56,128]{2,1,0:T(8,128)S(1)}, u32[]{:S(2)}, u32[]{:S(2)}) %collective-permute-start) | collective-permute-done | bytes 258080 | tf_op jit(solution)/shard_map/ppermute | solution.py:463
  33.2 0.0 copy-done.2
  33.2 8.6 %solve.1.w_ref = f32[24,48,128]{2,1,0:T(8,128)S(1)} custom-call(f32[9,56,128]{2,1,0:T(8,128)S(1)} %collective-permute-done.up, f32[9,56,128]{2,1,0:T(8,128)S(1)} %sample.1.own, f32[9,56,128]{2,1,0:T(8,128)S(1)} %collective-permute-done.1.down, f32[24,128]{1,0:T(8,128)S(1)} %copy-done.2), custom_call_target="tpu_custom_call" | custom-call | tf_op jit(solution)/shard_map/solve/pallas_call | solution.py:465
  41.8 0.0 all-to-all-done.1.x_ref
  41.8 0.0 copy-done.1
  41.8 9.3 %transform.1 = bf16[48,8,8,128]{3,2,1,0:T(8,128)(2,1)} custom-call(f32[24,48,128]{2,1,0:T(8,128)S(1)} %solve.1.w_ref, bf16[48,8,8,128]{3,2,1,0:T(8,128)(2,1)S(1)} %all-to-all-done.1.x_ref, bf16[256,512]{1,0:T(8,128)(2,1)S(1)} %copy-done.1), custom_call_target="tpu_custom_call" | custom-call | tf_op jit(solution)/shard_map/transform/pallas_call | solution.py:479
  51.1 6.9 %all-to-all-start.2 = ((bf16[48,8,8,128]{3,2,1,0:T(8,128)(2,1)}), bf16[48,8,8,128]{3,2,1,0:T(8,128)(2,1)S(1)}, u32[]{:S(2)}, u32[]{:S(2)}) async-start(bf16[48,8,8,128]{3,2,1,0:T(8,128)(2,1)} %transform.1), calls=%async_computation.2 | async-start | bytes 1572864 | tf_op jit(solution)/shard_map/all_to_all | solution.py:491
  58.1 2.9 %lower.1.partial = bf16[3,16,8,2048]{3,2,1,0:T(8,128)(2,1)} custom-call(bf16[3,16,8,2048]{3,2,1,0:T(8,128)(2,1)} %x_ref.5), custom_call_target="tpu_custom_call" | custom-call | tf_op jit(solution)/shard_map/lower/pallas_call | solution.py:441
  60.9 11.5 %all-to-all-done.2 = bf16[48,8,8,128]{3,2,1,0:T(8,128)(2,1)S(1)} async-done(((bf16[48,8,8,128]{3,2,1,0:T(8,128)(2,1)}), bf16[48,8,8,128]{3,2,1,0:T(8,128)(2,1)S(1)}, u32[]{:S(2)}, u32[]{:S(2)}) %all-to-all-start.2) | async-done | bytes 786464 | tf_op jit(solution)/shard_map/all_to_all | solution.py:491
  72.4 0.9 %finish.1 = bf16[3,16,8,2048]{3,2,1,0:T(8,128)(2,1)} custom-call(bf16[16,3,8,8,128]{4,3,2,1,0:T(8,128)(2,1)S(1)} %bitcast.8, bf16[3,16,8,2048]{3,2,1,0:T(8,128)(2,1)} %lower.1.partial), custom_call_target="tpu_custom_call", output_to_operand_aliasing={{}: (1, {})} | custom-call | tf_op jit(solution)/shard_map/finish/pallas_call | solution.py:492
  (1 shorter events, 0.0 us)
Async XLA Ops:
  3.0 14.2 %all-to-all-start = ((bf16[16,64,128]{2,1,0:T(8,128)(2,1)}), bf16[16,64,128]{2,1,0:T(8,128)(2,1)S(1)}, u32[]{:S(2)}, u32[]{:S(2)}) async-start(bf16[16,64,128]{2,1,0:T(8,128)(2,1)} %get-tuple-element.7), calls=%async_computation | async-start | bytes 524288 | tf_op jit(solution)/shard_map/all_to_all | solution.py:450
  9.8 11.1 %copy-start = (bf16[504,1024]{1,0:T(8,128)(2,1)S(1)}, bf16[504,1024]{1,0:T(8,128)(2,1)}, u32[]{:S(2)}) copy-start(bf16[504,1024]{1,0:T(8,128)(2,1)} %constant.17.clone.choose) | copy-start | bytes 3096580
  9.8 11.1 %copy-start.3 = (f32[16,128]{1,0:T(8,128)S(1)}, f32[16,128]{1,0:T(8,128)}, u32[]{:S(2)}) copy-start(f32[16,128]{1,0:T(8,128)} %get-tuple-element.8.own) | copy-start | bytes 24580
  12.1 21.2 %copy-start.2 = (f32[24,128]{1,0:T(8,128)S(1)}, f32[24,128]{1,0:T(8,128)}, u32[]{:S(2)}) copy-start(f32[24,128]{1,0:T(8,128)} %constant.18.clone.taper) | copy-start | bytes 36868
  17.3 24.6 %all-to-all-start.1 = ((bf16[48,8,8,128]{3,2,1,0:T(8,128)(2,1)}), bf16[48,8,8,128]{3,2,1,0:T(8,128)(2,1)S(1)}, u32[]{:S(2)}, u32[]{:S(2)}) async-start(bf16[48,8,8,128]{3,2,1,0:T(8,128)(2,1)} %bitcast.9), calls=%async_computation.1 | async-start | bytes 1572864 | tf_op jit(solution)/shard_map/all_to_all | solution.py:451
  20.9 20.9 %copy-start.1 = (bf16[256,512]{1,0:T(8,128)(2,1)S(1)}, bf16[256,512]{1,0:T(8,128)(2,1)}, u32[]{:S(2)}) copy-start(bf16[256,512]{1,0:T(8,128)(2,1)} %constant.19.clone.expand) | copy-start | bytes 786436
  21.4 11.0 %collective-permute-start.1 = (f32[9,56,128]{2,1,0:T(8,128)S(1)}, f32[9,56,128]{2,1,0:T(8,128)S(1)}, u32[]{:S(2)}, u32[]{:S(2)}) collective-permute-start(f32[9,56,128]{2,1,0:T(8,128)S(1)} %sample.1.own), channel_id=1, source_target_pairs={{1,0},{2,1},{3,2},{4,3},{5,4},{6,5},{7,6},{8,7},{9,8},{10,9},{11,1... | collective-permute-start | bytes 774152 | tf_op jit(solution)/shard_map/ppermute | solution.py:464
  25.3 7.9 %collective-permute-start = (f32[9,56,128]{2,1,0:T(8,128)S(1)}, f32[9,56,128]{2,1,0:T(8,128)S(1)}, u32[]{:S(2)}, u32[]{:S(2)}) collective-permute-start(f32[9,56,128]{2,1,0:T(8,128)S(1)} %sample.1.own), channel_id=1, source_target_pairs={{0,1},{1,2},{2,3},{3,4},{4,5},{5,6},{6,7},{7,8},{8,9},{9,10},{10,1... | collective-permute-start | bytes 774152 | tf_op jit(solution)/shard_map/ppermute | solution.py:463
  51.1 21.3 %all-to-all-start.2 = ((bf16[48,8,8,128]{3,2,1,0:T(8,128)(2,1)}), bf16[48,8,8,128]{3,2,1,0:T(8,128)(2,1)S(1)}, u32[]{:S(2)}, u32[]{:S(2)}) async-start(bf16[48,8,8,128]{3,2,1,0:T(8,128)(2,1)} %transform.1), calls=%async_computation.2 | async-start | bytes 1572864 | tf_op jit(solution)/shard_map/all_to_all | solution.py:491

commit v3 on v2

--- a/solution.py
+++ b/solution.py
@@ -99,7 +99,7 @@
     for h in range(2):
         for p in range(2):
             for y in range(128):
-                m[h * 64 + p * 32 + y // 4, h * 256 + p * 128 + y] = 1.0
+                m[p * 64 + h * 32 + y // 4, h * 256 + p * 128 + y] = 1.0
     return np.concatenate([m, m], 0)
 
 
@@ -180,108 +180,105 @@
 def solve_kernel(up, own, down, taper, out, grams, mat, piv, fac):
     segs = (up, own, down)
     lane = lax.broadcasted_iota(jnp.int32, (1, LANES), 1) % CHUNK
-
-    def group(g, carry):
-        before = jnp.where(g == 0, 8, g - 1)
-        after = jnp.where(g == 7, 8, g + 1)
+    first = lax.broadcasted_iota(jnp.int32, (16, LANES), 0) == 0
+    for g in range(GROUPS):
         for k, o in enumerate(OFFSETS):
-            v0, v1 = (before, g) if k < 2 else (g, after)
+            v0 = g - 1 if k < 2 else g
+            v1 = v0 + 1
+            v0, v1 = (8 if v in (-1, 8) else v for v in (v0, v1))
             mask = lane >= o
-            ahi, alo = [], []
-            lhi, llo = [], []
+            shi, slo, whi, wlo = [], [], [], []
             for s in range(3):
                 w = jnp.where(mask, segs[s][v0], segs[s][v1])
                 a = w[0:48]
                 prec, drv = w[48:49], w[49:50]
-                h, l = split2(a)
-                ahi.append(h)
-                alo.append(l)
-                t0 = taper[(k * 3 + s) * 2 : (k * 3 + s) * 2 + 1, :]
-                t1 = taper[(k * 3 + s) * 2 + 1 : (k * 3 + s) * 2 + 2, :]
-                sub = lax.broadcasted_iota(jnp.int32, (16, LANES), 0)
-                lhs = jnp.concatenate(
-                    [
-                        a * (prec * t0),
-                        a * (prec * t1),
-                        jnp.where(sub == 0, drv * t0, jnp.where(sub == 1, drv * t1, 0.0)),
-                    ],
-                    0,
+                row = (k * 3 + s) * 2
+                stream = jnp.concatenate([a * prec, jnp.where(first, drv, 0.0)], 0)
+                h, l = split2(stream)
+                shi.append(h)
+                slo.append(l)
+                h, l = split2(
+                    jnp.concatenate([a * taper[row : row + 1, :], a * taper[row + 1 : row + 2, :]], 0)
                 )
-                h, l = split2(lhs)
-                lhi.append(h)
-                llo.append(l)
-            left = jnp.concatenate(lhi + lhi + llo, 1)
-            right = jnp.concatenate(ahi + alo + ahi, 1)
-            res = nt(left, right)
+                whi.append(h)
+                wlo.append(l)
+            stream = jnp.concatenate(
+                [jnp.concatenate(shi + shi, 1), jnp.concatenate(slo + slo, 1)], 0
+            )
+            res = nt(stream, jnp.concatenate(whi + wlo, 1))
+            res = res[0:56] + res[64:120]
+            res = jnp.concatenate([res, jnp.zeros((56, LANES - 2 * MEMBERS), F32)], 1)
             q = g * 4 + k
-            res = jnp.concatenate([res, jnp.zeros((112, LANES - MEMBERS), F32)], 1)
-            row0 = pl.multiple_of(q * PACK, 8)
-            row1 = pl.multiple_of((q + BLOCKS_Y) * PACK, 8)
-            grams[pl.ds(row0, 48), :] = res[0:48]
-            grams[pl.ds(row0 + 48, 8), :] = res[96:104]
-            grams[pl.ds(row1, 48), :] = res[48:96]
-            grams[pl.ds(row1 + 48, 8), :] = pltpu.roll(res[96:104], 7, 0)
-        return carry
-
-    lax.fori_loop(0, 8, group, 0)
-
-    for t in range(25):
-        a = grams[pl.ds(2 * t, 64, stride=PACK), :]
-        b = grams[pl.ds(2 * t + 1, 64, stride=PACK), :] if t < 24 else a
-        mat[t] = jnp.concatenate([a, b], 0).T[0:48, :]
+            grams[q * PACK : (q + 1) * PACK, :] = res
 
     sub = lax.broadcasted_iota(jnp.int32, (8, LANES), 0)
-    half = lax.broadcasted_iota(jnp.int32, (8, LANES), 1) // 64
+    half = (lax.broadcasted_iota(jnp.int32, (8, LANES), 1) // 32) % 2
     half0 = half == 0
-
-    def tiles(t):
-        return [mat[t, 8 * j : 8 * j + 8, :] for j in range(6)]
-
-    drive = tiles(24)
+    low = lax.broadcasted_iota(jnp.int32, (48, LANES), 1) < 64
+
+    def columns(js):
+        t = jnp.concatenate([grams[pl.ds(j, 32, stride=PACK), :] for j in js], 0).T
+        return t[0:48], t[48:96]
+
+    for j in range(12):
+        t0, t1 = columns(range(4 * j, 4 * j + 4))
+        mat[2 * j] = jnp.where(low, t0, pltpu.roll(t1, 64, 1))
+        mat[2 * j + 1] = jnp.where(low, pltpu.roll(t0, 64, 1), t1)
+    t0, t1 = columns([48] * 4)
+    drive = jnp.where(low, t0, t1)
+    drive = [drive[8 * j : 8 * j + 8] for j in range(6)]
+
+    def bcast(x, k):
+        return jnp.broadcast_to(x[k : k + 1, :], (8, LANES))
+
+    def both(x, h):
+        return jnp.where(half == h, x, pltpu.roll(x, 32 if h == 0 else 96, 1))
+
     scale = []
     for panel in range(6):
-        rows = [tiles(4 * panel + n) for n in range(4)]
-        for n in range(4):
-            diag = jnp.where(sub == 2 * n + half, MEMBERS - 1.0, 0.0)
-            rows[n][panel] = rows[n][panel] + diag
+        buf = panel % 2
+        others = [j for j in range(6) if j != panel]
+        rows = [
+            [mat[4 * panel + n, 8 * j : 8 * j + 8, :] for j in range(6)] for n in range(4)
+        ]
+        d = [both(rows[r // 2][panel], r % 2) for r in range(8)]
+        d = [jnp.where(sub == r, d[r] + (MEMBERS - 1.0), d[r]) for r in range(8)]
+        invs, fds = [], []
         for k in range(8):
-            n, h = k // 2, k % 2
-            mine = half == h
-            row = [jnp.where(mine, x, pltpu.roll(x, 64, 1)) for x in rows[n]]
-            inv = 1.0 / jnp.broadcast_to(row[panel][k : k + 1, :], (8, LANES))
+            inv = 1.0 / bcast(d[k], k)
+            invs.append(inv)
             scale.append(jnp.sqrt((MEMBERS - 1.0) * inv[0:1, :]))
             here = sub == k
-            f = row[panel] * inv
-            for j in range(panel + 1, 6):
-                fac[k, 8 * j : 8 * j + 8, :] = row[j] * inv
-            row[panel] = jnp.where(here, 1.0, row[panel])
-            for j in range(6):
-                if j != panel:
-                    piv[k, 8 * j : 8 * j + 8, :] = row[j]
-            piv[k, 8 * panel : 8 * panel + 8, :] = jnp.where(sub <= k, row[panel], 0.0)
-            fd = jnp.broadcast_to(drive[panel][k : k + 1, :], (8, LANES)) * inv
-            drive[panel] = jnp.where(here, 0.0, drive[panel])
-            drive = [drive[j] - fd * row[j] for j in range(6)]
-            for n2 in range(n, 4):
-                if n2 == n and h == 1:
-                    rows[n][panel] = jnp.where(
-                        jnp.logical_and(here, mine), 1.0, rows[n][panel]
+            row = jnp.where(here, 1.0, d[k])
+            for r in range(k + 1, 8):
+                d[r] = jnp.where(here, 0.0, d[r]) - (bcast(d[k], r) * inv) * row
+            fd = bcast(drive[panel], k) * inv
+            fds.append(fd)
+            drive[panel] = jnp.where(here, 0.0, drive[panel]) - fd * row
+            d[k] = jnp.where(sub <= k, row, 0.0)
+            piv[buf, k, 8 * panel : 8 * panel + 8, :] = d[k]
+        for n in range(4):
+            mat[4 * panel + n, 8 * panel : 8 * panel + 8, :] = jnp.where(
+                half0, d[2 * n], d[2 * n + 1]
+            )
+        eb = [[bcast(d[r], c) for c in range(r)] for r in range(8)]
+        for j in others:
+            x = [both(rows[r // 2][j], r % 2) for r in range(8)]
+            y = []
+            for r in range(8):
+                t = x[r]
+                for c in range(r):
+                    t = t + eb[r][c] * x[c]
+                y.append(t)
+                piv[buf, r, 8 * j : 8 * j + 8, :] = t
+                if j > panel:
+                    fac[buf, r, 8 * j : 8 * j + 8, :] = t * invs[r]
+                drive[j] = drive[j] - fds[r] * t
+            if j < panel:
+                for n in range(4):
+                    mat[4 * panel + n, 8 * j : 8 * j + 8, :] = jnp.where(
+                        half0, y[2 * n], y[2 * n + 1]
                     )
-                    continue
-                fb = jnp.broadcast_to(f[2 * n2 + 1 : 2 * n2 + 2, :], (8, LANES))
-                if n2 == n:
-                    fp = jnp.where(half0, 0.0, fb)
-                    rows[n][panel] = jnp.where(
-                        here, jnp.where(half0, 1.0, 0.0), rows[n][panel]
-                    )
-                else:
-                    fa = jnp.broadcast_to(f[2 * n2 : 2 * n2 + 1, :], (8, LANES))
-                    fp = jnp.where(half0, fa, fb)
-                    rows[n2][panel] = jnp.where(here, 0.0, rows[n2][panel])
-                rows[n2] = [rows[n2][j] - fp * row[j] for j in range(6)]
-        for n in range(4):
-            for j in range(panel + 1):
-                mat[4 * panel + n, 8 * j : 8 * j + 8, :] = rows[n][j]
         for block in range(panel + 1, 6):
             js = list(range(panel + 1)) + list(range(block, 6))
             acc = [
@@ -294,11 +291,11 @@
                 for n in range(4)
             ]
             for k in range(8):
-                pr = {j: piv[k, 8 * j : 8 * j + 8, :] for j in js}
+                pr = {j: piv[buf, k, 8 * j : 8 * j + 8, :] for j in js}
                 for n in range(4):
                     i = 8 * block + 2 * n
-                    fa = jnp.broadcast_to(fac[k, i : i + 1, :], (8, LANES))
-                    fb = jnp.broadcast_to(fac[k, i + 1 : i + 2, :], (8, LANES))
+                    fa = jnp.broadcast_to(fac[buf, k, i : i + 1, :], (8, LANES))
+                    fb = jnp.broadcast_to(fac[buf, k, i + 1 : i + 2, :], (8, LANES))
                     fp = jnp.where(half0, fa, fb)
                     for j in js:
                         acc[n][j] = acc[n][j] - fp * pr[j]
@@ -307,16 +304,13 @@
                     mat[4 * block + n, 8 * j : 8 * j + 8, :] = acc[n][j]
 
     for t in range(24):
-        panel, n = t // 4, t % 4
+        panel = t // 4
         sc = jnp.where(half0, scale[2 * t], scale[2 * t + 1])
         w = []
         for j in range(6):
             x = -drive[j]
             if j <= panel:
-                e = mat[t, 8 * j : 8 * j + 8, :]
-                if j == panel:
-                    e = jnp.where(sub <= 2 * n + half, e, 0.0)
-                x = x + sc * e
+                x = x + sc * mat[t, 8 * j : 8 * j + 8, :]
             w.append(x)
         total = jnp.sum(w[0] + w[1] + w[2] + w[3] + w[4] + w[5], axis=0, keepdims=True)
         fix = (1.0 - total) * (1.0 / MEMBERS)
@@ -340,8 +334,8 @@
     def pair(t, c):
         def step(i, acc):
             acc = list(acc)
-            for u in range(4):
-                r = t * 48 + i * 4 + u
+            for u in range(16):
+                r = t * 48 + i * 16 + u
                 line = wide[pl.ds(r, 1), :]
                 ws = []
                 for h in range(2):
@@ -349,12 +343,12 @@
                     b = jnp.broadcast_to(line[:, h * 256 + 128 : h * 256 + 256], (8, LANES))
                     ws.append(jnp.where(top, a, b))
                 for l in range(8):
-                    x = xs[i * 4 + u, l]
+                    x = xs[i * 16 + u, l]
                     acc[l] = acc[l] + x * ws[0]
                     acc[8 + l] = acc[8 + l] + x * ws[1]
             return tuple(acc)
 
-        acc = lax.fori_loop(0, 12, step, tuple(jnp.zeros((8, LANES), F32) for _ in range(16)))
+        acc = lax.fori_loop(0, 3, step, tuple(jnp.zeros((8, LANES), F32) for _ in range(16)))
         for h in range(2):
             for l in range(8):
                 out[2 * t + h, l] = acc[8 * h + l].astype(BF16)
@@ -468,10 +462,10 @@
         out_specs=VM,
         out_shape=jax.ShapeDtypeStruct((24, 48, LANES), F32),
         scratch_shapes=[
-            pltpu.VMEM((64 * PACK, LANES), F32),
-            pltpu.VMEM((25, 48, LANES), F32),
-            pltpu.VMEM((8, 48, LANES), F32),
-            pltpu.VMEM((8, 48, LANES), F32),
+            pltpu.VMEM((BLOCKS_Y * PACK, LANES), F32),
+            pltpu.VMEM((24, 48, LANES), F32),
+            pltpu.VMEM((2, 8, 48, LANES), F32),
+            pltpu.VMEM((2, 8, 48, LANES), F32),
         ],
         compiler_params=LIMIT,
         name="solve",

time: 74.5 us -> 68 us (0.913)
  Pallas kernels: 26.7 us -> 20.3 us
    pallas_call x1, Pallas kernels: 8.58 us -> 3.93 us  [body(): pl.pallas_call(solve_kernel, in_specs=[VM, VM, VM, VM], out_specs=VM, out...]
    pallas_call x1, Pallas kernels: 9.28 us -> 7.5 us  [body(): pl.pallas_call(transform_kernel, in_specs=[VM, VM, VM], out_specs=VM, out...]
  transfers between devices with their start and end apart: 5 -> 5, of which waited for: 4 -> 4; matrix products, arithmetic and copies ran while one was open for 0% -> 0% of each run, Pallas kernels for 16% -> 11%
where the time goes in v3:
time: 68 us; the launch traced here: 67 us
  starting transfers between devices  25.9 us (38%)
  Pallas kernels  20.3 us (30%)
  waiting for transfers between devices  20 us (29%)
  between operations  0.76 us (1%)
    all_to_all x1, waiting for transfers between devices, body(): result = lax.all_to_all(result, 'member', 0, 0, tiled=True)  11.5 us
    pallas_call x1, Pallas kernels, body(): pl.pallas_call(transform_kernel, in_specs=[VM, VM, VM], out_specs=VM, out...  7.5 us
    all_to_all x1, starting transfers between devices, body(): result = lax.all_to_all(result, 'member', 0, 0, tiled=True)  6.93 us
    all_to_all x1, starting transfers between devices, body(): packed = lax.all_to_all(packed, 'member', 0, 0, tiled=True)  6.75 us
    all_to_all x1, waiting for transfers between devices, body(): packed = lax.all_to_all(packed, 'member', 0, 0, tiled=True)  5.19 us
    ppermute x1, starting transfers between devices, body(): up = lax.ppermute(sampled, 'tile', [(i, i + 1) for i in range(ends)])  4.66 us
    ppermute x1, starting transfers between devices, body(): down = lax.ppermute(sampled, 'tile', [(i + 1, i) for i in range(ends)])  3.94 us
    pallas_call x1, Pallas kernels, body(): pl.pallas_call(solve_kernel, in_specs=[VM, VM, VM, VM], out_specs=VM, out...  3.93 us
  transfers between devices with their start and end apart: 5, of which 4 were waited for; matrix products, arithmetic and copies ran while one was open for 0% of the time, Pallas kernels for 11%

profile of v3, /device:TPU:97, one launch (start us, length us, event | category | flops | bytes accessed | tf_op | source)
XLA Modules:
  0.0 67.0 jit_solution(8917053793402277004)
XLA Ops:
  0.7 2.4 %pack.1 = (bf16[16,64,128]{2,1,0:T(8,128)(2,1)}, f32[16,128]{1,0:T(8,128)}) custom-call(s32[1]{0:T(128)} %bitcast.where, s32[1]{0:T(128)} %bitcast.7.tally, bf16[3,16,8,2048]{3,2,1,0:T(8,128)(2,1)} %x_ref.5, f32[1,256]{1,0:T(1,128)} %bitcast.10, f32[1,256]{1,0:T(1,128)} %bitcast.11, s32[1,256]{1,0:T(1,128)} %bitcast.12, ...), custom_call_target="tpu_custom_call" | custom-call | tf_op jit(solution)/shard_map/pack/pallas_call | solution.py:394
  3.0 6.8 %all-to-all-start = ((bf16[16,64,128]{2,1,0:T(8,128)(2,1)}), bf16[16,64,128]{2,1,0:T(8,128)(2,1)S(1)}, u32[]{:S(2)}, u32[]{:S(2)}) async-start(bf16[16,64,128]{2,1,0:T(8,128)(2,1)} %get-tuple-element.7), calls=%async_computation | async-start | bytes 524288 | tf_op jit(solution)/shard_map/all_to_all | solution.py:444
  9.8 0.0 copy-start
  9.8 0.0 copy-start.3
  9.8 2.2 %send.1 = bf16[16,3,8,8,128]{4,3,2,1,0:T(8,128)(2,1)} custom-call(bf16[3,16,8,2048]{3,2,1,0:T(8,128)(2,1)} %x_ref.5), custom_call_target="tpu_custom_call" | custom-call | tf_op jit(solution)/shard_map/send/pallas_call | solution.py:425
  12.1 5.2 %all-to-all-done.r_ref = bf16[16,64,128]{2,1,0:T(8,128)(2,1)S(1)} async-done(((bf16[16,64,128]{2,1,0:T(8,128)(2,1)}), bf16[16,64,128]{2,1,0:T(8,128)(2,1)S(1)}, u32[]{:S(2)}, u32[]{:S(2)}) %all-to-all-start) | async-done | bytes 262176 | tf_op jit(solution)/shard_map/all_to_all | solution.py:444
  17.3 3.6 %all-to-all-start.1 = ((bf16[48,8,8,128]{3,2,1,0:T(8,128)(2,1)}), bf16[48,8,8,128]{3,2,1,0:T(8,128)(2,1)S(1)}, u32[]{:S(2)}, u32[]{:S(2)}) async-start(bf16[48,8,8,128]{3,2,1,0:T(8,128)(2,1)} %bitcast.9), calls=%async_computation.1 | async-start | bytes 1572864 | tf_op jit(solution)/shard_map/all_to_all | solution.py:445
  20.9 0.0 copy-start.1
  20.9 0.0 copy-done
  20.9 0.0 copy-done.3
  20.9 0.4 sample.1.own
  21.4 3.9 %collective-permute-start.1 = (f32[9,56,128]{2,1,0:T(8,128)S(1)}, f32[9,56,128]{2,1,0:T(8,128)S(1)}, u32[]{:S(2)}, u32[]{:S(2)}) collective-permute-start(f32[9,56,128]{2,1,0:T(8,128)S(1)} %sample.1.own), channel_id=1, source_target_pairs={{1,0},{2,1},{3,2},{4,3},{5,4},{6,5},{7,6},{8,7},{9,8},{10,9},{11,1... | collective-permute-start | bytes 774152 | tf_op jit(solution)/shard_map/ppermute | solution.py:458
  25.3 4.7 %collective-permute-start = (f32[9,56,128]{2,1,0:T(8,128)S(1)}, f32[9,56,128]{2,1,0:T(8,128)S(1)}, u32[]{:S(2)}, u32[]{:S(2)}) collective-permute-start(f32[9,56,128]{2,1,0:T(8,128)S(1)} %sample.1.own), channel_id=1, source_target_pairs={{0,1},{1,2},{2,3},{3,4},{4,5},{5,6},{6,7},{7,8},{8,9},{9,10},{10,1... | collective-permute-start | bytes 774152 | tf_op jit(solution)/shard_map/ppermute | solution.py:457
  30.0 2.4 %collective-permute-done.1.down = f32[9,56,128]{2,1,0:T(8,128)S(1)} collective-permute-done((f32[9,56,128]{2,1,0:T(8,128)S(1)}, f32[9,56,128]{2,1,0:T(8,128)S(1)}, u32[]{:S(2)}, u32[]{:S(2)}) %collective-permute-start.1) | collective-permute-done | bytes 258080 | tf_op jit(solution)/shard_map/ppermute | solution.py:458
  32.3 0.9 %collective-permute-done.up = f32[9,56,128]{2,1,0:T(8,128)S(1)} collective-permute-done((f32[9,56,128]{2,1,0:T(8,128)S(1)}, f32[9,56,128]{2,1,0:T(8,128)S(1)}, u32[]{:S(2)}, u32[]{:S(2)}) %collective-permute-start) | collective-permute-done | bytes 258080 | tf_op jit(solution)/shard_map/ppermute | solution.py:457
  33.2 0.0 copy-done.2
  33.2 3.9 %solve.1.w_ref = f32[24,48,128]{2,1,0:T(8,128)S(1)} custom-call(f32[9,56,128]{2,1,0:T(8,128)S(1)} %collective-permute-done.up, f32[9,56,128]{2,1,0:T(8,128)S(1)} %sample.1.own, f32[9,56,128]{2,1,0:T(8,128)S(1)} %collective-permute-done.1.down, f32[24,128]{1,0:T(8,128)S(1)} %copy-done.2), custom_call_target="tpu_custom_call" | custom-call | tf_op jit(solution)/shard_map/solve/pallas_call | solution.py:459
  37.2 0.0 all-to-all-done.1.x_ref
  37.2 0.0 copy-done.1
  37.2 7.5 %transform.1 = bf16[48,8,8,128]{3,2,1,0:T(8,128)(2,1)} custom-call(f32[24,48,128]{2,1,0:T(8,128)S(1)} %solve.1.w_ref, bf16[48,8,8,128]{3,2,1,0:T(8,128)(2,1)S(1)} %all-to-all-done.1.x_ref, bf16[256,512]{1,0:T(8,128)(2,1)S(1)} %copy-done.1), custom_call_target="tpu_custom_call" | custom-call | tf_op jit(solution)/shard_map/transform/pallas_call | solution.py:473
  44.7 6.9 %all-to-all-start.2 = ((bf16[48,8,8,128]{3,2,1,0:T(8,128)(2,1)}), bf16[48,8,8,128]{3,2,1,0:T(8,128)(2,1)S(1)}, u32[]{:S(2)}, u32[]{:S(2)}) async-start(bf16[48,8,8,128]{3,2,1,0:T(8,128)(2,1)} %transform.1), calls=%async_computation.2 | async-start | bytes 1572864 | tf_op jit(solution)/shard_map/all_to_all | solution.py:485
  51.6 2.9 %lower.1.partial = bf16[3,16,8,2048]{3,2,1,0:T(8,128)(2,1)} custom-call(bf16[3,16,8,2048]{3,2,1,0:T(8,128)(2,1)} %x_ref.5), custom_call_target="tpu_custom_call" | custom-call | tf_op jit(solution)/shard_map/lower/pallas_call | solution.py:435
  54.5 11.5 %all-to-all-done.2 = bf16[48,8,8,128]{3,2,1,0:T(8,128)(2,1)S(1)} async-done(((bf16[48,8,8,128]{3,2,1,0:T(8,128)(2,1)}), bf16[48,8,8,128]{3,2,1,0:T(8,128)(2,1)S(1)}, u32[]{:S(2)}, u32[]{:S(2)}) %all-to-all-start.2) | async-done | bytes 786464 | tf_op jit(solution)/shard_map/all_to_all | solution.py:485
  66.0 0.9 %finish.1 = bf16[3,16,8,2048]{3,2,1,0:T(8,128)(2,1)} custom-call(bf16[16,3,8,8,128]{4,3,2,1,0:T(8,128)(2,1)S(1)} %bitcast.8, bf16[3,16,8,2048]{3,2,1,0:T(8,128)(2,1)} %lower.1.partial), custom_call_target="tpu_custom_call", output_to_operand_aliasing={{}: (1, {})} | custom-call | tf_op jit(solution)/shard_map/finish/pallas_call | solution.py:486
  (1 shorter events, 0.0 us)
Async XLA Ops:
  3.0 14.2 %all-to-all-start = ((bf16[16,64,128]{2,1,0:T(8,128)(2,1)}), bf16[16,64,128]{2,1,0:T(8,128)(2,1)S(1)}, u32[]{:S(2)}, u32[]{:S(2)}) async-start(bf16[16,64,128]{2,1,0:T(8,128)(2,1)} %get-tuple-element.7), calls=%async_computation | async-start | bytes 524288 | tf_op jit(solution)/shard_map/all_to_all | solution.py:444
  9.8 11.1 %copy-start = (bf16[504,1024]{1,0:T(8,128)(2,1)S(1)}, bf16[504,1024]{1,0:T(8,128)(2,1)}, u32[]{:S(2)}) copy-start(bf16[504,1024]{1,0:T(8,128)(2,1)} %constant.17.clone.choose) | copy-start | bytes 3096580
  9.8 11.1 %copy-start.3 = (f32[16,128]{1,0:T(8,128)S(1)}, f32[16,128]{1,0:T(8,128)}, u32[]{:S(2)}) copy-start(f32[16,128]{1,0:T(8,128)} %get-tuple-element.8.own) | copy-start | bytes 24580
  12.1 21.2 %copy-start.2 = (f32[24,128]{1,0:T(8,128)S(1)}, f32[24,128]{1,0:T(8,128)}, u32[]{:S(2)}) copy-start(f32[24,128]{1,0:T(8,128)} %constant.18.clone.taper) | copy-start | bytes 36868
  17.3 19.9 %all-to-all-start.1 = ((bf16[48,8,8,128]{3,2,1,0:T(8,128)(2,1)}), bf16[48,8,8,128]{3,2,1,0:T(8,128)(2,1)S(1)}, u32[]{:S(2)}, u32[]{:S(2)}) async-start(bf16[48,8,8,128]{3,2,1,0:T(8,128)(2,1)} %bitcast.9), calls=%async_computation.1 | async-start | bytes 1572864 | tf_op jit(solution)/shard_map/all_to_all | solution.py:445
  20.9 16.3 %copy-start.1 = (bf16[256,512]{1,0:T(8,128)(2,1)S(1)}, bf16[256,512]{1,0:T(8,128)(2,1)}, u32[]{:S(2)}) copy-start(bf16[256,512]{1,0:T(8,128)(2,1)} %constant.19.clone.expand) | copy-start | bytes 786436
  21.4 11.0 %collective-permute-start.1 = (f32[9,56,128]{2,1,0:T(8,128)S(1)}, f32[9,56,128]{2,1,0:T(8,128)S(1)}, u32[]{:S(2)}, u32[]{:S(2)}) collective-permute-start(f32[9,56,128]{2,1,0:T(8,128)S(1)} %sample.1.own), channel_id=1, source_target_pairs={{1,0},{2,1},{3,2},{4,3},{5,4},{6,5},{7,6},{8,7},{9,8},{10,9},{11,1... | collective-permute-start | bytes 774152 | tf_op jit(solution)/shard_map/ppermute | solution.py:458
  25.3 7.9 %collective-permute-start = (f32[9,56,128]{2,1,0:T(8,128)S(1)}, f32[9,56,128]{2,1,0:T(8,128)S(1)}, u32[]{:S(2)}, u32[]{:S(2)}) collective-permute-start(f32[9,56,128]{2,1,0:T(8,128)S(1)} %sample.1.own), channel_id=1, source_target_pairs={{0,1},{1,2},{2,3},{3,4},{4,5},{5,6},{6,7},{7,8},{8,9},{9,10},{10,1... | collective-permute-start | bytes 774152 | tf_op jit(solution)/shard_map/ppermute | solution.py:457
  44.7 21.3 %all-to-all-start.2 = ((bf16[48,8,8,128]{3,2,1,0:T(8,128)(2,1)}), bf16[48,8,8,128]{3,2,1,0:T(8,128)(2,1)S(1)}, u32[]{:S(2)}, u32[]{:S(2)}) async-start(bf16[48,8,8,128]{3,2,1,0:T(8,128)(2,1)} %transform.1), calls=%async_computation.2 | async-start | bytes 1572864 | tf_op jit(solution)/shard_map/all_to_all | solution.py:485

commit v4 on v3

--- a/solution.py
+++ b/solution.py
@@ -323,12 +323,9 @@
     hi, low = split2(w)
     wide[...] = nn(jnp.concatenate([hi, low], 1), expand[...])
 
-    def widen(i, c):
+    for i in range(MEMBERS):
         for l in range(8):
             xs[i, l] = x_ref[i, l].astype(F32)
-        return c
-
-    lax.fori_loop(0, MEMBERS, widen, 0)
     top = lax.broadcasted_iota(jnp.int32, (8, LANES), 0) < 4
 
     def pair(t, c):
@@ -357,14 +354,10 @@
     lax.fori_loop(0, 24, pair, 0)
 
 
-def send_kernel(x_ref, out):
+def send_kernel(x_ref, out, lower):
     for d in range(DOMS):
-        for m in range(3):
-            out[d, m] = x_ref[m, :, :, d * LANES : (d + 1) * LANES]
-
-
-def lower_kernel(x_ref, out):
-    out[...] = x_ref[...]
+        out[d, 0] = x_ref[0, 0:UPPER, :, d * LANES : (d + 1) * LANES]
+    lower[...] = x_ref[:, UPPER : 2 * UPPER]
 
 
 def finish_kernel(b_ref, partial, out, work, sems):
@@ -422,24 +415,20 @@
         const(row_spread(), BF16),
         const(row_compact(), BF16),
     )
-    fields = pl.pallas_call(
+    fields, partial = pl.pallas_call(
         send_kernel,
-        grid=(1,),
-        in_specs=[whole(3, UPPER, 8, 2048)],
-        out_specs=VM,
-        out_shape=jax.ShapeDtypeStruct((DOMS, 3, UPPER, 8, LANES), BF16),
+        grid=(3,),
+        in_specs=[pl.BlockSpec((1, 2 * UPPER, 8, 2048), lambda g: (g, 0, 0, 0))],
+        out_specs=[
+            pl.BlockSpec((DOMS, 1, UPPER, 8, LANES), lambda g: (0, g, 0, 0, 0)),
+            pl.BlockSpec((1, UPPER, 8, 2048), lambda g: (g, 1, 0, 0)),
+        ],
+        out_shape=[
+            jax.ShapeDtypeStruct((DOMS, 3, UPPER, 8, LANES), BF16),
+            jax.ShapeDtypeStruct(prior.shape, BF16),
+        ],
         compiler_params=FULL,
         name="send",
-    )(prior)
-    lower = pl.BlockSpec((1, UPPER, 8, 2048), lambda g: (g, 1, 0, 0))
-    partial = pl.pallas_call(
-        lower_kernel,
-        grid=(3,),
-        in_specs=[lower],
-        out_specs=lower,
-        out_shape=jax.ShapeDtypeStruct(prior.shape, BF16),
-        compiler_params=FULL,
-        name="lower",
     )(prior)
     packed = lax.all_to_all(packed, "member", 0, 0, tiled=True)
     fields = lax.all_to_all(

time: 68 us -> 66 us (0.971)
  blocking collectives: 0 us -> 20.3 us
  waiting for transfers between devices: 20 us -> 7.18 us
  starting transfers between devices: 25.9 us -> 19 us
  Pallas kernels: 20.3 us -> 17.6 us
    all_to_all x0 -> x1, blocking collectives: none -> 20.3 us  [body(): result = lax.all_to_all(result, 'member', 0, 0, tiled=True)]
    all_to_all x1 -> x0, waiting for transfers between devices: 11.5 us -> none  [body(): result = lax.all_to_all(result, 'member', 0, 0, tiled=True)]
    all_to_all x1 -> x0, starting transfers between devices: 6.93 us -> none  [body(): result = lax.all_to_all(result, 'member', 0, 0, tiled=True)]
    pallas_call x2 -> x1, Pallas kernels: 5.1 us -> 3.5 us  [body(): pl.pallas_call(send_kernel, grid=(3,), in_specs=[pl.BlockSpec((1, 2 * UPP...]
    all_to_all x1, waiting for transfers between devices: 5.19 us -> 3.93 us  [body(): packed = lax.all_to_all(packed, 'member', 0, 0, tiled=True)]
    pallas_call x1, Pallas kernels: 7.5 us -> 6.35 us  [body(): pl.pallas_call(transform_kernel, in_specs=[VM, VM, VM], out_specs=VM, out...]
  transfers between devices with their start and end apart: 5 -> 4, of which waited for: 4 -> 3; matrix products, arithmetic and copies ran while one was open for 0% -> 0% of each run, Pallas kernels for 11% -> 7%
where the time goes in v4:
time: 66 us; the launch traced here: 64.8 us
  blocking collectives  20.3 us (31%)
  starting transfers between devices  19 us (29%)
  Pallas kernels  17.6 us (27%)
  waiting for transfers between devices  7.18 us (11%)
  between operations  0.76 us (1%)
    all_to_all x1, blocking collectives, body(): result = lax.all_to_all(result, 'member', 0, 0, tiled=True)  20.3 us
    all_to_all x1, starting transfers between devices, body(): packed = lax.all_to_all(packed, 'member', 0, 0, tiled=True)  6.75 us
    pallas_call x1, Pallas kernels, body(): pl.pallas_call(transform_kernel, in_specs=[VM, VM, VM], out_specs=VM, out...  6.35 us
    ppermute x1, starting transfers between devices, body(): up = lax.ppermute(sampled, 'tile', [(i, i + 1) for i in range(ends)])  4.65 us
    pallas_call x1, Pallas kernels, body(): pl.pallas_call(solve_kernel, in_specs=[VM, VM, VM, VM], out_specs=VM, out...  3.94 us
    ppermute x1, starting transfers between devices, body(): down = lax.ppermute(sampled, 'tile', [(i + 1, i) for i in range(ends)])  3.94 us
    all_to_all x1, waiting for transfers between devices, body(): packed = lax.all_to_all(packed, 'member', 0, 0, tiled=True)  3.93 us
    all_to_all x1, starting transfers between devices, body(): lax.all_to_all(fields.reshape(MEMBERS, UPPER, 8, LANES), 'member', 0, 0,...  3.61 us
  transfers between devices with their start and end apart: 4, of which 3 were waited for; matrix products, arithmetic and copies ran while one was open for 0% of the time, Pallas kernels for 7%

profile of v4, /device:TPU:97, one launch (start us, length us, event | category | flops | bytes accessed | tf_op | source)
XLA Modules:
  0.0 64.8 jit_solution(15170186946426957388)
XLA Ops:
  0.7 2.4 %pack.1 = (bf16[16,64,128]{2,1,0:T(8,128)(2,1)}, f32[16,128]{1,0:T(8,128)}) custom-call(s32[1]{0:T(128)} %bitcast.where, s32[1]{0:T(128)} %bitcast.7.tally, bf16[3,16,8,2048]{3,2,1,0:T(8,128)(2,1)} %x_ref.3, f32[1,256]{1,0:T(1,128)} %bitcast.10, f32[1,256]{1,0:T(1,128)} %bitcast.11, s32[1,256]{1,0:T(1,128)} %bitcast.12, ...), custom_call_target="tpu_custom_call" | custom-call | tf_op jit(solution)/shard_map/pack/pallas_call | solution.py:387
  3.0 6.8 %all-to-all-start = ((bf16[16,64,128]{2,1,0:T(8,128)(2,1)}), bf16[16,64,128]{2,1,0:T(8,128)(2,1)S(1)}, u32[]{:S(2)}, u32[]{:S(2)}) async-start(bf16[16,64,128]{2,1,0:T(8,128)(2,1)} %get-tuple-element.9), calls=%async_computation | async-start | bytes 524288 | tf_op jit(solution)/shard_map/all_to_all | solution.py:433
  9.8 0.0 copy-start
  9.8 0.0 copy-start.3
  9.8 3.5 %send.1 = (bf16[16,3,8,8,128]{4,3,2,1,0:T(8,128)(2,1)}, bf16[3,16,8,2048]{3,2,1,0:T(8,128)(2,1)}) custom-call(bf16[3,16,8,2048]{3,2,1,0:T(8,128)(2,1)} %x_ref.3), custom_call_target="tpu_custom_call" | custom-call | tf_op jit(solution)/shard_map/send/pallas_call | solution.py:418
  13.3 0.0 copy-start.2
  13.3 3.9 %all-to-all-done.r_ref = bf16[16,64,128]{2,1,0:T(8,128)(2,1)S(1)} async-done(((bf16[16,64,128]{2,1,0:T(8,128)(2,1)}), bf16[16,64,128]{2,1,0:T(8,128)(2,1)S(1)}, u32[]{:S(2)}, u32[]{:S(2)}) %all-to-all-start) | async-done | bytes 262176 | tf_op jit(solution)/shard_map/all_to_all | solution.py:433
  17.3 3.6 %all-to-all-start.1 = ((bf16[48,8,8,128]{3,2,1,0:T(8,128)(2,1)}), bf16[48,8,8,128]{3,2,1,0:T(8,128)(2,1)S(1)}, u32[]{:S(2)}, u32[]{:S(2)}) async-start(bf16[48,8,8,128]{3,2,1,0:T(8,128)(2,1)} %bitcast.9), calls=%async_computation.1 | async-start | bytes 1572864 | tf_op jit(solution)/shard_map/all_to_all | solution.py:434
  20.9 0.0 copy-start.1
  20.9 0.0 copy-done
  20.9 0.0 copy-done.3
  20.9 0.4 sample.1.own
  21.4 3.9 %collective-permute-start.1 = (f32[9,56,128]{2,1,0:T(8,128)S(1)}, f32[9,56,128]{2,1,0:T(8,128)S(1)}, u32[]{:S(2)}, u32[]{:S(2)}) collective-permute-start(f32[9,56,128]{2,1,0:T(8,128)S(1)} %sample.1.own), channel_id=1, source_target_pairs={{1,0},{2,1},{3,2},{4,3},{5,4},{6,5},{7,6},{8,7},{9,8},{10,9},{11,1... | collective-permute-start | bytes 774152 | tf_op jit(solution)/shard_map/ppermute | solution.py:447
  25.3 4.7 %collective-permute-start = (f32[9,56,128]{2,1,0:T(8,128)S(1)}, f32[9,56,128]{2,1,0:T(8,128)S(1)}, u32[]{:S(2)}, u32[]{:S(2)}) collective-permute-start(f32[9,56,128]{2,1,0:T(8,128)S(1)} %sample.1.own), channel_id=1, source_target_pairs={{0,1},{1,2},{2,3},{3,4},{4,5},{5,6},{6,7},{7,8},{8,9},{9,10},{10,1... | collective-permute-start | bytes 774152 | tf_op jit(solution)/shard_map/ppermute | solution.py:446
  30.0 2.4 %collective-permute-done.1.down = f32[9,56,128]{2,1,0:T(8,128)S(1)} collective-permute-done((f32[9,56,128]{2,1,0:T(8,128)S(1)}, f32[9,56,128]{2,1,0:T(8,128)S(1)}, u32[]{:S(2)}, u32[]{:S(2)}) %collective-permute-start.1) | collective-permute-done | bytes 258080 | tf_op jit(solution)/shard_map/ppermute | solution.py:447
  32.3 0.9 %collective-permute-done.up = f32[9,56,128]{2,1,0:T(8,128)S(1)} collective-permute-done((f32[9,56,128]{2,1,0:T(8,128)S(1)}, f32[9,56,128]{2,1,0:T(8,128)S(1)}, u32[]{:S(2)}, u32[]{:S(2)}) %collective-permute-start) | collective-permute-done | bytes 258080 | tf_op jit(solution)/shard_map/ppermute | solution.py:446
  33.2 0.0 copy-done.2
  33.2 3.9 %solve.1.w_ref = f32[24,48,128]{2,1,0:T(8,128)S(1)} custom-call(f32[9,56,128]{2,1,0:T(8,128)S(1)} %collective-permute-done.up, f32[9,56,128]{2,1,0:T(8,128)S(1)} %sample.1.own, f32[9,56,128]{2,1,0:T(8,128)S(1)} %collective-permute-done.1.down, f32[24,128]{1,0:T(8,128)S(1)} %copy-done.2), custom_call_target="tpu_custom_call" | custom-call | tf_op jit(solution)/shard_map/solve/pallas_call | solution.py:448
  37.2 0.0 all-to-all-done.1.x_ref
  37.2 0.0 copy-done.1
  37.2 6.3 %transform.1 = bf16[48,8,8,128]{3,2,1,0:T(8,128)(2,1)S(1)} custom-call(f32[24,48,128]{2,1,0:T(8,128)S(1)} %solve.1.w_ref, bf16[48,8,8,128]{3,2,1,0:T(8,128)(2,1)S(1)} %all-to-all-done.1.x_ref, bf16[256,512]{1,0:T(8,128)(2,1)S(1)} %copy-done.1), custom_call_target="tpu_custom_call" | custom-call | tf_op jit(solution)/shard_map/transform/pallas_call | solution.py:462
  43.6 20.3 %all_to_all.15 = bf16[48,8,8,128]{3,2,1,0:T(8,128)(2,1)S(1)} all-to-all(bf16[48,8,8,128]{3,2,1,0:T(8,128)(2,1)S(1)} %transform.1), channel_id=1, replica_groups=mesh['member'=16,'tile'=16] {'member'}, dimensions={0} | all-to-all | bytes 1572864 | tf_op jit(solution)/shard_map/all_to_all | solution.py:474
  63.9 0.9 %finish.1 = bf16[3,16,8,2048]{3,2,1,0:T(8,128)(2,1)} custom-call(bf16[16,3,8,8,128]{4,3,2,1,0:T(8,128)(2,1)S(1)} %bitcast.8, bf16[3,16,8,2048]{3,2,1,0:T(8,128)(2,1)} %get-tuple-element.12.partial), custom_call_target="tpu_custom_call", output_to_operand_aliasing={{}: (1, {})} | custom-call | tf_op jit(solution)/shard_map/finish/pallas_call | solution.py:475
Async XLA Ops:
  3.0 14.2 %all-to-all-start = ((bf16[16,64,128]{2,1,0:T(8,128)(2,1)}), bf16[16,64,128]{2,1,0:T(8,128)(2,1)S(1)}, u32[]{:S(2)}, u32[]{:S(2)}) async-start(bf16[16,64,128]{2,1,0:T(8,128)(2,1)} %get-tuple-element.9), calls=%async_computation | async-start | bytes 524288 | tf_op jit(solution)/shard_map/all_to_all | solution.py:433
  9.8 11.1 %copy-start = (bf16[504,1024]{1,0:T(8,128)(2,1)S(1)}, bf16[504,1024]{1,0:T(8,128)(2,1)}, u32[]{:S(2)}) copy-start(bf16[504,1024]{1,0:T(8,128)(2,1)} %constant.17.clone.choose) | copy-start | bytes 3096580
  9.8 11.1 %copy-start.3 = (f32[16,128]{1,0:T(8,128)S(1)}, f32[16,128]{1,0:T(8,128)}, u32[]{:S(2)}) copy-start(f32[16,128]{1,0:T(8,128)} %get-tuple-element.10.own) | copy-start | bytes 24580
  13.3 19.9 %copy-start.2 = (f32[24,128]{1,0:T(8,128)S(1)}, f32[24,128]{1,0:T(8,128)}, u32[]{:S(2)}) copy-start(f32[24,128]{1,0:T(8,128)} %constant.18.clone.taper) | copy-start | bytes 36868
  17.3 19.9 %all-to-all-start.1 = ((bf16[48,8,8,128]{3,2,1,0:T(8,128)(2,1)}), bf16[48,8,8,128]{3,2,1,0:T(8,128)(2,1)S(1)}, u32[]{:S(2)}, u32[]{:S(2)}) async-start(bf16[48,8,8,128]{3,2,1,0:T(8,128)(2,1)} %bitcast.9), calls=%async_computation.1 | async-start | bytes 1572864 | tf_op jit(solution)/shard_map/all_to_all | solution.py:434
  20.9 16.3 %copy-start.1 = (bf16[256,512]{1,0:T(8,128)(2,1)S(1)}, bf16[256,512]{1,0:T(8,128)(2,1)}, u32[]{:S(2)}) copy-start(bf16[256,512]{1,0:T(8,128)(2,1)} %constant.19.clone.expand) | copy-start | bytes 786436
  21.4 11.0 %collective-permute-start.1 = (f32[9,56,128]{2,1,0:T(8,128)S(1)}, f32[9,56,128]{2,1,0:T(8,128)S(1)}, u32[]{:S(2)}, u32[]{:S(2)}) collective-permute-start(f32[9,56,128]{2,1,0:T(8,128)S(1)} %sample.1.own), channel_id=1, source_target_pairs={{1,0},{2,1},{3,2},{4,3},{5,4},{6,5},{7,6},{8,7},{9,8},{10,9},{11,1... | collective-permute-start | bytes 774152 | tf_op jit(solution)/shard_map/ppermute | solution.py:447
  25.3 7.9 %collective-permute-start = (f32[9,56,128]{2,1,0:T(8,128)S(1)}, f32[9,56,128]{2,1,0:T(8,128)S(1)}, u32[]{:S(2)}, u32[]{:S(2)}) collective-permute-start(f32[9,56,128]{2,1,0:T(8,128)S(1)} %sample.1.own), channel_id=1, source_target_pairs={{0,1},{1,2},{2,3},{3,4},{4,5},{5,6},{6,7},{7,8},{8,9},{9,10},{10,1... | collective-permute-start | bytes 774152 | tf_op jit(solution)/shard_map/ppermute | solution.py:446

commit v5 on v4

--- a/solution.py
+++ b/solution.py
@@ -78,6 +78,14 @@
 
 
 OFFSETS = (10, 14, 2, 6)
+MEAN_ROW = 672
+FIX_ROW = 720
+WEIGHT_ROWS = 744
+
+
+def first_row(t):
+    panel = t // 4
+    return 16 * panel * (panel + 1) + (t % 4) * 8 * (panel + 1)
 
 
 def taper_rows():
@@ -303,55 +311,82 @@
                 for j in js:
                     mat[4 * block + n, 8 * j : 8 * j + 8, :] = acc[n][j]
 
+    mean = [-x for x in drive]
+    mean_total = mean[0] + mean[1] + mean[2] + mean[3] + mean[4] + mean[5]
+    for j in range(6):
+        out[MEAN_ROW + 8 * j : MEAN_ROW + 8 * j + 8, :] = mean[j]
     for t in range(24):
         panel = t // 4
+        base = first_row(t)
         sc = jnp.where(half0, scale[2 * t], scale[2 * t + 1])
-        w = []
-        for j in range(6):
-            x = -drive[j]
-            if j <= panel:
-                x = x + sc * mat[t, 8 * j : 8 * j + 8, :]
-            w.append(x)
-        total = jnp.sum(w[0] + w[1] + w[2] + w[3] + w[4] + w[5], axis=0, keepdims=True)
-        fix = (1.0 - total) * (1.0 / MEMBERS)
-        for j in range(6):
-            out[t, 8 * j : 8 * j + 8, :] = w[j] + fix
-
-
-def transform_kernel(w_ref, x_ref, expand, out, wide, xs):
-    w = w_ref[...].reshape(24 * 48, LANES)
-    hi, low = split2(w)
+        total = mean_total
+        for j in range(panel + 1):
+            x = sc * mat[t, 8 * j : 8 * j + 8, :]
+            out[base + 8 * j : base + 8 * j + 8, :] = x
+            total = total + x
+        total = jnp.sum(total, axis=0, keepdims=True)
+        out[FIX_ROW + t : FIX_ROW + t + 1, :] = (1.0 - total) * (1.0 / MEMBERS)
+
+
+def transform_kernel(w_ref, x_ref, expand, out, wide, xs, base):
+    hi, low = split2(w_ref[...])
     wide[...] = nn(jnp.concatenate([hi, low], 1), expand[...])
-
     for i in range(MEMBERS):
         for l in range(8):
             xs[i, l] = x_ref[i, l].astype(F32)
     top = lax.broadcasted_iota(jnp.int32, (8, LANES), 0) < 4
 
-    def pair(t, c):
-        def step(i, acc):
-            acc = list(acc)
-            for u in range(16):
-                r = t * 48 + i * 16 + u
-                line = wide[pl.ds(r, 1), :]
-                ws = []
-                for h in range(2):
-                    a = jnp.broadcast_to(line[:, h * 256 : h * 256 + 128], (8, LANES))
-                    b = jnp.broadcast_to(line[:, h * 256 + 128 : h * 256 + 256], (8, LANES))
-                    ws.append(jnp.where(top, a, b))
+    def weights(r, halves):
+        line = wide[pl.ds(r, 1), :]
+        res = []
+        for h in range(halves):
+            a = jnp.broadcast_to(line[:, h * 256 : h * 256 + 128], (8, LANES))
+            b = jnp.broadcast_to(line[:, h * 256 + 128 : h * 256 + 256], (8, LANES))
+            res.append(jnp.where(top, a, b))
+        return res
+
+    def common(i, acc):
+        acc = list(acc)
+        for u in range(16):
+            w = weights(MEAN_ROW + i * 16 + u, 1)[0]
+            for l in range(8):
+                x = xs[i * 16 + u, l]
+                acc[l] = acc[l] + x * w
+                acc[8 + l] = acc[8 + l] + x
+        return tuple(acc)
+
+    zeros = tuple(jnp.zeros((8, LANES), F32) for _ in range(16))
+    acc = lax.fori_loop(0, 3, common, zeros)
+    for l in range(8):
+        base[l] = acc[l]
+        base[8 + l] = acc[8 + l]
+
+    for panel, step in enumerate((8, 16, 24, 16, 20, 24)):
+        count = 8 * (panel + 1)
+
+        def pair(n, c, panel=panel, step=step, count=count):
+            t = 4 * panel + n
+            row = first_row(4 * panel) + n * count
+            fix = weights(FIX_ROW + t, 2)
+
+            def some(i, acc):
+                acc = list(acc)
+                for u in range(step):
+                    w = weights(row + i * step + u, 2)
+                    for l in range(8):
+                        x = xs[i * step + u, l]
+                        acc[l] = acc[l] + x * w[0]
+                        acc[8 + l] = acc[8 + l] + x * w[1]
+                return tuple(acc)
+
+            acc = tuple(base[l] + base[8 + l] * fix[h] for h in range(2) for l in range(8))
+            acc = lax.fori_loop(0, count // step, some, acc)
+            for h in range(2):
                 for l in range(8):
-                    x = xs[i * 16 + u, l]
-                    acc[l] = acc[l] + x * ws[0]
-                    acc[8 + l] = acc[8 + l] + x * ws[1]
-            return tuple(acc)
-
-        acc = lax.fori_loop(0, 3, step, tuple(jnp.zeros((8, LANES), F32) for _ in range(16)))
-        for h in range(2):
-            for l in range(8):
-                out[2 * t + h, l] = acc[8 * h + l].astype(BF16)
-        return c
-
-    lax.fori_loop(0, 24, pair, 0)
+                    out[2 * t + h, l] = acc[8 * h + l].astype(BF16)
+            return c
+
+        lax.fori_loop(0, 4, pair, 0)
 
 
 def send_kernel(x_ref, out, lower):
@@ -449,7 +484,7 @@
         solve_kernel,
         in_specs=[VM, VM, VM, VM],
         out_specs=VM,
-        out_shape=jax.ShapeDtypeStruct((24, 48, LANES), F32),
+        out_shape=jax.ShapeDtypeStruct((WEIGHT_ROWS, LANES), F32),
         scratch_shapes=[
             pltpu.VMEM((BLOCKS_Y * PACK, LANES), F32),
             pltpu.VMEM((24, 48, LANES), F32),
@@ -465,8 +500,9 @@
         out_specs=VM,
         out_shape=jax.ShapeDtypeStruct((MEMBERS, UPPER, 8, LANES), BF16),
         scratch_shapes=[
-            pltpu.VMEM((24 * 48, 512), F32),
+            pltpu.VMEM((WEIGHT_ROWS, 512), F32),
             pltpu.VMEM((MEMBERS, UPPER, 8, LANES), F32),
+            pltpu.VMEM((16, 8, LANES), F32),
         ],
         compiler_params=LIMIT,
         name="transform",

time: 66 us -> 63.9 us (0.968)
  Pallas kernels: 17.6 us -> 15.5 us
    pallas_call x1, Pallas kernels: 6.35 us -> 4.32 us  [body(): pl.pallas_call(transform_kernel, in_specs=[VM, VM, VM], out_specs=VM, out...]
where the time goes in v5:
time: 63.9 us; the launch traced here: 62.8 us
  blocking collectives  20.3 us (32%)
  starting transfers between devices  19 us (30%)
  Pallas kernels  15.5 us (24%)
  waiting for transfers between devices  7.18 us (11%)
  between operations  0.76 us (1%)
    all_to_all x1, blocking collectives, body(): result = lax.all_to_all(result, 'member', 0, 0, tiled=True)  20.3 us
    all_to_all x1, starting transfers between devices, body(): packed = lax.all_to_all(packed, 'member', 0, 0, tiled=True)  6.75 us
    ppermute x1, starting transfers between devices, body(): up = lax.ppermute(sampled, 'tile', [(i, i + 1) for i in range(ends)])  4.65 us
    pallas_call x1, Pallas kernels, body(): pl.pallas_call(transform_kernel, in_specs=[VM, VM, VM], out_specs=VM, out...  4.32 us
    ppermute x1, starting transfers between devices, body(): down = lax.ppermute(sampled, 'tile', [(i + 1, i) for i in range(ends)])  3.94 us
    all_to_all x1, waiting for transfers between devices, body(): packed = lax.all_to_all(packed, 'member', 0, 0, tiled=True)  3.93 us
    pallas_call x1, Pallas kernels, body(): pl.pallas_call(solve_kernel, in_specs=[VM, VM, VM, VM], out_specs=VM, out...  3.89 us
    all_to_all x1, starting transfers between devices, body(): lax.all_to_all(fields.reshape(MEMBERS, UPPER, 8, LANES), 'member', 0, 0,...  3.61 us
  transfers between devices with their start and end apart: 4, of which 3 were waited for; matrix products, arithmetic and copies ran while one was open for 0% of the time, Pallas kernels for 7%

profile of v5, /device:TPU:97, one launch (start us, length us, event | category | flops | bytes accessed | tf_op | source)
XLA Modules:
  0.0 62.8 jit_solution(8371879124154222637)
XLA Ops:
  0.7 2.4 %pack.1 = (bf16[16,64,128]{2,1,0:T(8,128)(2,1)}, f32[16,128]{1,0:T(8,128)}) custom-call(s32[1]{0:T(128)} %bitcast.where, s32[1]{0:T(128)} %bitcast.7.tally, bf16[3,16,8,2048]{3,2,1,0:T(8,128)(2,1)} %x_ref.3, f32[1,256]{1,0:T(1,128)} %bitcast.10, f32[1,256]{1,0:T(1,128)} %bitcast.11, s32[1,256]{1,0:T(1,128)} %bitcast.12, ...), custom_call_target="tpu_custom_call" | custom-call | tf_op jit(solution)/shard_map/pack/pallas_call | solution.py:422
  3.0 6.8 %all-to-all-start = ((bf16[16,64,128]{2,1,0:T(8,128)(2,1)}), bf16[16,64,128]{2,1,0:T(8,128)(2,1)S(1)}, u32[]{:S(2)}, u32[]{:S(2)}) async-start(bf16[16,64,128]{2,1,0:T(8,128)(2,1)} %get-tuple-element.9), calls=%async_computation | async-start | bytes 524288 | tf_op jit(solution)/shard_map/all_to_all | solution.py:468
  9.8 0.0 copy-start
  9.8 0.0 copy-start.3
  9.8 3.5 %send.1 = (bf16[16,3,8,8,128]{4,3,2,1,0:T(8,128)(2,1)}, bf16[3,16,8,2048]{3,2,1,0:T(8,128)(2,1)}) custom-call(bf16[3,16,8,2048]{3,2,1,0:T(8,128)(2,1)} %x_ref.3), custom_call_target="tpu_custom_call" | custom-call | tf_op jit(solution)/shard_map/send/pallas_call | solution.py:453
  13.3 0.0 copy-start.2
  13.3 3.9 %all-to-all-done.r_ref = bf16[16,64,128]{2,1,0:T(8,128)(2,1)S(1)} async-done(((bf16[16,64,128]{2,1,0:T(8,128)(2,1)}), bf16[16,64,128]{2,1,0:T(8,128)(2,1)S(1)}, u32[]{:S(2)}, u32[]{:S(2)}) %all-to-all-start) | async-done | bytes 262176 | tf_op jit(solution)/shard_map/all_to_all | solution.py:468
  17.3 3.6 %all-to-all-start.1 = ((bf16[48,8,8,128]{3,2,1,0:T(8,128)(2,1)}), bf16[48,8,8,128]{3,2,1,0:T(8,128)(2,1)S(1)}, u32[]{:S(2)}, u32[]{:S(2)}) async-start(bf16[48,8,8,128]{3,2,1,0:T(8,128)(2,1)} %bitcast.9), calls=%async_computation.1 | async-start | bytes 1572864 | tf_op jit(solution)/shard_map/all_to_all | solution.py:469
  20.9 0.0 copy-start.1
  20.9 0.0 copy-done
  20.9 0.0 copy-done.3
  20.9 0.4 sample.1.own
  21.4 3.9 %collective-permute-start.1 = (f32[9,56,128]{2,1,0:T(8,128)S(1)}, f32[9,56,128]{2,1,0:T(8,128)S(1)}, u32[]{:S(2)}, u32[]{:S(2)}) collective-permute-start(f32[9,56,128]{2,1,0:T(8,128)S(1)} %sample.1.own), channel_id=1, source_target_pairs={{1,0},{2,1},{3,2},{4,3},{5,4},{6,5},{7,6},{8,7},{9,8},{10,9},{11,1... | collective-permute-start | bytes 774152 | tf_op jit(solution)/shard_map/ppermute | solution.py:482
  25.3 4.7 %collective-permute-start = (f32[9,56,128]{2,1,0:T(8,128)S(1)}, f32[9,56,128]{2,1,0:T(8,128)S(1)}, u32[]{:S(2)}, u32[]{:S(2)}) collective-permute-start(f32[9,56,128]{2,1,0:T(8,128)S(1)} %sample.1.own), channel_id=1, source_target_pairs={{0,1},{1,2},{2,3},{3,4},{4,5},{5,6},{6,7},{7,8},{8,9},{9,10},{10,1... | collective-permute-start | bytes 774152 | tf_op jit(solution)/shard_map/ppermute | solution.py:481
  30.0 2.4 %collective-permute-done.1.down = f32[9,56,128]{2,1,0:T(8,128)S(1)} collective-permute-done((f32[9,56,128]{2,1,0:T(8,128)S(1)}, f32[9,56,128]{2,1,0:T(8,128)S(1)}, u32[]{:S(2)}, u32[]{:S(2)}) %collective-permute-start.1) | collective-permute-done | bytes 258080 | tf_op jit(solution)/shard_map/ppermute | solution.py:482
  32.3 0.9 %collective-permute-done.up = f32[9,56,128]{2,1,0:T(8,128)S(1)} collective-permute-done((f32[9,56,128]{2,1,0:T(8,128)S(1)}, f32[9,56,128]{2,1,0:T(8,128)S(1)}, u32[]{:S(2)}, u32[]{:S(2)}) %collective-permute-start) | collective-permute-done | bytes 258080 | tf_op jit(solution)/shard_map/ppermute | solution.py:481
  33.2 0.0 copy-done.2
  33.2 3.9 %solve.1.w_ref = f32[744,128]{1,0:T(8,128)S(1)} custom-call(f32[9,56,128]{2,1,0:T(8,128)S(1)} %collective-permute-done.up, f32[9,56,128]{2,1,0:T(8,128)S(1)} %sample.1.own, f32[9,56,128]{2,1,0:T(8,128)S(1)} %collective-permute-done.1.down, f32[24,128]{1,0:T(8,128)S(1)} %copy-done.2), custom_call_target="tpu_custom_call" | custom-call | tf_op jit(solution)/shard_map/solve/pallas_call | solution.py:483
  37.1 0.0 all-to-all-done.1.x_ref
  37.1 0.0 copy-done.1
  37.1 4.3 %transform.1 = bf16[48,8,8,128]{3,2,1,0:T(8,128)(2,1)S(1)} custom-call(f32[744,128]{1,0:T(8,128)S(1)} %solve.1.w_ref, bf16[48,8,8,128]{3,2,1,0:T(8,128)(2,1)S(1)} %all-to-all-done.1.x_ref, bf16[256,512]{1,0:T(8,128)(2,1)S(1)} %copy-done.1), custom_call_target="tpu_custom_call" | custom-call | tf_op jit(solution)/shard_map/transform/pallas_call | solution.py:497
  41.5 20.3 %all_to_all.15 = bf16[48,8,8,128]{3,2,1,0:T(8,128)(2,1)S(1)} all-to-all(bf16[48,8,8,128]{3,2,1,0:T(8,128)(2,1)S(1)} %transform.1), channel_id=1, replica_groups=mesh['member'=16,'tile'=16] {'member'}, dimensions={0} | all-to-all | bytes 1572864 | tf_op jit(solution)/shard_map/all_to_all | solution.py:510
  61.8 0.9 %finish.1 = bf16[3,16,8,2048]{3,2,1,0:T(8,128)(2,1)} custom-call(bf16[16,3,8,8,128]{4,3,2,1,0:T(8,128)(2,1)S(1)} %bitcast.8, bf16[3,16,8,2048]{3,2,1,0:T(8,128)(2,1)} %get-tuple-element.12.partial), custom_call_target="tpu_custom_call", output_to_operand_aliasing={{}: (1, {})} | custom-call | tf_op jit(solution)/shard_map/finish/pallas_call | solution.py:511
Async XLA Ops:
  3.0 14.2 %all-to-all-start = ((bf16[16,64,128]{2,1,0:T(8,128)(2,1)}), bf16[16,64,128]{2,1,0:T(8,128)(2,1)S(1)}, u32[]{:S(2)}, u32[]{:S(2)}) async-start(bf16[16,64,128]{2,1,0:T(8,128)(2,1)} %get-tuple-element.9), calls=%async_computation | async-start | bytes 524288 | tf_op jit(solution)/shard_map/all_to_all | solution.py:468
  9.8 11.1 %copy-start = (bf16[504,1024]{1,0:T(8,128)(2,1)S(1)}, bf16[504,1024]{1,0:T(8,128)(2,1)}, u32[]{:S(2)}) copy-start(bf16[504,1024]{1,0:T(8,128)(2,1)} %constant.17.clone.choose) | copy-start | bytes 3096580
  9.8 11.1 %copy-start.3 = (f32[16,128]{1,0:T(8,128)S(1)}, f32[16,128]{1,0:T(8,128)}, u32[]{:S(2)}) copy-start(f32[16,128]{1,0:T(8,128)} %get-tuple-element.10.own) | copy-start | bytes 24580
  13.3 19.9 %copy-start.2 = (f32[24,128]{1,0:T(8,128)S(1)}, f32[24,128]{1,0:T(8,128)}, u32[]{:S(2)}) copy-start(f32[24,128]{1,0:T(8,128)} %constant.18.clone.taper) | copy-start | bytes 36868
  17.3 19.9 %all-to-all-start.1 = ((bf16[48,8,8,128]{3,2,1,0:T(8,128)(2,1)}), bf16[48,8,8,128]{3,2,1,0:T(8,128)(2,1)S(1)}, u32[]{:S(2)}, u32[]{:S(2)}) async-start(bf16[48,8,8,128]{3,2,1,0:T(8,128)(2,1)} %bitcast.9), calls=%async_computation.1 | async-start | bytes 1572864 | tf_op jit(solution)/shard_map/all_to_all | solution.py:469
  20.9 16.3 %copy-start.1 = (bf16[256,512]{1,0:T(8,128)(2,1)S(1)}, bf16[256,512]{1,0:T(8,128)(2,1)}, u32[]{:S(2)}) copy-start(bf16[256,512]{1,0:T(8,128)(2,1)} %constant.19.clone.expand) | copy-start | bytes 786436
  21.4 11.0 %collective-permute-start.1 = (f32[9,56,128]{2,1,0:T(8,128)S(1)}, f32[9,56,128]{2,1,0:T(8,128)S(1)}, u32[]{:S(2)}, u32[]{:S(2)}) collective-permute-start(f32[9,56,128]{2,1,0:T(8,128)S(1)} %sample.1.own), channel_id=1, source_target_pairs={{1,0},{2,1},{3,2},{4,3},{5,4},{6,5},{7,6},{8,7},{9,8},{10,9},{11,1... | collective-permute-start | bytes 774152 | tf_op jit(solution)/shard_map/ppermute | solution.py:482
  25.3 7.9 %collective-permute-start = (f32[9,56,128]{2,1,0:T(8,128)S(1)}, f32[9,56,128]{2,1,0:T(8,128)S(1)}, u32[]{:S(2)}, u32[]{:S(2)}) collective-permute-start(f32[9,56,128]{2,1,0:T(8,128)S(1)} %sample.1.own), channel_id=1, source_target_pairs={{0,1},{1,2},{2,3},{3,4},{4,5},{5,6},{6,7},{7,8},{8,9},{9,10},{10,1... | collective-permute-start | bytes 774152 | tf_op jit(solution)/shard_map/ppermute | solution.py:481

commit v6 on v5

--- a/solution.py
+++ b/solution.py
@@ -100,6 +100,18 @@
                 s = gap_x * gap_x + gap_y * gap_y
                 t[(k * 3 + seg) * 2 + p] = np.where(s < RADIUS * RADIUS, (1 - s / 64.0) ** 2, 0.0)
     return t
+
+
+def taper_table():
+    base = taper_rows().reshape(4, 3, 2, LANES)
+    table = np.zeros((4, 4, 3, 2, LANES), np.float32)
+    for odd in range(2):
+        for edge in range(2):
+            t = table[2 * odd + edge]
+            t[:, 0] = base[:, 0 if odd else 2]
+            t[:, 1] = base[:, 1]
+            t[:, 2] = 0.0 if edge else base[:, 2 if odd else 0]
+    return table.reshape(96, LANES)
 
 
 def expand_rows():
@@ -185,8 +197,7 @@
         )
 
 
-def solve_kernel(up, own, down, taper, out, grams, mat, piv, fac):
-    segs = (up, own, down)
+def gram_products(segs, taper):
     lane = lax.broadcasted_iota(jnp.int32, (1, LANES), 1) % CHUNK
     first = lax.broadcasted_iota(jnp.int32, (16, LANES), 0) == 0
     for g in range(GROUPS):
@@ -196,8 +207,8 @@
             v0, v1 = (8 if v in (-1, 8) else v for v in (v0, v1))
             mask = lane >= o
             shi, slo, whi, wlo = [], [], [], []
-            for s in range(3):
-                w = jnp.where(mask, segs[s][v0], segs[s][v1])
+            for s, ref in segs:
+                w = jnp.where(mask, ref[v0], ref[v1])
                 a = w[0:48]
                 prec, drv = w[48:49], w[49:50]
                 row = (k * 3 + s) * 2
@@ -206,7 +217,7 @@
                 shi.append(h)
                 slo.append(l)
                 h, l = split2(
-                    jnp.concatenate([a * taper[row : row + 1, :], a * taper[row + 1 : row + 2, :]], 0)
+                    jnp.concatenate([a * taper[row : row + 1], a * taper[row + 1 : row + 2]], 0)
                 )
                 whi.append(h)
                 wlo.append(l)
@@ -216,8 +227,24 @@
             res = nt(stream, jnp.concatenate(whi + wlo, 1))
             res = res[0:56] + res[64:120]
             res = jnp.concatenate([res, jnp.zeros((56, LANES - 2 * MEMBERS), F32)], 1)
-            q = g * 4 + k
-            grams[q * PACK : (q + 1) * PACK, :] = res
+            yield g * 4 + k, res
+
+
+def pick_taper(tile, taper):
+    place = tile[0]
+    edge = jnp.logical_or(place == 0, place == 15).astype(jnp.int32)
+    variant = 2 * (place % 2) + edge
+    return taper[pl.ds(pl.multiple_of(variant * 24, 8), 24), :]
+
+
+def near_kernel(tile, own, pair, taper, out):
+    for q, res in gram_products([(0, pair), (1, own)], pick_taper(tile, taper)):
+        out[q * PACK : (q + 1) * PACK, :] = res
+
+
+def solve_kernel(tile, following, partial, taper, out, grams, mat, piv, fac):
+    for q, res in gram_products([(2, following)], pick_taper(tile, taper)):
+        grams[q * PACK : (q + 1) * PACK, :] = partial[q * PACK : (q + 1) * PACK, :] + res
 
     sub = lax.broadcasted_iota(jnp.int32, (8, LANES), 0)
     half = (lax.broadcasted_iota(jnp.int32, (8, LANES), 1) // 32) % 2
@@ -417,6 +444,7 @@
 
 def body(prior, reading, error, cell, tally):
     me = lax.axis_index("member").astype(jnp.int32).reshape(1)
+    tile = lax.axis_index("tile").astype(jnp.int32).reshape(1)
     const = lambda a, t: jnp.asarray(a, t)
     whole = lambda *shape: pl.BlockSpec(shape, lambda g: (0,) * len(shape))
     packed, own = pl.pallas_call(
@@ -477,12 +505,24 @@
         compiler_params=LIMIT,
         name="sample",
     )(packed, own, const(row_sample(), BF16))
-    ends = lax.axis_size("tile") - 1
-    up = lax.ppermute(sampled, "tile", [(i, i + 1) for i in range(ends)])
-    down = lax.ppermute(sampled, "tile", [(i + 1, i) for i in range(ends)])
+    tiles = lax.axis_size("tile")
+    pair = lax.ppermute(sampled, "tile", [(i, i ^ 1) for i in range(tiles)])
+    following = lax.ppermute(
+        sampled, "tile", [(i, (i + 1 if i % 2 else i - 1) % tiles) for i in range(tiles)]
+    )
+    table = const(taper_table(), F32)
+    partial_gram = pl.pallas_call(
+        near_kernel,
+        in_specs=[SM, VM, VM, VM],
+        out_specs=VM,
+        out_shape=jax.ShapeDtypeStruct((BLOCKS_Y * PACK, LANES), F32),
+        compiler_params=LIMIT,
+        cost_estimate=pl.CostEstimate(flops=10**9, bytes_accessed=3 * 10**6, transcendentals=0),
+        name="near_gram",
+    )(tile, sampled, pair, table)
     weights = pl.pallas_call(
         solve_kernel,
-        in_specs=[VM, VM, VM, VM],
+        in_specs=[SM, VM, VM, VM],
         out_specs=VM,
         out_shape=jax.ShapeDtypeStruct((WEIGHT_ROWS, LANES), F32),
         scratch_shapes=[
@@ -493,7 +533,7 @@
         ],
         compiler_params=LIMIT,
         name="solve",
-    )(up, sampled, down, const(taper_rows(), F32))
+    )(tile, following, partial_gram, table)
     result = pl.pallas_call(
         transform_kernel,
         in_specs=[VM, VM, VM],

time: 63.9 us -> 59.8 us (0.936); the launches traced: 62.8 us -> 59.4 us
  starting transfers between devices: 19 us -> 15.3 us
    ppermute x2, starting transfers between devices: 8.6 us -> 4.95 us  [the longest x1 2.84 us: body(): lax.ppermute(sampled, 'tile', [(i, (i + 1 if i % 2 else i - 1) % tiles) f...]
    pallas_call x1 -> x2, Pallas kernels: 3.89 us -> 4.05 us  [the longest x1 2.77 us: body(): pl.pallas_call(solve_kernel, in_specs=[SM, VM, VM, VM], out_specs=VM, out...]
  transfers between devices with their start and end apart: 4 -> 4, of which waited for: 3 -> 2; matrix products, arithmetic and copies ran while one was open for 0% -> 0% of each run, Pallas kernels for 7% -> 8%
where the time goes in v6:
time: 59.8 us; the launch traced here: 59.4 us
  blocking collectives  20.7 us (35%)
  Pallas kernels  15.6 us (26%)
  starting transfers between devices  15.3 us (26%)
  waiting for transfers between devices  7.05 us (12%)
  between operations  0.76 us (1%)
    all_to_all x1, blocking collectives, body(): result = lax.all_to_all(result, 'member', 0, 0, tiled=True)  20.7 us
    all_to_all x1, starting transfers between devices, body(): packed = lax.all_to_all(packed, 'member', 0, 0, tiled=True)  6.75 us
    pallas_call x1, Pallas kernels, body(): pl.pallas_call(transform_kernel, in_specs=[VM, VM, VM], out_specs=VM, out...  4.23 us
    all_to_all x1, waiting for transfers between devices, body(): packed = lax.all_to_all(packed, 'member', 0, 0, tiled=True)  3.93 us
    all_to_all x1, starting transfers between devices, body(): lax.all_to_all(fields.reshape(MEMBERS, UPPER, 8, LANES), 'member', 0, 0,...  3.61 us
    pallas_call x1, Pallas kernels, body(): pl.pallas_call(send_kernel, grid=(3,), in_specs=[pl.BlockSpec((1, 2 * UPP...  3.5 us
    ppermute x1, waiting for transfers between devices, body(): lax.ppermute(sampled, 'tile', [(i, (i + 1 if i % 2 else i - 1) % tiles) f...  3.12 us
    ppermute x1, starting transfers between devices, body(): lax.ppermute(sampled, 'tile', [(i, (i + 1 if i % 2 else i - 1) % tiles) f...  2.84 us
  transfers between devices with their start and end apart: 4, of which 2 were waited for; matrix products, arithmetic and copies ran while one was open for 0% of the time, Pallas kernels for 8%

profile of v6, /device:TPU:97, one launch (start us, length us, event | category | flops | bytes accessed | tf_op | source)
XLA Modules:
  0.0 59.4 jit_solution(1581004917306420523)
XLA Ops:
  0.7 2.4 %pack.1 = (bf16[16,64,128]{2,1,0:T(8,128)(2,1)}, f32[16,128]{1,0:T(8,128)}) custom-call(s32[1]{0:T(128)} %bitcast.1.where, s32[1]{0:T(128)} %bitcast.8.tally, bf16[3,16,8,2048]{3,2,1,0:T(8,128)(2,1)} %x_ref.3, f32[1,256]{1,0:T(1,128)} %bitcast.11, f32[1,256]{1,0:T(1,128)} %bitcast.12, s32[1,256]{1,0:T(1,128)} %bitcast.13, ...), custom_call_target="tpu_custom_call" | custom-call | tf_op jit(solution)/shard_map/pack/pallas_call | solution.py:450
  3.0 6.8 %all-to-all-start = ((bf16[16,64,128]{2,1,0:T(8,128)(2,1)}), bf16[16,64,128]{2,1,0:T(8,128)(2,1)S(1)}, u32[]{:S(2)}, u32[]{:S(2)}) async-start(bf16[16,64,128]{2,1,0:T(8,128)(2,1)} %get-tuple-element.9), calls=%async_computation | async-start | bytes 524288 | tf_op jit(solution)/shard_map/all_to_all | solution.py:496
  9.8 0.0 copy-start
  9.8 0.0 copy-start.3
  9.8 3.5 %send.1 = (bf16[16,3,8,8,128]{4,3,2,1,0:T(8,128)(2,1)}, bf16[3,16,8,2048]{3,2,1,0:T(8,128)(2,1)}) custom-call(bf16[3,16,8,2048]{3,2,1,0:T(8,128)(2,1)} %x_ref.3), custom_call_target="tpu_custom_call" | custom-call | tf_op jit(solution)/shard_map/send/pallas_call | solution.py:481
  13.3 0.0 copy-start.2
  13.3 3.9 %all-to-all-done.r_ref = bf16[16,64,128]{2,1,0:T(8,128)(2,1)S(1)} async-done(((bf16[16,64,128]{2,1,0:T(8,128)(2,1)}), bf16[16,64,128]{2,1,0:T(8,128)(2,1)S(1)}, u32[]{:S(2)}, u32[]{:S(2)}) %all-to-all-start) | async-done | bytes 262176 | tf_op jit(solution)/shard_map/all_to_all | solution.py:496
  17.3 3.6 %all-to-all-start.1 = ((bf16[48,8,8,128]{3,2,1,0:T(8,128)(2,1)}), bf16[48,8,8,128]{3,2,1,0:T(8,128)(2,1)S(1)}, u32[]{:S(2)}, u32[]{:S(2)}) async-start(bf16[48,8,8,128]{3,2,1,0:T(8,128)(2,1)} %bitcast.10), calls=%async_computation.1 | async-start | bytes 1572864 | tf_op jit(solution)/shard_map/all_to_all | solution.py:497
  20.9 0.0 copy-done
  20.9 0.0 copy-done.3
  20.9 0.4 sample.1.own
  21.3 2.1 %collective-permute-start.1 = (f32[9,56,128]{2,1,0:T(8,128)S(1)}, f32[9,56,128]{2,1,0:T(8,128)S(1)}, u32[]{:S(2)}, u32[]{:S(2)}) collective-permute-start(f32[9,56,128]{2,1,0:T(8,128)S(1)} %sample.1.own), channel_id=1, source_target_pairs={{0,1},{1,0},{2,3},{3,2},{4,5},{5,4},{6,7},{7,6},{8,9},{9,8},{10,11... | collective-permute-start | bytes 774152 | tf_op jit(solution)/shard_map/ppermute | solution.py:509
  23.5 2.8 %collective-permute-start = (f32[9,56,128]{2,1,0:T(8,128)S(1)}, f32[9,56,128]{2,1,0:T(8,128)S(1)}, u32[]{:S(2)}, u32[]{:S(2)}) collective-permute-start(f32[9,56,128]{2,1,0:T(8,128)S(1)} %sample.1.own), channel_id=1, source_target_pairs={{0,15},{1,2},{2,1},{3,4},{4,3},{5,6},{6,5},{7,8},{8,7},{9,10},{10,... | collective-permute-start | bytes 774152 | tf_op jit(solution)/shard_map/ppermute | solution.py:510
  26.3 0.0 collective-permute-done.1.pair
  26.3 0.0 copy-done.2
  26.3 1.3 %near_gram.1.partial = f32[1792,128]{1,0:T(8,128)S(1)} custom-call(s32[1]{0:T(128)} %bitcast.tile, f32[9,56,128]{2,1,0:T(8,128)S(1)} %sample.1.own, f32[9,56,128]{2,1,0:T(8,128)S(1)} %collective-permute-done.1.pair, f32[96,128]{1,0:T(8,128)S(1)} %copy-done.2), custom_call_target="tpu_custom_call" | custom-call | flops 1000000000 | bytes 3000000 | tf_op jit(solution)/shard_map/near_gram/pallas_call | solution.py:514
  27.6 0.0 copy-start.1
  27.6 3.1 %collective-permute-done.following = f32[9,56,128]{2,1,0:T(8,128)S(1)} collective-permute-done((f32[9,56,128]{2,1,0:T(8,128)S(1)}, f32[9,56,128]{2,1,0:T(8,128)S(1)}, u32[]{:S(2)}, u32[]{:S(2)}) %collective-permute-start) | collective-permute-done | bytes 258080 | tf_op jit(solution)/shard_map/ppermute | solution.py:510
  30.7 2.8 %solve.1.w_ref = f32[744,128]{1,0:T(8,128)S(1)} custom-call(s32[1]{0:T(128)} %bitcast.tile, f32[9,56,128]{2,1,0:T(8,128)S(1)} %collective-permute-done.following, f32[1792,128]{1,0:T(8,128)S(1)} %near_gram.1.partial, f32[96,128]{1,0:T(8,128)S(1)} %copy-done.2), custom_call_target="tpu_custom_call" | custom-call | tf_op jit(solution)/shard_map/solve/pallas_call | solution.py:523
  33.5 0.0 all-to-all-done.1.x_ref
  33.5 0.0 copy-done.1
  33.5 4.2 %transform.1 = bf16[48,8,8,128]{3,2,1,0:T(8,128)(2,1)S(1)} custom-call(f32[744,128]{1,0:T(8,128)S(1)} %solve.1.w_ref, bf16[48,8,8,128]{3,2,1,0:T(8,128)(2,1)S(1)} %all-to-all-done.1.x_ref, bf16[256,512]{1,0:T(8,128)(2,1)S(1)} %copy-done.1), custom_call_target="tpu_custom_call" | custom-call | tf_op jit(solution)/shard_map/transform/pallas_call | solution.py:537
  37.8 20.7 %all_to_all.15 = bf16[48,8,8,128]{3,2,1,0:T(8,128)(2,1)S(1)} all-to-all(bf16[48,8,8,128]{3,2,1,0:T(8,128)(2,1)S(1)} %transform.1), channel_id=1, replica_groups=mesh['member'=16,'tile'=16] {'member'}, dimensions={0} | all-to-all | bytes 1572864 | tf_op jit(solution)/shard_map/all_to_all | solution.py:550
  58.5 0.9 %finish.1 = bf16[3,16,8,2048]{3,2,1,0:T(8,128)(2,1)} custom-call(bf16[16,3,8,8,128]{4,3,2,1,0:T(8,128)(2,1)S(1)} %bitcast.9, bf16[3,16,8,2048]{3,2,1,0:T(8,128)(2,1)} %get-tuple-element.12.partial), custom_call_target="tpu_custom_call", output_to_operand_aliasing={{}: (1, {})} | custom-call | tf_op jit(solution)/shard_map/finish/pallas_call | solution.py:551
Async XLA Ops:
  3.0 14.2 %all-to-all-start = ((bf16[16,64,128]{2,1,0:T(8,128)(2,1)}), bf16[16,64,128]{2,1,0:T(8,128)(2,1)S(1)}, u32[]{:S(2)}, u32[]{:S(2)}) async-start(bf16[16,64,128]{2,1,0:T(8,128)(2,1)} %get-tuple-element.9), calls=%async_computation | async-start | bytes 524288 | tf_op jit(solution)/shard_map/all_to_all | solution.py:496
  9.8 11.1 %copy-start = (bf16[504,1024]{1,0:T(8,128)(2,1)S(1)}, bf16[504,1024]{1,0:T(8,128)(2,1)}, u32[]{:S(2)}) copy-start(bf16[504,1024]{1,0:T(8,128)(2,1)} %constant.19.clone.choose) | copy-start | bytes 3096580
  9.8 11.1 %copy-start.3 = (f32[16,128]{1,0:T(8,128)S(1)}, f32[16,128]{1,0:T(8,128)}, u32[]{:S(2)}) copy-start(f32[16,128]{1,0:T(8,128)} %get-tuple-element.10.own) | copy-start | bytes 24580
  13.3 13.0 %copy-start.2 = (f32[96,128]{1,0:T(8,128)S(1)}, f32[96,128]{1,0:T(8,128)}, u32[]{:S(2)}) copy-start(f32[96,128]{1,0:T(8,128)} %constant.20.clone.taper) | copy-start | bytes 147460
  17.3 16.2 %all-to-all-start.1 = ((bf16[48,8,8,128]{3,2,1,0:T(8,128)(2,1)}), bf16[48,8,8,128]{3,2,1,0:T(8,128)(2,1)S(1)}, u32[]{:S(2)}, u32[]{:S(2)}) async-start(bf16[48,8,8,128]{3,2,1,0:T(8,128)(2,1)} %bitcast.10), calls=%async_computation.1 | async-start | bytes 1572864 | tf_op jit(solution)/shard_map/all_to_all | solution.py:497
  21.3 5.0 %collective-permute-start.1 = (f32[9,56,128]{2,1,0:T(8,128)S(1)}, f32[9,56,128]{2,1,0:T(8,128)S(1)}, u32[]{:S(2)}, u32[]{:S(2)}) collective-permute-start(f32[9,56,128]{2,1,0:T(8,128)S(1)} %sample.1.own), channel_id=1, source_target_pairs={{0,1},{1,0},{2,3},{3,2},{4,5},{5,4},{6,7},{7,6},{8,9},{9,8},{10,11... | collective-permute-start | bytes 774152 | tf_op jit(solution)/shard_map/ppermute | solution.py:509
  23.5 7.3 %collective-permute-start = (f32[9,56,128]{2,1,0:T(8,128)S(1)}, f32[9,56,128]{2,1,0:T(8,128)S(1)}, u32[]{:S(2)}, u32[]{:S(2)}) collective-permute-start(f32[9,56,128]{2,1,0:T(8,128)S(1)} %sample.1.own), channel_id=1, source_target_pairs={{0,15},{1,2},{2,1},{3,4},{4,3},{5,6},{6,5},{7,8},{8,7},{9,10},{10,... | collective-permute-start | bytes 774152 | tf_op jit(solution)/shard_map/ppermute | solution.py:510
  27.6 5.9 %copy-start.1 = (bf16[256,512]{1,0:T(8,128)(2,1)S(1)}, bf16[256,512]{1,0:T(8,128)(2,1)}, u32[]{:S(2)}) copy-start(bf16[256,512]{1,0:T(8,128)(2,1)} %constant.21.clone.expand) | copy-start | bytes 786436

commit v7 on v6

--- a/solution.py
+++ b/solution.py
@@ -526,7 +526,7 @@
         out_specs=VM,
         out_shape=jax.ShapeDtypeStruct((WEIGHT_ROWS, LANES), F32),
         scratch_shapes=[
-            pltpu.VMEM((BLOCKS_Y * PACK, LANES), F32),
+            pltpu.VMEM((BLOCKS_Y * PACK + 64, LANES), F32),
             pltpu.VMEM((24, 48, LANES), F32),
             pltpu.VMEM((2, 8, 48, LANES), F32),
             pltpu.VMEM((2, 8, 48, LANES), F32),

time: 59.8 us -> 59.8 us (level)
  no operation moved by 1% of the time
where the time goes in v7:
time: 59.8 us; the launch traced here: 59.4 us
  blocking collectives  20.7 us (35%)
  Pallas kernels  15.6 us (26%)
  starting transfers between devices  15.3 us (26%)
  waiting for transfers between devices  7.05 us (12%)
  between operations  0.76 us (1%)
    all_to_all x1, blocking collectives, body(): result = lax.all_to_all(result, 'member', 0, 0, tiled=True)  20.7 us
    all_to_all x1, starting transfers between devices, body(): packed = lax.all_to_all(packed, 'member', 0, 0, tiled=True)  6.75 us
    pallas_call x1, Pallas kernels, body(): pl.pallas_call(transform_kernel, in_specs=[VM, VM, VM], out_specs=VM, out...  4.23 us
    all_to_all x1, waiting for transfers between devices, body(): packed = lax.all_to_all(packed, 'member', 0, 0, tiled=True)  3.93 us
    all_to_all x1, starting transfers between devices, body(): lax.all_to_all(fields.reshape(MEMBERS, UPPER, 8, LANES), 'member', 0, 0,...  3.61 us
    pallas_call x1, Pallas kernels, body(): pl.pallas_call(send_kernel, grid=(3,), in_specs=[pl.BlockSpec((1, 2 * UPP...  3.5 us
    ppermute x1, waiting for transfers between devices, body(): lax.ppermute(sampled, 'tile', [(i, (i + 1 if i % 2 else i - 1) % tiles) f...  3.12 us
    ppermute x1, starting transfers between devices, body(): lax.ppermute(sampled, 'tile', [(i, (i + 1 if i % 2 else i - 1) % tiles) f...  2.84 us
  transfers between devices with their start and end apart: 4, of which 2 were waited for; matrix products, arithmetic and copies ran while one was open for 0% of the time, Pallas kernels for 8%

profile of v7, /device:TPU:97, one launch (start us, length us, event | category | flops | bytes accessed | tf_op | source)
XLA Modules:
  0.0 59.4 jit_solution(5425943361081805192)
XLA Ops:
  0.7 2.4 %pack.1 = (bf16[16,64,128]{2,1,0:T(8,128)(2,1)}, f32[16,128]{1,0:T(8,128)}) custom-call(s32[1]{0:T(128)} %bitcast.1.where, s32[1]{0:T(128)} %bitcast.8.tally, bf16[3,16,8,2048]{3,2,1,0:T(8,128)(2,1)} %x_ref.3, f32[1,256]{1,0:T(1,128)} %bitcast.11, f32[1,256]{1,0:T(1,128)} %bitcast.12, s32[1,256]{1,0:T(1,128)} %bitcast.13, ...), custom_call_target="tpu_custom_call" | custom-call | tf_op jit(solution)/shard_map/pack/pallas_call | solution.py:450
  3.0 6.8 %all-to-all-start = ((bf16[16,64,128]{2,1,0:T(8,128)(2,1)}), bf16[16,64,128]{2,1,0:T(8,128)(2,1)S(1)}, u32[]{:S(2)}, u32[]{:S(2)}) async-start(bf16[16,64,128]{2,1,0:T(8,128)(2,1)} %get-tuple-element.9), calls=%async_computation | async-start | bytes 524288 | tf_op jit(solution)/shard_map/all_to_all | solution.py:496
  9.8 0.0 copy-start
  9.8 0.0 copy-start.3
  9.8 3.5 %send.1 = (bf16[16,3,8,8,128]{4,3,2,1,0:T(8,128)(2,1)}, bf16[3,16,8,2048]{3,2,1,0:T(8,128)(2,1)}) custom-call(bf16[3,16,8,2048]{3,2,1,0:T(8,128)(2,1)} %x_ref.3), custom_call_target="tpu_custom_call" | custom-call | tf_op jit(solution)/shard_map/send/pallas_call | solution.py:481
  13.3 0.0 copy-start.2
  13.3 3.9 %all-to-all-done.r_ref = bf16[16,64,128]{2,1,0:T(8,128)(2,1)S(1)} async-done(((bf16[16,64,128]{2,1,0:T(8,128)(2,1)}), bf16[16,64,128]{2,1,0:T(8,128)(2,1)S(1)}, u32[]{:S(2)}, u32[]{:S(2)}) %all-to-all-start) | async-done | bytes 262176 | tf_op jit(solution)/shard_map/all_to_all | solution.py:496
  17.3 3.6 %all-to-all-start.1 = ((bf16[48,8,8,128]{3,2,1,0:T(8,128)(2,1)}), bf16[48,8,8,128]{3,2,1,0:T(8,128)(2,1)S(1)}, u32[]{:S(2)}, u32[]{:S(2)}) async-start(bf16[48,8,8,128]{3,2,1,0:T(8,128)(2,1)} %bitcast.10), calls=%async_computation.1 | async-start | bytes 1572864 | tf_op jit(solution)/shard_map/all_to_all | solution.py:497
  20.9 0.0 copy-done
  20.9 0.0 copy-done.3
  20.9 0.4 sample.1.own
  21.3 2.1 %collective-permute-start.1 = (f32[9,56,128]{2,1,0:T(8,128)S(1)}, f32[9,56,128]{2,1,0:T(8,128)S(1)}, u32[]{:S(2)}, u32[]{:S(2)}) collective-permute-start(f32[9,56,128]{2,1,0:T(8,128)S(1)} %sample.1.own), channel_id=1, source_target_pairs={{0,1},{1,0},{2,3},{3,2},{4,5},{5,4},{6,7},{7,6},{8,9},{9,8},{10,11... | collective-permute-start | bytes 774152 | tf_op jit(solution)/shard_map/ppermute | solution.py:509
  23.5 2.8 %collective-permute-start = (f32[9,56,128]{2,1,0:T(8,128)S(1)}, f32[9,56,128]{2,1,0:T(8,128)S(1)}, u32[]{:S(2)}, u32[]{:S(2)}) collective-permute-start(f32[9,56,128]{2,1,0:T(8,128)S(1)} %sample.1.own), channel_id=1, source_target_pairs={{0,15},{1,2},{2,1},{3,4},{4,3},{5,6},{6,5},{7,8},{8,7},{9,10},{10,... | collective-permute-start | bytes 774152 | tf_op jit(solution)/shard_map/ppermute | solution.py:510
  26.3 0.0 collective-permute-done.1.pair
  26.3 0.0 copy-done.2
  26.3 1.3 %near_gram.1.partial = f32[1792,128]{1,0:T(8,128)S(1)} custom-call(s32[1]{0:T(128)} %bitcast.tile, f32[9,56,128]{2,1,0:T(8,128)S(1)} %sample.1.own, f32[9,56,128]{2,1,0:T(8,128)S(1)} %collective-permute-done.1.pair, f32[96,128]{1,0:T(8,128)S(1)} %copy-done.2), custom_call_target="tpu_custom_call" | custom-call | flops 1000000000 | bytes 3000000 | tf_op jit(solution)/shard_map/near_gram/pallas_call | solution.py:514
  27.6 0.0 copy-start.1
  27.6 3.1 %collective-permute-done.following = f32[9,56,128]{2,1,0:T(8,128)S(1)} collective-permute-done((f32[9,56,128]{2,1,0:T(8,128)S(1)}, f32[9,56,128]{2,1,0:T(8,128)S(1)}, u32[]{:S(2)}, u32[]{:S(2)}) %collective-permute-start) | collective-permute-done | bytes 258080 | tf_op jit(solution)/shard_map/ppermute | solution.py:510
  30.7 2.8 %solve.1.w_ref = f32[744,128]{1,0:T(8,128)S(1)} custom-call(s32[1]{0:T(128)} %bitcast.tile, f32[9,56,128]{2,1,0:T(8,128)S(1)} %collective-permute-done.following, f32[1792,128]{1,0:T(8,128)S(1)} %near_gram.1.partial, f32[96,128]{1,0:T(8,128)S(1)} %copy-done.2), custom_call_target="tpu_custom_call" | custom-call | tf_op jit(solution)/shard_map/solve/pallas_call | solution.py:523
  33.5 0.0 all-to-all-done.1.x_ref
  33.5 0.0 copy-done.1
  33.5 4.2 %transform.1 = bf16[48,8,8,128]{3,2,1,0:T(8,128)(2,1)S(1)} custom-call(f32[744,128]{1,0:T(8,128)S(1)} %solve.1.w_ref, bf16[48,8,8,128]{3,2,1,0:T(8,128)(2,1)S(1)} %all-to-all-done.1.x_ref, bf16[256,512]{1,0:T(8,128)(2,1)S(1)} %copy-done.1), custom_call_target="tpu_custom_call" | custom-call | tf_op jit(solution)/shard_map/transform/pallas_call | solution.py:537
  37.8 20.7 %all_to_all.15 = bf16[48,8,8,128]{3,2,1,0:T(8,128)(2,1)S(1)} all-to-all(bf16[48,8,8,128]{3,2,1,0:T(8,128)(2,1)S(1)} %transform.1), channel_id=1, replica_groups=mesh['member'=16,'tile'=16] {'member'}, dimensions={0} | all-to-all | bytes 1572864 | tf_op jit(solution)/shard_map/all_to_all | solution.py:550
  58.5 0.9 %finish.1 = bf16[3,16,8,2048]{3,2,1,0:T(8,128)(2,1)} custom-call(bf16[16,3,8,8,128]{4,3,2,1,0:T(8,128)(2,1)S(1)} %bitcast.9, bf16[3,16,8,2048]{3,2,1,0:T(8,128)(2,1)} %get-tuple-element.12.partial), custom_call_target="tpu_custom_call", output_to_operand_aliasing={{}: (1, {})} | custom-call | tf_op jit(solution)/shard_map/finish/pallas_call | solution.py:551
Async XLA Ops:
  3.0 14.2 %all-to-all-start = ((bf16[16,64,128]{2,1,0:T(8,128)(2,1)}), bf16[16,64,128]{2,1,0:T(8,128)(2,1)S(1)}, u32[]{:S(2)}, u32[]{:S(2)}) async-start(bf16[16,64,128]{2,1,0:T(8,128)(2,1)} %get-tuple-element.9), calls=%async_computation | async-start | bytes 524288 | tf_op jit(solution)/shard_map/all_to_all | solution.py:496
  9.8 11.1 %copy-start = (bf16[504,1024]{1,0:T(8,128)(2,1)S(1)}, bf16[504,1024]{1,0:T(8,128)(2,1)}, u32[]{:S(2)}) copy-start(bf16[504,1024]{1,0:T(8,128)(2,1)} %constant.19.clone.choose) | copy-start | bytes 3096580
  9.8 11.1 %copy-start.3 = (f32[16,128]{1,0:T(8,128)S(1)}, f32[16,128]{1,0:T(8,128)}, u32[]{:S(2)}) copy-start(f32[16,128]{1,0:T(8,128)} %get-tuple-element.10.own) | copy-start | bytes 24580
  13.3 13.0 %copy-start.2 = (f32[96,128]{1,0:T(8,128)S(1)}, f32[96,128]{1,0:T(8,128)}, u32[]{:S(2)}) copy-start(f32[96,128]{1,0:T(8,128)} %constant.20.clone.taper) | copy-start | bytes 147460
  17.3 16.2 %all-to-all-start.1 = ((bf16[48,8,8,128]{3,2,1,0:T(8,128)(2,1)}), bf16[48,8,8,128]{3,2,1,0:T(8,128)(2,1)S(1)}, u32[]{:S(2)}, u32[]{:S(2)}) async-start(bf16[48,8,8,128]{3,2,1,0:T(8,128)(2,1)} %bitcast.10), calls=%async_computation.1 | async-start | bytes 1572864 | tf_op jit(solution)/shard_map/all_to_all | solution.py:497
  21.3 5.0 %collective-permute-start.1 = (f32[9,56,128]{2,1,0:T(8,128)S(1)}, f32[9,56,128]{2,1,0:T(8,128)S(1)}, u32[]{:S(2)}, u32[]{:S(2)}) collective-permute-start(f32[9,56,128]{2,1,0:T(8,128)S(1)} %sample.1.own), channel_id=1, source_target_pairs={{0,1},{1,0},{2,3},{3,2},{4,5},{5,4},{6,7},{7,6},{8,9},{9,8},{10,11... | collective-permute-start | bytes 774152 | tf_op jit(solution)/shard_map/ppermute | solution.py:509
  23.5 7.3 %collective-permute-start = (f32[9,56,128]{2,1,0:T(8,128)S(1)}, f32[9,56,128]{2,1,0:T(8,128)S(1)}, u32[]{:S(2)}, u32[]{:S(2)}) collective-permute-start(f32[9,56,128]{2,1,0:T(8,128)S(1)} %sample.1.own), channel_id=1, source_target_pairs={{0,15},{1,2},{2,1},{3,4},{4,3},{5,6},{6,5},{7,8},{8,7},{9,10},{10,... | collective-permute-start | bytes 774152 | tf_op jit(solution)/shard_map/ppermute | solution.py:510
  27.6 5.9 %copy-start.1 = (bf16[256,512]{1,0:T(8,128)(2,1)S(1)}, bf16[256,512]{1,0:T(8,128)(2,1)}, u32[]{:S(2)}) copy-start(bf16[256,512]{1,0:T(8,128)(2,1)} %constant.21.clone.expand) | copy-start | bytes 786436

commit v8 on v7

--- a/solution.py
+++ b/solution.py
@@ -123,7 +123,7 @@
     return np.concatenate([m, m], 0)
 
 
-def pack_kernel(where, tally, x_ref, reading, error, cell, spread, compact, out, own, work):
+def pack_kernel(where, tally, x_ref, reading, error, cell, spread, compact, out, own, work, chunk, sems):
     me = where[0]
     live = lax.broadcasted_iota(jnp.int32, (1, SLOTS), 1) < tally[0]
     prec = jnp.where(live, 1.0 / error[...], 0.0)
@@ -176,8 +176,14 @@
         work[d, 72:80, :] = jnp.where(
             me == d - 1, last, jnp.where(me == d + 1, first, jnp.zeros_like(first))
         )
+    copies = []
     for d in range(DOMS):
-        out[d] = nn(compact[...], work[d].astype(BF16)).astype(BF16)
+        chunk[d] = nn(compact[...], work[d].astype(BF16)).astype(BF16)
+        copy = pltpu.make_async_copy(chunk.at[d], out.at[d], sems.at[d])
+        copy.start()
+        copies.append(copy)
+    for copy in copies:
+        copy.wait()
 
 
 def sample_kernel(r_ref, own, choose, out):
@@ -413,7 +419,7 @@
                     out[2 * t + h, l] = acc[8 * h + l].astype(BF16)
             return c
 
-        lax.fori_loop(0, 4, pair, 0)
+        lax.fori_loop(0, 4, pair, 0, unroll=2)
 
 
 def send_kernel(x_ref, out, lower):
@@ -460,12 +466,16 @@
             whole(64, 48),
             whole(ROWS, 80),
         ],
-        out_specs=[VM, VM],
+        out_specs=[ANY, VM],
         out_shape=[
             jax.ShapeDtypeStruct((DOMS, ROWS, LANES), BF16),
             jax.ShapeDtypeStruct((16, LANES), F32),
         ],
-        scratch_shapes=[pltpu.VMEM((DOMS, 80, LANES), F32)],
+        scratch_shapes=[
+            pltpu.VMEM((DOMS, 80, LANES), F32),
+            pltpu.VMEM((DOMS, ROWS, LANES), BF16),
+            pltpu.SemaphoreType.DMA((DOMS,)),
+        ],
         compiler_params=FULL,
         name="pack",
     )(

time: 59.8 us -> 60.4 us (1.010)
    pallas_call x1, Pallas kernels: 2.38 us -> 3.04 us  [body(): pl.pallas_call(pack_kernel, grid=(1,), in_specs=[SM, SM, whole(3, 2, 8, 2...]
  transfers between devices with their start and end apart: 4 -> 4, of which waited for: 2 -> 2; matrix products, arithmetic and copies ran while one was open for 0% -> 0% of each run, Pallas kernels for 8% -> 7%
where the time goes in v8:
time: 60.4 us; the launch traced here: 60 us
  blocking collectives  20.8 us (34%)
  Pallas kernels  16.1 us (27%)
  starting transfers between devices  15.3 us (25%)
  waiting for transfers between devices  7.05 us (12%)
  between operations  0.76 us (1%)
    all_to_all x1, blocking collectives, body(): result = lax.all_to_all(result, 'member', 0, 0, tiled=True)  20.8 us
    all_to_all x1, starting transfers between devices, body(): packed = lax.all_to_all(packed, 'member', 0, 0, tiled=True)  6.77 us
    pallas_call x1, Pallas kernels, body(): pl.pallas_call(transform_kernel, in_specs=[VM, VM, VM], out_specs=VM, out...  4.12 us
    all_to_all x1, waiting for transfers between devices, body(): packed = lax.all_to_all(packed, 'member', 0, 0, tiled=True)  3.93 us
    all_to_all x1, starting transfers between devices, body(): lax.all_to_all(fields.reshape(MEMBERS, UPPER, 8, LANES), 'member', 0, 0,...  3.61 us
    pallas_call x1, Pallas kernels, body(): pl.pallas_call(send_kernel, grid=(3,), in_specs=[pl.BlockSpec((1, 2 * UPP...  3.5 us
    ppermute x1, waiting for transfers between devices, body(): lax.ppermute(sampled, 'tile', [(i, (i + 1 if i % 2 else i - 1) % tiles) f...  3.12 us
    pallas_call x1, Pallas kernels, body(): pl.pallas_call(pack_kernel, grid=(1,), in_specs=[SM, SM, whole(3, 2, 8, 2...  3.04 us
  transfers between devices with their start and end apart: 4, of which 2 were waited for; matrix products, arithmetic and copies ran while one was open for 0% of the time, Pallas kernels for 7%

profile of v8, /device:TPU:97, one launch (start us, length us, event | category | flops | bytes accessed | tf_op | source)
XLA Modules:
  0.0 60.0 jit_solution(4472440706708258404)
XLA Ops:
  0.7 3.0 %pack.1 = (bf16[16,64,128]{2,1,0:T(8,128)(2,1)}, f32[16,128]{1,0:T(8,128)}) custom-call(s32[1]{0:T(128)} %bitcast.1.where, s32[1]{0:T(128)} %bitcast.8.tally, bf16[3,16,8,2048]{3,2,1,0:T(8,128)(2,1)} %x_ref.3, f32[1,256]{1,0:T(1,128)} %bitcast.11, f32[1,256]{1,0:T(1,128)} %bitcast.12, s32[1,256]{1,0:T(1,128)} %bitcast.13, ...), custom_call_target="tpu_custom_call" | custom-call | tf_op jit(solution)/shard_map/pack/pallas_call | solution.py:456
  3.7 6.8 %all-to-all-start = ((bf16[16,64,128]{2,1,0:T(8,128)(2,1)}), bf16[16,64,128]{2,1,0:T(8,128)(2,1)S(1)}, u32[]{:S(2)}, u32[]{:S(2)}) async-start(bf16[16,64,128]{2,1,0:T(8,128)(2,1)} %get-tuple-element.9), calls=%async_computation | async-start | bytes 524288 | tf_op jit(solution)/shard_map/all_to_all | solution.py:506
  10.5 0.0 copy-start
  10.5 0.0 copy-start.3
  10.5 3.5 %send.1 = (bf16[16,3,8,8,128]{4,3,2,1,0:T(8,128)(2,1)}, bf16[3,16,8,2048]{3,2,1,0:T(8,128)(2,1)}) custom-call(bf16[3,16,8,2048]{3,2,1,0:T(8,128)(2,1)} %x_ref.3), custom_call_target="tpu_custom_call" | custom-call | tf_op jit(solution)/shard_map/send/pallas_call | solution.py:491
  14.0 0.0 copy-start.2
  14.0 3.9 %all-to-all-done.r_ref = bf16[16,64,128]{2,1,0:T(8,128)(2,1)S(1)} async-done(((bf16[16,64,128]{2,1,0:T(8,128)(2,1)}), bf16[16,64,128]{2,1,0:T(8,128)(2,1)S(1)}, u32[]{:S(2)}, u32[]{:S(2)}) %all-to-all-start) | async-done | bytes 262176 | tf_op jit(solution)/shard_map/all_to_all | solution.py:506
  17.9 3.6 %all-to-all-start.1 = ((bf16[48,8,8,128]{3,2,1,0:T(8,128)(2,1)}), bf16[48,8,8,128]{3,2,1,0:T(8,128)(2,1)S(1)}, u32[]{:S(2)}, u32[]{:S(2)}) async-start(bf16[48,8,8,128]{3,2,1,0:T(8,128)(2,1)} %bitcast.10), calls=%async_computation.1 | async-start | bytes 1572864 | tf_op jit(solution)/shard_map/all_to_all | solution.py:507
  21.5 0.0 copy-done
  21.6 0.0 copy-done.3
  21.6 0.4 sample.1.own
  22.0 2.1 %collective-permute-start.1 = (f32[9,56,128]{2,1,0:T(8,128)S(1)}, f32[9,56,128]{2,1,0:T(8,128)S(1)}, u32[]{:S(2)}, u32[]{:S(2)}) collective-permute-start(f32[9,56,128]{2,1,0:T(8,128)S(1)} %sample.1.own), channel_id=1, source_target_pairs={{0,1},{1,0},{2,3},{3,2},{4,5},{5,4},{6,7},{7,6},{8,9},{9,8},{10,11... | collective-permute-start | bytes 774152 | tf_op jit(solution)/shard_map/ppermute | solution.py:519
  24.1 2.8 %collective-permute-start = (f32[9,56,128]{2,1,0:T(8,128)S(1)}, f32[9,56,128]{2,1,0:T(8,128)S(1)}, u32[]{:S(2)}, u32[]{:S(2)}) collective-permute-start(f32[9,56,128]{2,1,0:T(8,128)S(1)} %sample.1.own), channel_id=1, source_target_pairs={{0,15},{1,2},{2,1},{3,4},{4,3},{5,6},{6,5},{7,8},{8,7},{9,10},{10,... | collective-permute-start | bytes 774152 | tf_op jit(solution)/shard_map/ppermute | solution.py:520
  27.0 0.0 collective-permute-done.1.pair
  27.0 0.0 copy-done.2
  27.0 1.3 %near_gram.1.partial = f32[1792,128]{1,0:T(8,128)S(1)} custom-call(s32[1]{0:T(128)} %bitcast.tile, f32[9,56,128]{2,1,0:T(8,128)S(1)} %sample.1.own, f32[9,56,128]{2,1,0:T(8,128)S(1)} %collective-permute-done.1.pair, f32[96,128]{1,0:T(8,128)S(1)} %copy-done.2), custom_call_target="tpu_custom_call" | custom-call | flops 1000000000 | bytes 3000000 | tf_op jit(solution)/shard_map/near_gram/pallas_call | solution.py:524
  28.3 0.0 copy-start.1
  28.3 3.1 %collective-permute-done.following = f32[9,56,128]{2,1,0:T(8,128)S(1)} collective-permute-done((f32[9,56,128]{2,1,0:T(8,128)S(1)}, f32[9,56,128]{2,1,0:T(8,128)S(1)}, u32[]{:S(2)}, u32[]{:S(2)}) %collective-permute-start) | collective-permute-done | bytes 258080 | tf_op jit(solution)/shard_map/ppermute | solution.py:520
  31.4 2.8 %solve.1.w_ref = f32[744,128]{1,0:T(8,128)S(1)} custom-call(s32[1]{0:T(128)} %bitcast.tile, f32[9,56,128]{2,1,0:T(8,128)S(1)} %collective-permute-done.following, f32[1792,128]{1,0:T(8,128)S(1)} %near_gram.1.partial, f32[96,128]{1,0:T(8,128)S(1)} %copy-done.2), custom_call_target="tpu_custom_call" | custom-call | tf_op jit(solution)/shard_map/solve/pallas_call | solution.py:533
  34.2 0.0 all-to-all-done.1.x_ref
  34.2 0.0 copy-done.1
  34.2 4.1 %transform.1 = bf16[48,8,8,128]{3,2,1,0:T(8,128)(2,1)S(1)} custom-call(f32[744,128]{1,0:T(8,128)S(1)} %solve.1.w_ref, bf16[48,8,8,128]{3,2,1,0:T(8,128)(2,1)S(1)} %all-to-all-done.1.x_ref, bf16[256,512]{1,0:T(8,128)(2,1)S(1)} %copy-done.1), custom_call_target="tpu_custom_call" | custom-call | tf_op jit(solution)/shard_map/transform/pallas_call | solution.py:547
  38.3 20.8 %all_to_all.15 = bf16[48,8,8,128]{3,2,1,0:T(8,128)(2,1)S(1)} all-to-all(bf16[48,8,8,128]{3,2,1,0:T(8,128)(2,1)S(1)} %transform.1), channel_id=1, replica_groups=mesh['member'=16,'tile'=16] {'member'}, dimensions={0} | all-to-all | bytes 1572864 | tf_op jit(solution)/shard_map/all_to_all | solution.py:560
  59.1 0.9 %finish.1 = bf16[3,16,8,2048]{3,2,1,0:T(8,128)(2,1)} custom-call(bf16[16,3,8,8,128]{4,3,2,1,0:T(8,128)(2,1)S(1)} %bitcast.9, bf16[3,16,8,2048]{3,2,1,0:T(8,128)(2,1)} %get-tuple-element.12.partial), custom_call_target="tpu_custom_call", output_to_operand_aliasing={{}: (1, {})} | custom-call | tf_op jit(solution)/shard_map/finish/pallas_call | solution.py:561
Async XLA Ops:
  3.7 14.2 %all-to-all-start = ((bf16[16,64,128]{2,1,0:T(8,128)(2,1)}), bf16[16,64,128]{2,1,0:T(8,128)(2,1)S(1)}, u32[]{:S(2)}, u32[]{:S(2)}) async-start(bf16[16,64,128]{2,1,0:T(8,128)(2,1)} %get-tuple-element.9), calls=%async_computation | async-start | bytes 524288 | tf_op jit(solution)/shard_map/all_to_all | solution.py:506
  10.5 11.1 %copy-start = (bf16[504,1024]{1,0:T(8,128)(2,1)S(1)}, bf16[504,1024]{1,0:T(8,128)(2,1)}, u32[]{:S(2)}) copy-start(bf16[504,1024]{1,0:T(8,128)(2,1)} %constant.19.clone.choose) | copy-start | bytes 3096580
  10.5 11.1 %copy-start.3 = (f32[16,128]{1,0:T(8,128)S(1)}, f32[16,128]{1,0:T(8,128)}, u32[]{:S(2)}) copy-start(f32[16,128]{1,0:T(8,128)} %get-tuple-element.10.own) | copy-start | bytes 24580
  14.0 13.0 %copy-start.2 = (f32[96,128]{1,0:T(8,128)S(1)}, f32[96,128]{1,0:T(8,128)}, u32[]{:S(2)}) copy-start(f32[96,128]{1,0:T(8,128)} %constant.20.clone.taper) | copy-start | bytes 147460
  17.9 16.3 %all-to-all-start.1 = ((bf16[48,8,8,128]{3,2,1,0:T(8,128)(2,1)}), bf16[48,8,8,128]{3,2,1,0:T(8,128)(2,1)S(1)}, u32[]{:S(2)}, u32[]{:S(2)}) async-start(bf16[48,8,8,128]{3,2,1,0:T(8,128)(2,1)} %bitcast.10), calls=%async_computation.1 | async-start | bytes 1572864 | tf_op jit(solution)/shard_map/all_to_all | solution.py:507
  22.0 5.0 %collective-permute-start.1 = (f32[9,56,128]{2,1,0:T(8,128)S(1)}, f32[9,56,128]{2,1,0:T(8,128)S(1)}, u32[]{:S(2)}, u32[]{:S(2)}) collective-permute-start(f32[9,56,128]{2,1,0:T(8,128)S(1)} %sample.1.own), channel_id=1, source_target_pairs={{0,1},{1,0},{2,3},{3,2},{4,5},{5,4},{6,7},{7,6},{8,9},{9,8},{10,11... | collective-permute-start | bytes 774152 | tf_op jit(solution)/shard_map/ppermute | solution.py:519
  24.1 7.3 %collective-permute-start = (f32[9,56,128]{2,1,0:T(8,128)S(1)}, f32[9,56,128]{2,1,0:T(8,128)S(1)}, u32[]{:S(2)}, u32[]{:S(2)}) collective-permute-start(f32[9,56,128]{2,1,0:T(8,128)S(1)} %sample.1.own), channel_id=1, source_target_pairs={{0,15},{1,2},{2,1},{3,4},{4,3},{5,6},{6,5},{7,8},{8,7},{9,10},{10,... | collective-permute-start | bytes 774152 | tf_op jit(solution)/shard_map/ppermute | solution.py:520
  28.3 5.9 %copy-start.1 = (bf16[256,512]{1,0:T(8,128)(2,1)S(1)}, bf16[256,512]{1,0:T(8,128)(2,1)}, u32[]{:S(2)}) copy-start(bf16[256,512]{1,0:T(8,128)(2,1)} %constant.21.clone.expand) | copy-start | bytes 786436

commit v9 on v7

--- a/solution.py
+++ b/solution.py
@@ -413,7 +413,7 @@
                     out[2 * t + h, l] = acc[8 * h + l].astype(BF16)
             return c
 
-        lax.fori_loop(0, 4, pair, 0)
+        lax.fori_loop(0, 4, pair, 0, unroll=2)
 
 
 def send_kernel(x_ref, out, lower):

time: 59.8 us -> 59.7 us (level)
  no operation moved by 1% of the time
where the time goes in v9:
time: 59.7 us; the launch traced here: 59.3 us
  blocking collectives  20.7 us (35%)
  Pallas kernels  15.4 us (26%)
  starting transfers between devices  15.3 us (26%)
  waiting for transfers between devices  7.05 us (12%)
  between operations  0.76 us (1%)
    all_to_all x1, blocking collectives, body(): result = lax.all_to_all(result, 'member', 0, 0, tiled=True)  20.7 us
    all_to_all x1, starting transfers between devices, body(): packed = lax.all_to_all(packed, 'member', 0, 0, tiled=True)  6.75 us
    pallas_call x1, Pallas kernels, body(): pl.pallas_call(transform_kernel, in_specs=[VM, VM, VM], out_specs=VM, out...  4.12 us
    all_to_all x1, waiting for transfers between devices, body(): packed = lax.all_to_all(packed, 'member', 0, 0, tiled=True)  3.93 us
    all_to_all x1, starting transfers between devices, body(): lax.all_to_all(fields.reshape(MEMBERS, UPPER, 8, LANES), 'member', 0, 0,...  3.61 us
    pallas_call x1, Pallas kernels, body(): pl.pallas_call(send_kernel, grid=(3,), in_specs=[pl.BlockSpec((1, 2 * UPP...  3.5 us
    ppermute x1, waiting for transfers between devices, body(): lax.ppermute(sampled, 'tile', [(i, (i + 1 if i % 2 else i - 1) % tiles) f...  3.12 us
    ppermute x1, starting transfers between devices, body(): lax.ppermute(sampled, 'tile', [(i, (i + 1 if i % 2 else i - 1) % tiles) f...  2.84 us
  transfers between devices with their start and end apart: 4, of which 2 were waited for; matrix products, arithmetic and copies ran while one was open for 0% of the time, Pallas kernels for 8%

profile of v9, /device:TPU:97, one launch (start us, length us, event | category | flops | bytes accessed | tf_op | source)
XLA Modules:
  0.0 59.3 jit_solution(12886441266974374119)
XLA Ops:
  0.7 2.4 %pack.1 = (bf16[16,64,128]{2,1,0:T(8,128)(2,1)}, f32[16,128]{1,0:T(8,128)}) custom-call(s32[1]{0:T(128)} %bitcast.1.where, s32[1]{0:T(128)} %bitcast.8.tally, bf16[3,16,8,2048]{3,2,1,0:T(8,128)(2,1)} %x_ref.3, f32[1,256]{1,0:T(1,128)} %bitcast.11, f32[1,256]{1,0:T(1,128)} %bitcast.12, s32[1,256]{1,0:T(1,128)} %bitcast.13, ...), custom_call_target="tpu_custom_call" | custom-call | tf_op jit(solution)/shard_map/pack/pallas_call | solution.py:450
  3.0 6.8 %all-to-all-start = ((bf16[16,64,128]{2,1,0:T(8,128)(2,1)}), bf16[16,64,128]{2,1,0:T(8,128)(2,1)S(1)}, u32[]{:S(2)}, u32[]{:S(2)}) async-start(bf16[16,64,128]{2,1,0:T(8,128)(2,1)} %get-tuple-element.9), calls=%async_computation | async-start | bytes 524288 | tf_op jit(solution)/shard_map/all_to_all | solution.py:496
  9.8 0.0 copy-start
  9.8 0.0 copy-start.3
  9.8 3.5 %send.1 = (bf16[16,3,8,8,128]{4,3,2,1,0:T(8,128)(2,1)}, bf16[3,16,8,2048]{3,2,1,0:T(8,128)(2,1)}) custom-call(bf16[3,16,8,2048]{3,2,1,0:T(8,128)(2,1)} %x_ref.3), custom_call_target="tpu_custom_call" | custom-call | tf_op jit(solution)/shard_map/send/pallas_call | solution.py:481
  13.3 0.0 copy-start.2
  13.3 3.9 %all-to-all-done.r_ref = bf16[16,64,128]{2,1,0:T(8,128)(2,1)S(1)} async-done(((bf16[16,64,128]{2,1,0:T(8,128)(2,1)}), bf16[16,64,128]{2,1,0:T(8,128)(2,1)S(1)}, u32[]{:S(2)}, u32[]{:S(2)}) %all-to-all-start) | async-done | bytes 262176 | tf_op jit(solution)/shard_map/all_to_all | solution.py:496
  17.3 3.6 %all-to-all-start.1 = ((bf16[48,8,8,128]{3,2,1,0:T(8,128)(2,1)}), bf16[48,8,8,128]{3,2,1,0:T(8,128)(2,1)S(1)}, u32[]{:S(2)}, u32[]{:S(2)}) async-start(bf16[48,8,8,128]{3,2,1,0:T(8,128)(2,1)} %bitcast.10), calls=%async_computation.1 | async-start | bytes 1572864 | tf_op jit(solution)/shard_map/all_to_all | solution.py:497
  20.9 0.0 copy-done
  20.9 0.0 copy-done.3
  20.9 0.4 sample.1.own
  21.3 2.1 %collective-permute-start.1 = (f32[9,56,128]{2,1,0:T(8,128)S(1)}, f32[9,56,128]{2,1,0:T(8,128)S(1)}, u32[]{:S(2)}, u32[]{:S(2)}) collective-permute-start(f32[9,56,128]{2,1,0:T(8,128)S(1)} %sample.1.own), channel_id=1, source_target_pairs={{0,1},{1,0},{2,3},{3,2},{4,5},{5,4},{6,7},{7,6},{8,9},{9,8},{10,11... | collective-permute-start | bytes 774152 | tf_op jit(solution)/shard_map/ppermute | solution.py:509
  23.5 2.8 %collective-permute-start = (f32[9,56,128]{2,1,0:T(8,128)S(1)}, f32[9,56,128]{2,1,0:T(8,128)S(1)}, u32[]{:S(2)}, u32[]{:S(2)}) collective-permute-start(f32[9,56,128]{2,1,0:T(8,128)S(1)} %sample.1.own), channel_id=1, source_target_pairs={{0,15},{1,2},{2,1},{3,4},{4,3},{5,6},{6,5},{7,8},{8,7},{9,10},{10,... | collective-permute-start | bytes 774152 | tf_op jit(solution)/shard_map/ppermute | solution.py:510
  26.3 0.0 collective-permute-done.1.pair
  26.3 0.0 copy-done.2
  26.3 1.3 %near_gram.1.partial = f32[1792,128]{1,0:T(8,128)S(1)} custom-call(s32[1]{0:T(128)} %bitcast.tile, f32[9,56,128]{2,1,0:T(8,128)S(1)} %sample.1.own, f32[9,56,128]{2,1,0:T(8,128)S(1)} %collective-permute-done.1.pair, f32[96,128]{1,0:T(8,128)S(1)} %copy-done.2), custom_call_target="tpu_custom_call" | custom-call | flops 1000000000 | bytes 3000000 | tf_op jit(solution)/shard_map/near_gram/pallas_call | solution.py:514
  27.6 0.0 copy-start.1
  27.6 3.1 %collective-permute-done.following = f32[9,56,128]{2,1,0:T(8,128)S(1)} collective-permute-done((f32[9,56,128]{2,1,0:T(8,128)S(1)}, f32[9,56,128]{2,1,0:T(8,128)S(1)}, u32[]{:S(2)}, u32[]{:S(2)}) %collective-permute-start) | collective-permute-done | bytes 258080 | tf_op jit(solution)/shard_map/ppermute | solution.py:510
  30.7 2.8 %solve.1.w_ref = f32[744,128]{1,0:T(8,128)S(1)} custom-call(s32[1]{0:T(128)} %bitcast.tile, f32[9,56,128]{2,1,0:T(8,128)S(1)} %collective-permute-done.following, f32[1792,128]{1,0:T(8,128)S(1)} %near_gram.1.partial, f32[96,128]{1,0:T(8,128)S(1)} %copy-done.2), custom_call_target="tpu_custom_call" | custom-call | tf_op jit(solution)/shard_map/solve/pallas_call | solution.py:523
  33.5 0.0 all-to-all-done.1.x_ref
  33.5 0.0 copy-done.1
  33.5 4.1 %transform.1 = bf16[48,8,8,128]{3,2,1,0:T(8,128)(2,1)S(1)} custom-call(f32[744,128]{1,0:T(8,128)S(1)} %solve.1.w_ref, bf16[48,8,8,128]{3,2,1,0:T(8,128)(2,1)S(1)} %all-to-all-done.1.x_ref, bf16[256,512]{1,0:T(8,128)(2,1)S(1)} %copy-done.1), custom_call_target="tpu_custom_call" | custom-call | tf_op jit(solution)/shard_map/transform/pallas_call | solution.py:537
  37.6 20.7 %all_to_all.15 = bf16[48,8,8,128]{3,2,1,0:T(8,128)(2,1)S(1)} all-to-all(bf16[48,8,8,128]{3,2,1,0:T(8,128)(2,1)S(1)} %transform.1), channel_id=1, replica_groups=mesh['member'=16,'tile'=16] {'member'}, dimensions={0} | all-to-all | bytes 1572864 | tf_op jit(solution)/shard_map/all_to_all | solution.py:550
  58.4 0.9 %finish.1 = bf16[3,16,8,2048]{3,2,1,0:T(8,128)(2,1)} custom-call(bf16[16,3,8,8,128]{4,3,2,1,0:T(8,128)(2,1)S(1)} %bitcast.9, bf16[3,16,8,2048]{3,2,1,0:T(8,128)(2,1)} %get-tuple-element.12.partial), custom_call_target="tpu_custom_call", output_to_operand_aliasing={{}: (1, {})} | custom-call | tf_op jit(solution)/shard_map/finish/pallas_call | solution.py:551
Async XLA Ops:
  3.0 14.2 %all-to-all-start = ((bf16[16,64,128]{2,1,0:T(8,128)(2,1)}), bf16[16,64,128]{2,1,0:T(8,128)(2,1)S(1)}, u32[]{:S(2)}, u32[]{:S(2)}) async-start(bf16[16,64,128]{2,1,0:T(8,128)(2,1)} %get-tuple-element.9), calls=%async_computation | async-start | bytes 524288 | tf_op jit(solution)/shard_map/all_to_all | solution.py:496
  9.8 11.1 %copy-start = (bf16[504,1024]{1,0:T(8,128)(2,1)S(1)}, bf16[504,1024]{1,0:T(8,128)(2,1)}, u32[]{:S(2)}) copy-start(bf16[504,1024]{1,0:T(8,128)(2,1)} %constant.19.clone.choose) | copy-start | bytes 3096580
  9.8 11.1 %copy-start.3 = (f32[16,128]{1,0:T(8,128)S(1)}, f32[16,128]{1,0:T(8,128)}, u32[]{:S(2)}) copy-start(f32[16,128]{1,0:T(8,128)} %get-tuple-element.10.own) | copy-start | bytes 24580
  13.3 13.0 %copy-start.2 = (f32[96,128]{1,0:T(8,128)S(1)}, f32[96,128]{1,0:T(8,128)}, u32[]{:S(2)}) copy-start(f32[96,128]{1,0:T(8,128)} %constant.20.clone.taper) | copy-start | bytes 147460
  17.3 16.2 %all-to-all-start.1 = ((bf16[48,8,8,128]{3,2,1,0:T(8,128)(2,1)}), bf16[48,8,8,128]{3,2,1,0:T(8,128)(2,1)S(1)}, u32[]{:S(2)}, u32[]{:S(2)}) async-start(bf16[48,8,8,128]{3,2,1,0:T(8,128)(2,1)} %bitcast.10), calls=%async_computation.1 | async-start | bytes 1572864 | tf_op jit(solution)/shard_map/all_to_all | solution.py:497
  21.3 5.0 %collective-permute-start.1 = (f32[9,56,128]{2,1,0:T(8,128)S(1)}, f32[9,56,128]{2,1,0:T(8,128)S(1)}, u32[]{:S(2)}, u32[]{:S(2)}) collective-permute-start(f32[9,56,128]{2,1,0:T(8,128)S(1)} %sample.1.own), channel_id=1, source_target_pairs={{0,1},{1,0},{2,3},{3,2},{4,5},{5,4},{6,7},{7,6},{8,9},{9,8},{10,11... | collective-permute-start | bytes 774152 | tf_op jit(solution)/shard_map/ppermute | solution.py:509
  23.5 7.3 %collective-permute-start = (f32[9,56,128]{2,1,0:T(8,128)S(1)}, f32[9,56,128]{2,1,0:T(8,128)S(1)}, u32[]{:S(2)}, u32[]{:S(2)}) collective-permute-start(f32[9,56,128]{2,1,0:T(8,128)S(1)} %sample.1.own), channel_id=1, source_target_pairs={{0,15},{1,2},{2,1},{3,4},{4,3},{5,6},{6,5},{7,8},{8,7},{9,10},{10,... | collective-permute-start | bytes 774152 | tf_op jit(solution)/shard_map/ppermute | solution.py:510
  27.6 5.9 %copy-start.1 = (bf16[256,512]{1,0:T(8,128)(2,1)S(1)}, bf16[256,512]{1,0:T(8,128)(2,1)}, u32[]{:S(2)}) copy-start(bf16[256,512]{1,0:T(8,128)(2,1)} %constant.21.clone.expand) | copy-start | bytes 786436
